TPU v7x, 32 devices: a whole 2x2x4 slice. The times are simulated.
32 devices in a mesh: dp: 8 (over y, x, core), seq: 4 (over z).
Axes of the slice: x: 2, y: 2, z: 4, core: 2. Of those that a mesh axis runs over, the one named last changes fastest.
Arguments:
- tokens: float32 [8, 896, 1024], P('dp', 'seq'), may hold values from -6 to 6
- ln1_gain: float32 [1024], P(('dp', 'seq')), may hold values from 0.5 to 1.5
- ln1_bias: float32 [1024], P(('dp', 'seq')), may hold values from -2 to 2
- w_qkv: float32 [1024, 3072], P('dp', 'seq'), may hold values from -0.1875 to 0.1875
- w_out: float32 [1024, 1024], P('dp', 'seq'), may hold values from -0.75 to 0.75
- ln2_gain: float32 [1024], P(('dp', 'seq')), may hold values from 0.5 to 1.5
- ln2_bias: float32 [1024], P(('dp', 'seq')), may hold values from -2 to 2
- w_up: float32 [1024, 4096], P('dp', 'seq'), may hold values from -0.1875 to 0.1875
- w_down: float32 [4096, 1024], P(('dp', 'seq')), may hold values from -0.09375 to 0.09375
- w_unpatch: float32 [1024, 2048], P('dp', 'seq'), may hold values from -0.1875 to 0.1875
- dec_w1: float32 [96, 64], replicated, may hold values from -0.625 to 0.625
- dec_b1: float32 [64], replicated, may hold values from -3 to 3
- dec_w2: float32 [64, 4], replicated, may hold values from -0.75 to 0.75
- dec_b2: float32 [4], replicated, may hold values from -3 to 3
- counts: int32 [8], P('dp'), may hold values from 32 to 128, as said below
- sample_texels: int32 [8, 3, 8192], P('dp', None, 'seq'), may hold values from 0 to 16383
- d_density: float32 [8, 8192], P('dp', 'seq'), may hold values from -6 to 6
- d_color: float32 [8, 3, 8192], P('dp', None, 'seq'), may hold values from -6 to 6
Outputs:
- density: float32 [8, 8192], P('dp', 'seq')
- color: float32 [8, 3, 8192], P('dp', None, 'seq')
- g_tokens: float32 [8, 896, 1024], P('dp', 'seq')
- g_ln1_gain: float32 [1024], P(('dp', 'seq'))
- g_ln1_bias: float32 [1024], P(('dp', 'seq'))
- g_w_qkv: float32 [1024, 3072], P('dp', 'seq')
- g_w_out: float32 [1024, 1024], P('dp', 'seq')
- g_ln2_gain: float32 [1024], P(('dp', 'seq'))
- g_ln2_bias: float32 [1024], P(('dp', 'seq'))
- g_w_up: float32 [1024, 4096], P('dp', 'seq')
- g_w_down: float32 [4096, 1024], P(('dp', 'seq'))
- g_w_unpatch: float32 [1024, 2048], P('dp', 'seq')
- g_dec_w1: float32 [96, 64], replicated
- g_dec_b1: float32 [64], replicated
- g_dec_w2: float32 [64, 4], replicated
- g_dec_b2: float32 [4], replicated
Inputs may be any that keep to these rules, and one draw needn't show every extreme that they name: A scene's image tokens fill its first counts slots in part order; some scene has all 128 slots filled.
All inputs are finite; a program needn't handle non-finite values.
Results may differ from a plain program's by a relative error of at most 0.023.
Values may be sent and summed in bfloat16 or wider, within the bound.
A program may use at most 192 MiB of HBM per device.

v0:
```python
import jax
import jax.numpy as jnp
from jax import lax
from jax.sharding import PartitionSpec as P

HEADS = 16
PATCH = 8
CH = 32
PRES = 16


EPSILON = 1e-05
NEGATIVE = -1e30


def matmul(left, right):
    return jnp.dot(left, right, preferred_element_type=jnp.float32)


def matmul_tn(left, right):
    return lax.dot_general(
        left, right, (((0,), (0,)), ((), ())), preferred_element_type=jnp.float32
    )


def matmul_nt(left, right):
    return lax.dot_general(
        left, right, (((1,), (1,)), ((), ())), preferred_element_type=jnp.float32
    )


def exact(left, right):
    return jnp.dot(left, right, precision=lax.Precision.HIGHEST, preferred_element_type=jnp.float32)


def exact_tn(left, right):
    return lax.dot_general(
        left,
        right,
        (((0,), (0,)), ((), ())),
        precision=lax.Precision.HIGHEST,
        preferred_element_type=jnp.float32,
    )


def exact_nt(left, right):
    return lax.dot_general(
        left,
        right,
        (((1,), (1,)), ((), ())),
        precision=lax.Precision.HIGHEST,
        preferred_element_type=jnp.float32,
    )


def gelu_exact(values):
    return jax.nn.gelu(values, approximate=False)


def norm_forward(values, gain, shift):
    center = values - jnp.mean(values, axis=-1, keepdims=True)
    inverse = lax.rsqrt(jnp.mean(center * center, axis=-1, keepdims=True) + EPSILON)
    normed = center * inverse
    return (normed * gain + shift, normed, inverse)


def norm_backward(grad, normed, inverse, gain):
    scaled = grad * gain
    inner = scaled - jnp.mean(scaled, axis=-1, keepdims=True)
    inner = inner - normed * jnp.mean(scaled * normed, axis=-1, keepdims=True)
    return (inner * inverse, jnp.sum(grad * normed, axis=0), jnp.sum(grad, axis=0))


def split_heads(matrix, heads):
    return matrix.reshape(matrix.shape[0], heads, matrix.shape[1] // heads).transpose(1, 0, 2)


def join_heads(stacked):
    return stacked.transpose(1, 0, 2).reshape(stacked.shape[1], stacked.shape[0] * stacked.shape[2])


def tiles_to_whole(stacked, groups, parts):
    tile_rows = stacked.shape[0] // (groups * parts)
    tile_cols = stacked.shape[1]
    blocks = stacked.reshape(groups, parts, tile_rows, tile_cols).transpose(0, 2, 1, 3)
    return blocks.reshape(groups * tile_rows, parts * tile_cols)


def whole_to_tiles(whole, groups, parts):
    tile_rows = whole.shape[0] // groups
    tile_cols = whole.shape[1] // parts
    blocks = whole.reshape(groups, tile_rows, parts, tile_cols).transpose(0, 2, 1, 3)
    return blocks.reshape(groups * parts * tile_rows, tile_cols)


def shards(
    tokens,
    ln1_gain,
    ln1_bias,
    w_qkv,
    w_out,
    ln2_gain,
    ln2_bias,
    w_up,
    w_down,
    w_unpatch,
    dec_w1,
    dec_b1,
    dec_w2,
    dec_b2,
    counts,
    sample_texels,
    d_density,
    d_color,
):
    seq_size = lax.axis_size("seq")
    dp_size = lax.axis_size("dp")
    quarter = PRES * PRES // seq_size
    plane_dev = 3 * quarter
    rows_in = tokens[0]
    tok_dev = rows_in.shape[0]
    width = rows_in.shape[1]
    head_dim = width // HEADS
    scale = head_dim ** (-0.5)
    bfloat = jnp.bfloat16
    gathered = (
        lax.all_gather(w_qkv.astype(bfloat), ("dp", "seq"), axis=0, tiled=True),
        lax.all_gather(w_out.astype(bfloat), ("dp", "seq"), axis=0, tiled=True),
        lax.all_gather(w_up.astype(bfloat), ("dp", "seq"), axis=0, tiled=True),
        lax.all_gather(w_down.astype(bfloat), ("dp", "seq"), axis=0, tiled=True),
        lax.all_gather(w_unpatch.astype(bfloat), ("dp", "seq"), axis=0, tiled=True),
        lax.all_gather(ln1_gain.astype(bfloat), ("dp", "seq"), axis=0, tiled=True),
        lax.all_gather(ln1_bias.astype(bfloat), ("dp", "seq"), axis=0, tiled=True),
        lax.all_gather(ln2_gain.astype(bfloat), ("dp", "seq"), axis=0, tiled=True),
        lax.all_gather(ln2_bias.astype(bfloat), ("dp", "seq"), axis=0, tiled=True),
    )
    qkv_weight = tiles_to_whole(gathered[0], dp_size, seq_size)
    out_weight = tiles_to_whole(gathered[1], dp_size, seq_size)
    up_weight = tiles_to_whole(gathered[2], dp_size, seq_size)
    down_weight = gathered[3]
    unpatch_weight = tiles_to_whole(gathered[4], dp_size, seq_size)
    gain_one, shift_one, gain_two, shift_two = [part.astype(jnp.float32) for part in gathered[5:]]
    norm_one, normed_one, inverse_one = norm_forward(rows_in, gain_one, shift_one)
    hidden_one = norm_one.astype(bfloat)
    qkv = matmul(hidden_one, qkv_weight).astype(bfloat)
    keys_all, values_all = (
        lax.all_gather(qkv[:, width : 2 * width], "seq", axis=0, tiled=True),
        lax.all_gather(qkv[:, 2 * width :], "seq", axis=0, tiled=True),
    )
    position = jnp.arange(seq_size * tok_dev, dtype=jnp.int32)
    owner = position // tok_dev
    offset = position % tok_dev
    key_valid = (offset < plane_dev) | (
        owner * (tok_dev - plane_dev) + offset - plane_dev < counts[0]
    )
    query_heads = split_heads(qkv[:, :width], HEADS)
    key_heads = split_heads(keys_all, HEADS)
    value_heads = split_heads(values_all, HEADS)

    def head_forward(parts):
        query_h, key_h, value_h = parts
        scores = jnp.where(key_valid[None, :], matmul_nt(query_h, key_h) * scale, NEGATIVE)
        peak = jnp.max(scores, axis=-1, keepdims=True)
        expo = jnp.exp(scores - peak)
        total = jnp.sum(expo, axis=-1, keepdims=True)
        probs = (expo / total).astype(bfloat)
        return (matmul(probs, value_h), peak[:, 0] + jnp.log(total[:, 0]))

    head_out, log_norm = lax.map(head_forward, (query_heads, key_heads, value_heads))
    mixed = join_heads(head_out).astype(bfloat)
    after_attn = rows_in + matmul(mixed, out_weight)
    norm_two, normed_two, inverse_two = norm_forward(after_attn, gain_two, shift_two)
    hidden_two = norm_two.astype(bfloat)
    pre_act = matmul(hidden_two, up_weight)
    act_value, act_pull = jax.vjp(gelu_exact, pre_act)
    activated = act_value.astype(bfloat)
    layer_out = after_attn + matmul(activated, down_weight)
    plane_rows = layer_out[:plane_dev].astype(bfloat)
    own_texels = matmul(plane_rows, unpatch_weight).astype(bfloat)
    texels = lax.all_gather(own_texels, "seq", axis=0, tiled=True)
    table = texels.reshape(-1, CH)
    texel = sample_texels[0]
    samples = texel.shape[1]
    side = PRES * PATCH
    row_pos = texel // side
    col_pos = texel % side
    token = row_pos // PATCH * PRES + col_pos // PATCH
    sub_pos = row_pos % PATCH * PATCH + col_pos % PATCH
    plane = jnp.arange(3, dtype=jnp.int32)[:, None]
    grid_row = token // quarter * plane_dev + plane * quarter + token % quarter
    flat_rows = (grid_row * (PATCH * PATCH) + sub_pos).reshape(-1)
    picked = jnp.take(table, flat_rows, axis=0).astype(jnp.float32)
    features = picked.reshape(3, samples, CH).transpose(1, 0, 2).reshape(samples, 3 * CH)
    dec_pre = exact(features, dec_w1) + dec_b1
    dec_hidden, dec_pull = jax.vjp(gelu_exact, dec_pre)
    dec_out = exact(dec_hidden, dec_w2) + dec_b2
    density = jax.nn.softplus(dec_out[:, 0])
    color_value = jax.nn.sigmoid(dec_out[:, 1:])
    grad_dec_out = jnp.concatenate(
        [
            (d_density[0] * jax.nn.sigmoid(dec_out[:, 0]))[:, None],
            d_color[0].T * color_value * (1.0 - color_value),
        ],
        axis=1,
    )
    grad_w_two = exact_tn(dec_hidden, grad_dec_out)
    grad_b_two = jnp.sum(grad_dec_out, axis=0)
    grad_dec_pre = dec_pull(exact_nt(grad_dec_out, dec_w2))[0]
    grad_w_one = exact_tn(features, grad_dec_pre)
    grad_b_one = jnp.sum(grad_dec_pre, axis=0)
    grad_features = exact_nt(grad_dec_pre, dec_w1)
    decoder_sums = lax.psum((grad_w_one, grad_b_one, grad_w_two, grad_b_two), ("dp", "seq"))
    spread_grads = grad_features.reshape(samples, 3, CH).transpose(1, 0, 2).reshape(-1, CH)
    grad_table = jnp.zeros(table.shape, jnp.float32).at[flat_rows].add(spread_grads)
    own_grad_texels = (
        lax.psum_scatter(
            grad_table.reshape(texels.shape).astype(jnp.bfloat16),
            "seq",
            scatter_dimension=0,
            tiled=True,
        )
        .astype(jnp.float32)
        .astype(bfloat)
    )
    grad_planes = matmul_nt(own_grad_texels, unpatch_weight)
    grad_unpatch = whole_to_tiles(matmul_tn(plane_rows, own_grad_texels), dp_size, seq_size)
    grad_layer = jnp.concatenate(
        [grad_planes, jnp.zeros((tok_dev - plane_dev, width), jnp.float32)], axis=0
    )
    grad_layer_low = grad_layer.astype(bfloat)
    grad_down = matmul_tn(activated, grad_layer_low)
    grad_pre = act_pull(matmul_nt(grad_layer_low, down_weight))[0].astype(bfloat)
    grad_up = whole_to_tiles(matmul_tn(hidden_two, grad_pre), dp_size, seq_size)
    grad_norm_two, grad_gain_two, grad_shift_two = norm_backward(
        matmul_nt(grad_pre, up_weight), normed_two, inverse_two, gain_two
    )
    grad_after = grad_layer + grad_norm_two
    grad_after_low = grad_after.astype(bfloat)
    grad_out_weight = whole_to_tiles(matmul_tn(mixed, grad_after_low), dp_size, seq_size)
    grad_mixed = matmul_nt(grad_after_low, out_weight).astype(bfloat)
    grad_heads = split_heads(grad_mixed, HEADS)

    def head_backward(parts):
        query_h, key_h, value_h, norm_h, grad_h = parts
        scores = matmul_nt(query_h, key_h) * scale
        probs = jnp.where(key_valid[None, :], jnp.exp(scores - norm_h[:, None]), 0.0)
        grad_value = matmul_tn(probs.astype(bfloat), grad_h)
        grad_probs = matmul_nt(grad_h, value_h)
        grad_scores = (
            probs * (grad_probs - jnp.sum(probs * grad_probs, axis=-1, keepdims=True))
        ).astype(bfloat)
        grad_query = matmul(grad_scores, key_h) * scale
        grad_key = matmul_tn(grad_scores, query_h) * scale
        return (grad_query, grad_key, grad_value)

    grad_query, grad_key, grad_value = lax.map(
        head_backward, (query_heads, key_heads, value_heads, log_norm, grad_heads)
    )
    own_key_grad, own_value_grad = (
        lax.psum_scatter(
            join_heads(grad_key).astype(jnp.bfloat16), "seq", scatter_dimension=0, tiled=True
        ).astype(jnp.float32),
        lax.psum_scatter(
            join_heads(grad_value).astype(jnp.bfloat16), "seq", scatter_dimension=0, tiled=True
        ).astype(jnp.float32),
    )
    grad_qkv = jnp.concatenate(
        [join_heads(grad_query), own_key_grad, own_value_grad], axis=1
    ).astype(bfloat)
    grad_qkv_weight = whole_to_tiles(matmul_tn(hidden_one, grad_qkv), dp_size, seq_size)
    grad_norm_one, grad_gain_one, grad_shift_one = norm_backward(
        matmul_nt(grad_qkv, qkv_weight), normed_one, inverse_one, gain_one
    )
    grad_tokens = grad_after + grad_norm_one
    block_sums = (
        lax.psum_scatter(grad_qkv_weight, ("dp", "seq"), scatter_dimension=0, tiled=True),
        lax.psum_scatter(grad_out_weight, ("dp", "seq"), scatter_dimension=0, tiled=True),
        lax.psum_scatter(grad_up, ("dp", "seq"), scatter_dimension=0, tiled=True),
        lax.psum_scatter(grad_down, ("dp", "seq"), scatter_dimension=0, tiled=True),
        lax.psum_scatter(grad_unpatch, ("dp", "seq"), scatter_dimension=0, tiled=True),
        lax.psum_scatter(grad_gain_one, ("dp", "seq"), scatter_dimension=0, tiled=True),
        lax.psum_scatter(grad_shift_one, ("dp", "seq"), scatter_dimension=0, tiled=True),
        lax.psum_scatter(grad_gain_two, ("dp", "seq"), scatter_dimension=0, tiled=True),
        lax.psum_scatter(grad_shift_two, ("dp", "seq"), scatter_dimension=0, tiled=True),
    )
    sum_qkv, sum_out, sum_up, sum_down, sum_unpatch = block_sums[:5]
    sum_gain_one, sum_shift_one, sum_gain_two, sum_shift_two = block_sums[5:]
    return (
        density[None],
        color_value.T[None],
        grad_tokens[None],
        sum_gain_one,
        sum_shift_one,
        sum_qkv,
        sum_out,
        sum_gain_two,
        sum_shift_two,
        sum_up,
        sum_down,
        sum_unpatch,
        decoder_sums[0],
        decoder_sums[1],
        decoder_sums[2],
        decoder_sums[3],
    )


def solution(mesh):
    in_specs = (
        P("dp", "seq", None),
        P(("dp", "seq")),
        P(("dp", "seq")),
        P("dp", "seq"),
        P("dp", "seq"),
        P(("dp", "seq")),
        P(("dp", "seq")),
        P("dp", "seq"),
        P(("dp", "seq"), None),
        P("dp", "seq"),
        P(),
        P(),
        P(),
        P(),
        P("dp"),
        P("dp", None, "seq"),
        P("dp", "seq"),
        P("dp", None, "seq"),
    )
    out_specs = (
        P("dp", "seq"),
        P("dp", None, "seq"),
        P("dp", "seq", None),
        P(("dp", "seq")),
        P(("dp", "seq")),
        P("dp", "seq"),
        P("dp", "seq"),
        P(("dp", "seq")),
        P(("dp", "seq")),
        P("dp", "seq"),
        P(("dp", "seq"), None),
        P("dp", "seq"),
        P(),
        P(),
        P(),
        P(),
    )
    return jax.shard_map(shards, mesh=mesh, in_specs=in_specs, out_specs=out_specs, check_vma=False)
```

profile of v0, /device:TPU:0, one launch (start us, length us, event | category | flops | bytes accessed | tf_op | source)
XLA Modules:
  0.0 2182.0 jit_solution(14404447415542294104)
XLA Ops:
  15.8 42.3 %all-reduce.10 = (bf16[1024]{0:T(1024)(128)(2,1)S(1)}, bf16[1024]{0:T(1024)(128)(2,1)S(1)}, bf16[1024]{0:T(1024)(128)(2,1)S(1)}, bf16[1024]{0:T(1024)(128)(2,1)S(1)}) all-reduce(bf16[1024]{0:T(1024)(128)(2,1)S(1)} %dynamic-update-slice.1, bf16[1024]{0:T(1024)(128)(2,1)S(1)} %dynamic-update-slice, ...), channel_id=1, replica_groups=mesh['dp'=8,'seq'=4] {'dp','seq'}, use_global_device_ids=true, to_apply=%add.2 | all-reduce | flops 4096 | bytes 16384
  61.1 22.8 %all-gather.9.cloned.1.call-done = bf16[4096,768]{1,0:T(8,128)(2,1)} async-done(((bf16[128,768]{1,0:T(8,128)(2,1)}), bf16[4096,768]{1,0:T(8,128)(2,1)}) %all-gather.9.cloned.1.call-update) | async-done | bytes 6291472 | tf_op jit(solution)/shard_map/all_gather | solution.py:127
  84.0 9.2 copy.100
  93.2 5.0 fusion.86
  101.8 40.6 %all-gather.15.cloned.1.call-done = bf16[4096,256]{1,0:T(8,128)(2,1)} async-done(((bf16[128,256]{1,0:T(8,128)(2,1)}), bf16[4096,256]{1,0:T(8,128)(2,1)}) %all-gather.15.cloned.1.call-update) | async-done | bytes 2097168 | tf_op jit(solution)/shard_map/all_gather | solution.py:128
  142.4 4.4 copy.107
  146.8 60.2 %all-gather.21.cloned.1.call-done = bf16[4096,512]{1,0:T(8,128)(2,1)} async-done(((bf16[128,512]{1,0:T(8,128)(2,1)}), bf16[4096,512]{1,0:T(8,128)(2,1)}) %all-gather.21.cloned.1.call-update) | async-done | bytes 4194320 | tf_op jit(solution)/shard_map/all_gather | solution.py:131
  207.0 7.6 copy.109
  216.1 32.9 %all-gather.11.cloned.1.call-done = bf16[896,1024]{1,0:T(8,128)(2,1)} async-done(((bf16[224,1024]{1,0:T(8,128)(2,1)}), bf16[896,1024]{1,0:T(8,128)(2,1)}) %all-gather.11.cloned.1.call-update) | async-done | bytes 1835024 | tf_op jit(solution)/shard_map/all_gather | solution.py:147
  249.0 3.1 copy.102
  252.0 3.0 copy.105
  255.0 36.2 %all-gather.13.cloned.1.call-done = bf16[896,1024]{1,0:T(8,128)(2,1)} async-done(((bf16[224,1024]{1,0:T(8,128)(2,1)}), bf16[896,1024]{1,0:T(8,128)(2,1)}) %all-gather.13.cloned.1.call-update) | async-done | bytes 1835024 | tf_op jit(solution)/shard_map/all_gather | solution.py:148
  291.3 3.1 copy.103
  294.3 3.0 copy.106
  297.3 80.1 %while.28 = (s32[]{:T(128)}, bf16[16,224,64]{1,2,0:T(8,128)(2,1)S(1)}, f32[16,224]{1,0:T(8,128)}, bf16[16,224,64]{2,1,0:T(8,128)(2,1)}, bf16[16,896,64]{2,1,0:T(...) while((s32[]{:T(128)}, bf16[16,224,64]{1,2,0:T(8,128)(2,1)S(1)}, ...), condition=%wide.region_5.6_spmd.clone, body=%wide.region_2.5_spmd.clone.sunk | while | flops 53001760 | bytes 3003245 | solution.py:169
  380.4 12.4 copy.108
  392.9 15.7 multiply_convert_fusion.1
  408.6 42.0 %all-gather.19.cloned.1.call-done = bf16[4096,1024]{1,0:T(8,128)(2,1)} async-done(((bf16[128,1024]{1,0:T(8,128)(2,1)}), bf16[4096,1024]{1,0:T(8,128)(2,1)}) %all-gather.19.cloned.1.call-update) | async-done | bytes 8388624 | tf_op jit(solution)/shard_map/all_gather | solution.py:130
  450.6 6.1 fusion.179
  461.3 61.0 %all-gather.23.cloned.1.call-done = bf16[768,2048]{1,0:T(8,128)(2,1)} async-done(((bf16[192,2048]{1,0:T(8,128)(2,1)}), bf16[768,2048]{1,0:T(8,128)(2,1)}) %all-gather.23.cloned.1.call-update) | async-done | bytes 3145744 | tf_op jit(solution)/shard_map/all_gather | solution.py:180
  522.4 15.1 reshape.627
  537.4 22.7 %gather_fusion = bf16[6144,32]{1,0:T(8,128)(2,1)S(1)} fusion(bf16[49152,32]{1,0:T(8,128)(2,1)} %reshape.627, s32[6144]{0:T(1024)S(1)} %broadcast_clamp_fusion), kind=kCustom, calls=%fused_computation | custom fusion | bytes 811008 | tf_op jit(solution)/shard_map/jit(_take)/gather | solution.py:192
  569.6 43.5 %scatter_custom_fusion = f32[49152,32]{1,0:T(8,128)} fusion(s32[6144]{0:T(1024)} %bitcast.367, f32[6144,32]{1,0:T(8,128)} %bitcast.350, f32[]{:T(128)} %constant.255.clone.1), kind=kCustom, calls=%fused_computation.90 | custom fusion | flops 196608 | bytes 6291968 | tf_op jit(solution)/shard_map/scatter-add | solution.py:214
  613.1 13.1 convert_element_type.144
  626.2 17.4 convert_element_type.145
  643.6 59.0 %reduce-scatter.9.cloned.1.call-done = bf16[192,2048]{1,0:T(8,128)(2,1)} async-done(((bf16[768,2048]{1,0:T(8,128)(2,1)}), bf16[192,2048]{1,0:T(8,128)(2,1)}) %reduce-scatter.9.cloned.1.call-update) | async-done | bytes 786448 | tf_op jit(solution)/shard_map/reduce_scatter | solution.py:216
  702.6 3.6 fusion.82
  706.3 9.5 add_convert_fusion
  722.3 140.1 %while.29 = (s32[]{:T(128)}, bf16[16,224,64]{1,2,0:T(8,128)(2,1)S(1)}, bf16[16,896,64]{1,2,0:T(8,128)(2,1)}, bf16[16,896,64]{1,2,0:T(8,128)(2,1)}, bf16[16,224,6...) while((s32[]{:T(128)}, ...), condition=%wide.region_14.15_spmd.clone, body=%wide.region_12.14_spmd.clone.sunk | while | flops 130344480 | bytes 7425277 | solution.py:256
  862.4 3.8 copy.119
  866.3 3.9 copy.118
  872.3 3.9 fusion.125
  876.5 5.7 fusion.181
  882.2 10.8 reshape.637
  893.0 9.2 copy.127
  905.8 40.9 %reduce-scatter.11.cloned.1.call-done = bf16[224,1024]{1,0:T(8,128)(2,1)} async-done(((bf16[896,1024]{1,0:T(8,128)(2,1)}), bf16[224,1024]{1,0:T(8,128)(2,1)}) %reduce-scatter.11.cloned.1.call-update) | async-done | bytes 458768 | tf_op jit(solution)/shard_map/reduce_scatter | solution.py:260
  946.7 4.9 fusion.76
  952.5 6.3 fusion.106
  959.1 9.7 fusion.172
  968.8 20.5 reshape.635
  989.3 17.7 copy.126
  1008.1 9.7 fusion.133
  1022.5 41.2 %all-reduce.9 = (f32[1024]{0:T(1024)S(1)}, f32[1024]{0:T(1024)S(1)}, f32[1024]{0:T(1024)S(1)}, f32[1024]{0:T(1024)S(1)}, f32[96,64]{0,1:T(8,128)}, /*index=5*/f32[64]{0:T(128)}, f32[64,4]{0,1:T(4,128)}, f32[4]{0:T(128)}) all-reduce(f32[1024]{0:T(1024)S(1)} %get-tuple-element.270, ...), channel_id=5, replica_groups=mesh['dp'=8,'seq'=4] {'dp','seq'}, use_global_device_ids=true, to_apply=%region_20.21.clone | all-reduce | flops 10564 | bytes 84512
  1067.4 29.6 %reduce-scatter.17.cloned.1.call-done = f32[128,256]{1,0:T(8,128)} async-done(((f32[4096,256]{1,0:T(8,128)}), f32[128,256]{1,0:T(8,128)}) %reduce-scatter.17.cloned.1.call-update) | async-done | bytes 131088 | tf_op jit(solution)/shard_map/reduce_scatter | solution.py:277
  1096.9 187.4 %reduce-scatter.23.cloned.1.call-done = f32[128,512]{1,0:T(8,128)} async-done(((f32[4096,512]{1,0:T(8,128)}), f32[128,512]{1,0:T(8,128)}) %reduce-scatter.23.cloned.1.call-update) | async-done | bytes 262160 | tf_op jit(solution)/shard_map/reduce_scatter | solution.py:280
  1284.3 159.5 %reduce-scatter.15.cloned.1.call-done = f32[128,768]{1,0:T(8,128)} async-done(((f32[4096,768]{1,0:T(8,128)}), f32[128,768]{1,0:T(8,128)}) %reduce-scatter.15.cloned.1.call-update) | async-done | bytes 393232 | tf_op jit(solution)/shard_map/reduce_scatter | solution.py:276
  1443.8 366.1 %reduce-scatter.19.cloned.1.call-done = f32[128,1024]{1,0:T(8,128)} async-done(((f32[4096,1024]{1,0:T(8,128)}), f32[128,1024]{1,0:T(8,128)}) %reduce-scatter.19.cloned.1.call-update) | async-done | bytes 524304 | tf_op jit(solution)/shard_map/reduce_scatter | solution.py:278
  1810.0 365.0 %reduce-scatter.21.cloned.1.call-done = f32[128,1024]{1,0:T(8,128)} async-done(((f32[4096,1024]{1,0:T(8,128)}), f32[128,1024]{1,0:T(8,128)}) %reduce-scatter.21.cloned.1.call-update) | async-done | bytes 524304 | tf_op jit(solution)/shard_map/reduce_scatter | solution.py:279
  (429 shorter events, 276.1 us)
Async XLA Ops:
  7.2 555.3 %copy-start = (f32[96,64]{0,1:T(8,128)S(1)}, f32[96,64]{0,1:T(8,128)}, u32[]{:S(2)}) copy-start(f32[96,64]{0,1:T(8,128)} %param.32) | copy-start | bytes 73732
  7.2 76.8 %all-gather.9.cloned.1.call-start = ((), (), s32[]{:S(2)}) async-start(), calls=%async_computation.8 | async-start | bytes 6488064 | tf_op jit(solution)/shard_map/all_gather | solution.py:127
  9.0 133.5 %all-gather.15.cloned.1.call-start = ((), (), s32[]{:S(2)}) async-start(), calls=%async_computation.11 | async-start | bytes 2162688 | tf_op jit(solution)/shard_map/all_gather | solution.py:128
  10.6 196.4 %all-gather.21.cloned.1.call-start = ((), (), s32[]{:S(2)}) async-start(), calls=%async_computation.14 | async-start | bytes 4325376 | tf_op jit(solution)/shard_map/all_gather | solution.py:131
  12.3 236.7 %all-gather.11.cloned.1.call-start = ((), (), s32[]{:S(2)}) async-start(), calls=%async_computation.9 | async-start | bytes 2293760 | tf_op jit(solution)/shard_map/all_gather | solution.py:147
  58.1 35.1 %copy-start.33 = (f32[1024]{0:T(1024)}, f32[1024]{0:T(1024)S(1)}, u32[]{:S(2)}) copy-start(f32[1024]{0:T(1024)S(1)} %convert_element_type.125) | copy-start | bytes 12292
  58.1 35.1 %copy-start.24 = (f32[1024]{0:T(1024)}, f32[1024]{0:T(1024)S(1)}, u32[]{:S(2)}) copy-start(f32[1024]{0:T(1024)S(1)} %convert_element_type.123) | copy-start | bytes 12292
  59.4 33.7 %copy-start.31 = (f32[224]{0:T(256)}, f32[224]{0:T(256)S(1)}, u32[]{:S(2)}) copy-start(f32[224]{0:T(256)S(1)} %broadcast_multiply_fusion.5) | copy-start | bytes 2692
  61.1 32.0 %copy-start.35 = (f32[224]{0:T(256)}, f32[224]{0:T(256)S(1)}, u32[]{:S(2)}) copy-start(f32[224]{0:T(256)S(1)} %add_rsqrt_fusion.1) | copy-start | bytes 2692
  84.0 9.2 copy-start.2
  99.3 192.0 %all-gather.13.cloned.1.call-start = ((), (), s32[]{:S(2)}) async-start(), calls=%async_computation.10 | async-start | bytes 2293760 | tf_op jit(solution)/shard_map/all_gather | solution.py:148
  99.9 280.5 %all-gather.17.cloned.1.call-start = ((), (), s32[]{:S(2)}) async-start(), calls=%async_computation.12 | async-start | bytes 8650752 | tf_op jit(solution)/shard_map/all_gather | solution.py:129
  100.7 349.9 %all-gather.19.cloned.1.call-start = ((), (), s32[]{:S(2)}) async-start(), calls=%async_computation.13 | async-start | bytes 8650752 | tf_op jit(solution)/shard_map/all_gather | solution.py:130
  101.5 420.8 %all-gather.23.cloned.1.call-start = ((), (), s32[]{:S(2)}) async-start(), calls=%async_computation.15 | async-start | bytes 3932160 | tf_op jit(solution)/shard_map/all_gather | solution.py:180
  377.5 15.4 copy-start.4
  380.1 12.8 copy-start.26
  380.4 12.5 copy-start.28
  450.6 7.0 copy-start.6
  460.1 242.5 %reduce-scatter.9.cloned.1.call-start = ((), (), s32[]{:S(2)}) async-start(), calls=%async_computation.16 | async-start | bytes 3932160 | tf_op jit(solution)/shard_map/reduce_scatter | solution.py:216
  461.0 76.4 %copy-start.22 = (s32[6144,1]{0,1:T(1,128)}, s32[6144,1]{0,1:T(1,128)S(1)}, u32[]{:S(2)}) copy-start(s32[6144,1]{0,1:T(1,128)S(1)} %compare_select_fusion) | copy-start | bytes 73732
  537.4 25.1 %copy-start.43 = (f32[64]{0:T(128)S(1)}, f32[64]{0:T(128)}, u32[]{:S(2)}) copy-start(f32[64]{0:T(128)} %param.33) | copy-start | bytes 772
  643.6 262.2 %reduce-scatter.13.cloned.1.call-start = ((), (), s32[]{:S(2)}) async-start(), calls=%async_computation.18 | async-start | bytes 2293760 | tf_op jit(solution)/shard_map/reduce_scatter | solution.py:263
  702.6 13.1 slice-start
  706.2 12.4 copy-start.8
  706.2 9.6 slice-start.1
  706.2 9.6 copy-start.27
  706.2 9.6 copy-start.29
  715.8 2.8 copy-start.14
  866.2 4.0 copy-start.5
  866.2 80.5 %reduce-scatter.11.cloned.1.call-start = ((), (), s32[]{:S(2)}) async-start(), calls=%async_computation.17 | async-start | bytes 2293760 | tf_op jit(solution)/shard_map/reduce_scatter | solution.py:260
  870.2 226.8 %reduce-scatter.17.cloned.1.call-start = ((), (), s32[]{:S(2)}) async-start(), calls=%async_computation.20 | async-start | bytes 4325376 | tf_op jit(solution)/shard_map/reduce_scatter | solution.py:277
  872.3 4.2 copy-start.13
  876.2 408.1 %reduce-scatter.23.cloned.1.call-start = ((), (), s32[]{:S(2)}) async-start(), calls=%async_computation.23 | async-start | bytes 8650752 | tf_op jit(solution)/shard_map/reduce_scatter | solution.py:280
  902.3 541.5 %reduce-scatter.15.cloned.1.call-start = ((), (), s32[]{:S(2)}) async-start(), calls=%async_computation.19 | async-start | bytes 12976128 | tf_op jit(solution)/shard_map/reduce_scatter | solution.py:276
  903.3 48.3 %copy-start.25 = (f32[1024]{0:T(1024)S(1)}, f32[1024]{0:T(1024)}, u32[]{:S(2)}) copy-start(f32[1024]{0:T(1024)} %copy-done.24) | copy-start | bytes 12292
  903.3 48.3 %copy-start.32 = (f32[224]{0:T(256)S(1)}, f32[224]{0:T(256)}, u32[]{:S(2)}) copy-start(f32[224]{0:T(256)} %copy-done.31) | copy-start | bytes 2692
  903.3 48.3 %copy-start.34 = (f32[1024]{0:T(1024)S(1)}, f32[1024]{0:T(1024)}, u32[]{:S(2)}) copy-start(f32[1024]{0:T(1024)} %copy-done.33) | copy-start | bytes 12292
  903.3 48.4 %copy-start.36 = (f32[224]{0:T(256)S(1)}, f32[224]{0:T(256)}, u32[]{:S(2)}) copy-start(f32[224]{0:T(256)} %copy-done.35) | copy-start | bytes 2692
  946.7 5.6 copy-start.16
  946.7 5.6 copy-start.20
  946.7 5.6 copy-start.21
  958.8 851.2 %reduce-scatter.19.cloned.1.call-start = ((), (), s32[]{:S(2)}) async-start(), calls=%async_computation.21 | async-start | bytes 17301504 | tf_op jit(solution)/shard_map/reduce_scatter | solution.py:278
  1007.0 1167.9 %reduce-scatter.21.cloned.1.call-start = ((), (), s32[]{:S(2)}) async-start(), calls=%async_computation.22 | async-start | bytes 17301504 | tf_op jit(solution)/shard_map/reduce_scatter | solution.py:279
  1017.8 4.7 copy-start.38
  1017.8 4.7 copy-start.39
  1017.8 4.7 copy-start.42
  1017.8 48.3 %copy-start.7 = (f32[224,1024]{1,0:T(8,128)S(1)}, f32[224,1024]{1,0:T(8,128)}, u32[]{:S(2)}) copy-start(f32[224,1024]{1,0:T(8,128)} %get-tuple-element.323) | copy-start | bytes 2752516
  1017.8 1157.2 %copy-start.1 = (f32[96,64]{0,1:T(8,128)S(1)}, f32[96,64]{0,1:T(8,128)}, u32[]{:S(2)}) copy-start(f32[96,64]{0,1:T(8,128)} %param.32) | copy-start | bytes 73732
  (14 other events, 25.0 us)
Sparse Core Ops, SparseCore 0:
  11.5 72.4 all-gather.8
  87.5 54.9 all-gather.14
  146.0 60.9 all-gather.20
  209.0 39.9 all-gather.10
  251.0 40.2 all-gather.12
  294.6 76.2 all-gather.16
  374.4 76.2 all-gather.18
  460.2 62.0 all-gather.22
  643.7 58.8 reduce-scatter.8
  866.3 39.4 reduce-scatter.12
  908.1 38.5 reduce-scatter.10
  949.4 147.4 reduce-scatter.16
  1099.8 184.4 reduce-scatter.22
  1290.7 153.0 reduce-scatter.14
  1446.6 363.2 reduce-scatter.18
  1812.8 362.1 reduce-scatter.20
where the time goes:
time: 2190 us; the launch traced here: 2180 us
  waiting for transfers between devices  1510 us (69%)
  matrix products  255 us (12%)
  local copies, waits for them, and re-layouts  216 us (10%)
  other arithmetic  103 us (5%)
  blocking collectives  83.5 us (4%)
    reduce_scatter x1, waiting for transfers between devices, shards(): lax.psum_scatter(grad_up, ('dp', 'seq'), scatter_dimension=0, tiled=True)  366 us
    reduce_scatter x1, waiting for transfers between devices, shards(): lax.psum_scatter(grad_down, ('dp', 'seq'), scatter_dimension=0, tiled=True)  365 us
    reduce_scatter x1, waiting for transfers between devices, shards(): lax.psum_scatter(grad_unpatch, ('dp', 'seq'), scatter_dimension=0, tiled=...  187 us
    reduce_scatter x1, waiting for transfers between devices, shards(): lax.psum_scatter(grad_qkv_weight, ('dp', 'seq'), scatter_dimension=0, til...  160 us
    dot_general x37, matrix products, matmul_tn(): lax.dot_general(left, right, (((0,), (0,)), ((), ())), preferred_element_...  88.3 us
    dot_general x53, matrix products, matmul_nt(): lax.dot_general(left, right, (((1,), (1,)), ((), ())), preferred_element_...  86.1 us
    unnamed x2, blocking collectives  83.5 us
    dot_general x37, matrix products, matmul(): return jnp.dot(left, right, preferred_element_type=jnp.float32)  73.4 us
  transfers between devices with their start and end apart: 16, of which 15 were waited for; matrix products, arithmetic and copies ran while one was open for 13% of the time, Pallas kernels for 0%

commit v1 on v0

--- a/solution.py
+++ b/solution.py
@@ -1,6 +1,10 @@
+import functools
+
 import jax
 import jax.numpy as jnp
 from jax import lax
+from jax.experimental import pallas as pl
+from jax.experimental.pallas import tpu as pltpu
 from jax.sharding import PartitionSpec as P
 
 HEADS = 16
@@ -11,6 +15,427 @@
 
 EPSILON = 1e-05
 NEGATIVE = -1e30
+VMEM_LIMIT = 56 * 2**20
+AHEAD = 3
+
+
+MESH = pl.DeviceIdType.MESH
+
+
+class Place:
+    def __init__(self, n, seq_size):
+        dp = lax.axis_index("dp")
+        self.n, self.seq_size = n, seq_size
+        self.seq = lax.axis_index("seq")
+        self.i = (lax.div(dp, n * n), lax.rem(lax.div(dp, n), n), lax.rem(dp, n))
+        self.dp = dp
+
+    def size(self, axis):
+        return self.seq_size if axis == 3 else self.n
+
+    def me(self, axis):
+        return self.seq if axis == 3 else self.i[axis]
+
+    def peer(self, axis, step):
+        to = lax.rem(self.me(axis) + step, self.size(axis))
+        if axis == 3:
+            return to, (self.dp, to)
+        where = [to if a == axis else self.i[a] for a in range(3)]
+        return to, ((where[0] * self.n + where[1]) * self.n + where[2], self.seq)
+
+    def source(self, axis, step):
+        size = self.size(axis)
+        return lax.rem(self.me(axis) + (size - step), size)
+
+    def enter(self):
+        barrier = pltpu.get_barrier_semaphore()
+        count = 0
+        for axis in range(4):
+            for step in range(1, self.size(axis)):
+                pl.semaphore_signal(
+                    barrier, inc=1, device_id=self.peer(axis, step)[1], device_id_type=MESH
+                )
+                count += 1
+        pl.semaphore_wait(barrier, count)
+
+
+def remote(src, dst, send, recv, device):
+    return pltpu.make_async_remote_copy(
+        src_ref=src, dst_ref=dst, send_sem=send, recv_sem=recv, device_id=device, device_id_type=MESH
+    )
+
+
+class Matrix:
+    def __init__(self, name, rows, cols, by_rows, parts):
+        self.name, self.rows, self.cols, self.by_rows = name, rows, cols, by_rows
+        self.parts = parts if rows % (16 * parts) == 0 else 1
+
+    def shape(self, n, seq_size):
+        if self.by_rows:
+            return (n, n, n, seq_size, self.rows, self.cols)
+        return (n, n, n, self.rows, seq_size * self.cols)
+
+    def tail(self, part, first, count):
+        size = self.rows // self.parts
+        rows = pl.ds(part * size, size)
+        if self.by_rows:
+            return (pl.ds(first, count), rows, slice(None))
+        if isinstance(first, int):
+            return (rows, pl.ds(first * self.cols, count * self.cols))
+        return (rows, pl.ds(pl.multiple_of(first * self.cols, 128), count * self.cols))
+
+    def tail_shape(self, count):
+        size = self.rows // self.parts
+        return (count, size, self.cols) if self.by_rows else (size, count * self.cols)
+
+
+def small_sum(place, value, slots, send, recv):
+    for stage, axis in enumerate((2, 1, 0, 3)):
+        me = place.me(axis)
+        slots[stage, me] = value
+        copies = []
+        for step in range(1, place.size(axis)):
+            ref = slots.at[stage, me]
+            copy = remote(
+                ref, ref, send.at[stage, step - 1], recv.at[stage, step - 1], place.peer(axis, step)[1]
+            )
+            copy.start()
+            copies.append(copy)
+        for copy in copies:
+            copy.wait()
+        value = slots[stage, 0]
+        for other in range(1, place.size(axis)):
+            value = value + slots[stage, other]
+    return value
+
+
+class Gather:
+    def __init__(self, place, matrices, refs, sems):
+        self.place, self.refs = place, refs
+        self.chunks = [(w, m, p) for w, m in enumerate(matrices) for p in range(m.parts)]
+        self.seq_send, self.seq_recv, self.hop_send, self.hop_recv, self.far_send, self.far_recv = sems
+        self.copies = {}
+
+    def _send(self, key, axis, region, send, recv):
+        made = []
+        for step in range(1, self.place.size(axis)):
+            copy = remote(region, region, send.at[step - 1], recv.at[step - 1], self.place.peer(axis, step)[1])
+            copy.start()
+            made.append(copy)
+        self.copies[key] = made
+
+    def _take(self, key):
+        for copy in self.copies[key]:
+            copy.wait_recv()
+
+    def region(self, k, index, first, count):
+        w, matrix, part = self.chunks[k]
+        return self.refs[w].at[index + matrix.tail(part, first, count)]
+
+    def along_seq(self, k):
+        p = self.place
+        self._send((k, 0), 3, self.region(k, p.i, p.seq, 1), self.seq_send.at[k], self.seq_recv.at[k])
+
+    def hop(self, k, number):
+        p, half = self.place, self.place.seq_size // 2
+        if number == 0:
+            self._take((k, 0))
+        else:
+            self._take((k, 1, 0))
+            self._take((k, 1, 1))
+        for h in (0, 1):
+            axis = 1 - h if number == 0 else h
+            index = [p.i[0], p.i[1], p.i[2]]
+            if number == 1:
+                index[1 - axis] = slice(None)
+            at = 2 * number + h
+            region = self.region(k, tuple(index), h * half, half)
+            self._send((k, 1 + number, h), axis, region, self.hop_send.at[k, at], self.hop_recv.at[k, at])
+
+    def third(self, k):
+        p = self.place
+        self._take((k, 2, 0))
+        self._take((k, 2, 1))
+        region = self.region(k, (slice(None), slice(None), p.i[2]), 0, p.seq_size)
+        self._send((k, 3), 2, region, self.far_send.at[k], self.far_recv.at[k])
+
+    def arrived(self, k):
+        self._take((k, 3))
+
+    def finish(self):
+        for made in self.copies.values():
+            for copy in made:
+                copy.wait_send()
+
+
+def gather_sems(n, seq_size, chunks):
+    sem = pltpu.SemaphoreType.DMA
+    return [sem((chunks, seq_size - 1))] * 2 + [sem((chunks, 4, n - 1))] * 2 + [sem((chunks, n - 1))] * 2
+
+
+def gather_kernel(n, seq_size, matrices, *refs):
+    count = len(matrices)
+    shards, gains, wholes, gains_out = refs[:count], refs[count], refs[count + 1 : 2 * count + 1], refs[2 * count + 1]
+    rest = refs[2 * count + 2 :]
+    bufs, (slots, small_send, small_recv, out_sem), sems = rest[:count], rest[count : count + 4], rest[count + 4 :]
+    place = Place(n, seq_size)
+    for matrix, shard, buf in zip(matrices, shards, bufs):
+        if matrix.by_rows:
+            buf[place.i + (place.seq,)] = shard[...].astype(jnp.bfloat16)
+        else:
+            at = pl.ds(pl.multiple_of(place.seq * matrix.cols, 128), matrix.cols)
+            buf[place.i + (slice(None), at)] = shard[...].astype(jnp.bfloat16)
+    place.enter()
+    gather = Gather(place, matrices, bufs, sems)
+    total = len(gather.chunks)
+    for k in range(AHEAD):
+        gather.along_seq(k)
+    gains_out[...] = small_sum(place, gains[...], slots, small_send, small_recv)
+    outs = []
+    for t in range(total + 6):
+        if t < total:
+            gather.hop(t, 0)
+            if t + AHEAD < total:
+                gather.along_seq(t + AHEAD)
+        if 0 <= t - 2 < total:
+            gather.hop(t - 2, 1)
+        if 0 <= t - 4 < total:
+            gather.third(t - 4)
+        if 0 <= t - 6 < total:
+            gather.arrived(t - 6)
+            w, matrix, part = gather.chunks[t - 6]
+            index = (slice(None),) * 3 + matrix.tail(part, 0, seq_size)
+            copy = pltpu.make_async_copy(bufs[w].at[index], wholes[w].at[index], out_sem.at[t - 6])
+            copy.start()
+            outs.append(copy)
+    gather.finish()
+    for copy in outs:
+        copy.wait()
+
+
+def gather_weights(n, seq_size, matrices, shards, gains):
+    chunks = sum(m.parts for m in matrices)
+    vmem, any_space = pl.BlockSpec(memory_space=pltpu.VMEM), pl.BlockSpec(memory_space=pl.ANY)
+    shapes = [m.shape(n, seq_size) for m in matrices]
+    largest = max(n, seq_size)
+    return pl.pallas_call(
+        functools.partial(gather_kernel, n, seq_size, matrices),
+        out_shape=[jax.ShapeDtypeStruct(s, jnp.bfloat16) for s in shapes]
+        + [jax.ShapeDtypeStruct(gains.shape, jnp.float32)],
+        in_specs=[vmem] * (len(matrices) + 1),
+        out_specs=[any_space] * len(matrices) + [vmem],
+        scratch_shapes=[pltpu.VMEM(s, jnp.bfloat16) for s in shapes]
+        + [
+            pltpu.VMEM((4, largest) + gains.shape, jnp.float32),
+            pltpu.SemaphoreType.DMA((4, largest - 1)),
+            pltpu.SemaphoreType.DMA((4, largest - 1)),
+            pltpu.SemaphoreType.DMA((chunks,)),
+        ]
+        + gather_sems(n, seq_size, chunks),
+        compiler_params=pltpu.CompilerParams(
+            collective_id=0, has_side_effects=True, vmem_limit_bytes=VMEM_LIMIT
+        ),
+    )(*shards, gains)
+
+
+class Scatter:
+    def __init__(self, place, matrices, wholes, refs, far, hops, near, outs, sems):
+        self.place, self.wholes, self.refs = place, wholes, refs
+        self.far, self.hops, self.near, self.outs = far, hops, near, outs
+        self.chunks = [(w, m, p) for w, m in enumerate(matrices) for p in range(m.parts)]
+        self.seq_send, self.seq_recv, self.hop_send, self.hop_recv, self.far_send, self.far_recv = sems
+        self.copies = {}
+
+    def _send(self, key, axis, region_to, slot, send, recv):
+        made = []
+        for step in range(1, self.place.size(axis)):
+            to, device = self.place.peer(axis, step)
+            copy = remote(region_to(to), slot(step - 1), send.at[step - 1], recv.at[step - 1], device)
+            copy.start()
+            made.append(copy)
+        self.copies[key] = made
+
+    def _take(self, key):
+        for copy in self.copies[key]:
+            copy.wait_recv()
+
+    def _index(self, k, index, first, count):
+        w, matrix, part = self.chunks[k]
+        return index + matrix.tail(part, first, count)
+
+    def third(self, k):
+        w, matrix, part = self.chunks[k]
+        p, every = self.place, slice(None)
+        tail = matrix.tail(part, 0, p.seq_size)
+        self._send(
+            (k, 3),
+            2,
+            lambda to: self.wholes[w].at[(every, every, to) + tail],
+            lambda s: self.far[w].at[(s, every, every) + tail],
+            self.far_send.at[k],
+            self.far_recv.at[k],
+        )
+
+    def hop(self, k, number):
+        w, matrix, part = self.chunks[k]
+        p, half, n = self.place, self.place.seq_size // 2, self.place.n
+        ref = self.refs[w]
+        if number == 0:
+            self._take((k, 3))
+            tail = matrix.tail(part, 0, p.seq_size)
+
+            @pl.loop(0, n * n)
+            def _(at):
+                a, b = lax.div(at, n), lax.rem(at, n)
+                value = ref[(a, b) + tail].astype(jnp.float32)
+                for s in range(n - 1):
+                    value = value + self.far[w][(s, a, b) + tail].astype(jnp.float32)
+                ref[(a, b) + tail] = value.astype(jnp.bfloat16)
+
+        else:
+            for h in (0, 1):
+                self._take((k, 1, h))
+                tail, local = matrix.tail(part, h * half, half), matrix.tail(part, 0, half)
+                for a in range(n):
+                    index = (p.i[0], a) if h == 0 else (a, p.i[1])
+                    value = ref[index + tail].astype(jnp.float32)
+                    for s in range(n - 1):
+                        value = value + self.hops[w][(h, s, a) + local].astype(jnp.float32)
+                    ref[index + tail] = value.astype(jnp.bfloat16)
+        for h in (0, 1):
+            axis = h if number == 0 else 1 - h
+            tail, local = matrix.tail(part, h * half, half), matrix.tail(part, 0, half)
+            other = slice(None) if number == 0 else p.i[1 - axis]
+            at = 2 * number + h
+
+            def region_to(to, axis=axis, other=other, tail=tail):
+                index = (to, other) if axis == 0 else (other, to)
+                return ref.at[index + tail]
+
+            def slot(s, h=h, local=local):
+                return self.hops[w].at[(h, s, pl.ds(0, n) if number == 0 else n) + local]
+
+            self._send((k, 1 + number, h), axis, region_to, slot, self.hop_send.at[k, at], self.hop_recv.at[k, at])
+
+    def along_seq(self, k):
+        w, matrix, part = self.chunks[k]
+        p, half, n = self.place, self.place.seq_size // 2, self.place.n
+        ref = self.refs[w]
+        for h in (0, 1):
+            self._take((k, 2, h))
+            tail, local = matrix.tail(part, h * half, half), matrix.tail(part, 0, half)
+            value = ref[p.i[:2] + tail].astype(jnp.float32)
+            for s in range(n - 1):
+                value = value + self.hops[w][(h, s, n) + local].astype(jnp.float32)
+            ref[p.i[:2] + tail] = value.astype(jnp.bfloat16)
+        size = matrix.rows // matrix.parts
+        self._send(
+            (k, 0),
+            3,
+            lambda to: ref.at[p.i[:2] + matrix.tail(part, to, 1)],
+            lambda s: self.near[w].at[(s,) + matrix.tail(part, 0, 1)],
+            self.seq_send.at[k],
+            self.seq_recv.at[k],
+        )
+
+    def arrived(self, k):
+        w, matrix, part = self.chunks[k]
+        p = self.place
+        self._take((k, 0))
+        value = self.refs[w][p.i[:2] + matrix.tail(part, p.seq, 1)].astype(jnp.float32)
+        for s in range(p.seq_size - 1):
+            value = value + self.near[w][(s,) + matrix.tail(part, 0, 1)].astype(jnp.float32)
+        size = matrix.rows // matrix.parts
+        self.outs[w][pl.ds(part * size, size)] = value.reshape(size, matrix.cols)
+
+    def finish(self):
+        for made in self.copies.values():
+            for copy in made:
+                copy.wait_send()
+
+
+def scatter_kernel(n, seq_size, matrices, *refs):
+    count = len(matrices)
+    grads, small, outs, small_out = refs[:count], refs[count], refs[count + 1 : 2 * count + 1], refs[2 * count + 1]
+    rest = refs[2 * count + 2 :]
+    bufs, far, hops, near = [rest[i * count : (i + 1) * count] for i in range(4)]
+    slots, small_send, small_recv, in_sem = rest[4 * count : 4 * count + 4]
+    sems = rest[4 * count + 4 :]
+    place = Place(n, seq_size)
+    scatter = Scatter(place, matrices, grads, bufs, far, hops, near, outs, sems)
+    total = len(scatter.chunks)
+    loads = []
+    for k, (w, matrix, part) in enumerate(scatter.chunks):
+        tail, every = matrix.tail(part, 0, seq_size), (slice(None),) * 2
+        copy = pltpu.make_async_copy(
+            grads[w].at[every + (place.i[2],) + tail], bufs[w].at[every + tail], in_sem.at[k]
+        )
+        copy.start()
+        loads.append(copy)
+    place.enter()
+    for t in range(total + 8):
+        if t < total:
+            scatter.third(t)
+        if 0 <= t - 2 < total:
+            loads[t - 2].wait()
+            scatter.hop(t - 2, 0)
+        if 0 <= t - 4 < total:
+            scatter.hop(t - 4, 1)
+        if 0 <= t - 6 < total:
+            scatter.along_seq(t - 6)
+        if 0 <= t - 8 < total:
+            scatter.arrived(t - 8)
+        if t == 8:
+            small_out[...] = small_sum(place, small[...], slots, small_send, small_recv)
+    scatter.finish()
+
+
+def scatter_grads(n, seq_size, matrices, grads, small):
+    chunks = sum(m.parts for m in matrices)
+    vmem, any_space = pl.BlockSpec(memory_space=pltpu.VMEM), pl.BlockSpec(memory_space=pl.ANY)
+    shapes = [m.shape(n, seq_size) for m in matrices]
+    largest = max(n, seq_size)
+    bfloat = jnp.bfloat16
+    return pl.pallas_call(
+        functools.partial(scatter_kernel, n, seq_size, matrices),
+        out_shape=[jax.ShapeDtypeStruct((m.rows, m.cols), jnp.float32) for m in matrices]
+        + [jax.ShapeDtypeStruct(small.shape, jnp.float32)],
+        in_specs=[any_space] * len(matrices) + [vmem],
+        out_specs=[vmem] * (len(matrices) + 1),
+        scratch_shapes=[pltpu.VMEM((n, n) + s[3:], bfloat) for s in shapes]
+        + [pltpu.VMEM((n - 1, n, n) + s[3:], bfloat) for s in shapes]
+        + [
+            pltpu.VMEM(
+                (2, n - 1, n + 1)
+                + ((seq_size // 2, m.rows, m.cols) if m.by_rows else (m.rows, seq_size // 2 * m.cols)),
+                bfloat,
+            )
+            for m in matrices
+        ]
+        + [
+            pltpu.VMEM((seq_size - 1,) + ((1, m.rows, m.cols) if m.by_rows else (m.rows, m.cols)), bfloat)
+            for m in matrices
+        ]
+        + [
+            pltpu.VMEM((4, largest) + small.shape, jnp.float32),
+            pltpu.SemaphoreType.DMA((4, largest - 1)),
+            pltpu.SemaphoreType.DMA((4, largest - 1)),
+            pltpu.SemaphoreType.DMA((chunks,)),
+        ]
+        + gather_sems(n, seq_size, chunks),
+        compiler_params=pltpu.CompilerParams(
+            collective_id=1, has_side_effects=True, vmem_limit_bytes=VMEM_LIMIT
+        ),
+    )(*grads, small)
+
+
+def weight_list(shards):
+    names = ("qkv", "out", "up", "down", "unpatch")
+    parts = (4, 1, 4, 4, 2)
+    return tuple(
+        Matrix(name, shard.shape[0], shard.shape[1], name == "down", part)
+        for name, shard, part in zip(names, shards, parts)
+    )
 
 
 def matmul(left, right):
@@ -77,20 +502,6 @@
 
 def join_heads(stacked):
     return stacked.transpose(1, 0, 2).reshape(stacked.shape[1], stacked.shape[0] * stacked.shape[2])
-
-
-def tiles_to_whole(stacked, groups, parts):
-    tile_rows = stacked.shape[0] // (groups * parts)
-    tile_cols = stacked.shape[1]
-    blocks = stacked.reshape(groups, parts, tile_rows, tile_cols).transpose(0, 2, 1, 3)
-    return blocks.reshape(groups * tile_rows, parts * tile_cols)
-
-
-def whole_to_tiles(whole, groups, parts):
-    tile_rows = whole.shape[0] // groups
-    tile_cols = whole.shape[1] // parts
-    blocks = whole.reshape(groups, tile_rows, parts, tile_cols).transpose(0, 2, 1, 3)
-    return blocks.reshape(groups * parts * tile_rows, tile_cols)
 
 
 def shards(
@@ -123,23 +534,20 @@
     head_dim = width // HEADS
     scale = head_dim ** (-0.5)
     bfloat = jnp.bfloat16
-    gathered = (
-        lax.all_gather(w_qkv.astype(bfloat), ("dp", "seq"), axis=0, tiled=True),
-        lax.all_gather(w_out.astype(bfloat), ("dp", "seq"), axis=0, tiled=True),
-        lax.all_gather(w_up.astype(bfloat), ("dp", "seq"), axis=0, tiled=True),
-        lax.all_gather(w_down.astype(bfloat), ("dp", "seq"), axis=0, tiled=True),
-        lax.all_gather(w_unpatch.astype(bfloat), ("dp", "seq"), axis=0, tiled=True),
-        lax.all_gather(ln1_gain.astype(bfloat), ("dp", "seq"), axis=0, tiled=True),
-        lax.all_gather(ln1_bias.astype(bfloat), ("dp", "seq"), axis=0, tiled=True),
-        lax.all_gather(ln2_gain.astype(bfloat), ("dp", "seq"), axis=0, tiled=True),
-        lax.all_gather(ln2_bias.astype(bfloat), ("dp", "seq"), axis=0, tiled=True),
-    )
-    qkv_weight = tiles_to_whole(gathered[0], dp_size, seq_size)
-    out_weight = tiles_to_whole(gathered[1], dp_size, seq_size)
-    up_weight = tiles_to_whole(gathered[2], dp_size, seq_size)
-    down_weight = gathered[3]
-    unpatch_weight = tiles_to_whole(gathered[4], dp_size, seq_size)
-    gain_one, shift_one, gain_two, shift_two = [part.astype(jnp.float32) for part in gathered[5:]]
+    n = round(dp_size ** (1 / 3))
+    shards_of = (w_qkv, w_out, w_up, w_down, w_unpatch)
+    matrices = weight_list(shards_of)
+    device = lax.axis_index("dp") * seq_size + lax.axis_index("seq")
+    gains = jnp.stack([ln1_gain, ln1_bias, ln2_gain, ln2_bias])
+    spread = jnp.zeros((8, width), jnp.float32)
+    spread = lax.dynamic_update_slice(spread, gains, (0, device * gains.shape[1]))
+    *wholes, gains_all = gather_weights(n, seq_size, matrices, shards_of, spread)
+    qkv_weight, out_weight, up_weight, down_weight, unpatch_weight = [
+        w.reshape(-1, w.shape[-1]) for w in wholes
+    ]
+    gain_one, shift_one, gain_two, shift_two = [
+        lax.reduce_precision(gains_all[i], 8, 7) for i in range(4)
+    ]
     norm_one, normed_one, inverse_one = norm_forward(rows_in, gain_one, shift_one)
     hidden_one = norm_one.astype(bfloat)
     qkv = matmul(hidden_one, qkv_weight).astype(bfloat)
@@ -209,7 +617,6 @@
     grad_w_one = exact_tn(features, grad_dec_pre)
     grad_b_one = jnp.sum(grad_dec_pre, axis=0)
     grad_features = exact_nt(grad_dec_pre, dec_w1)
-    decoder_sums = lax.psum((grad_w_one, grad_b_one, grad_w_two, grad_b_two), ("dp", "seq"))
     spread_grads = grad_features.reshape(samples, 3, CH).transpose(1, 0, 2).reshape(-1, CH)
     grad_table = jnp.zeros(table.shape, jnp.float32).at[flat_rows].add(spread_grads)
     own_grad_texels = (
@@ -223,20 +630,20 @@
         .astype(bfloat)
     )
     grad_planes = matmul_nt(own_grad_texels, unpatch_weight)
-    grad_unpatch = whole_to_tiles(matmul_tn(plane_rows, own_grad_texels), dp_size, seq_size)
+    grad_unpatch = matmul_tn(plane_rows, own_grad_texels)
     grad_layer = jnp.concatenate(
         [grad_planes, jnp.zeros((tok_dev - plane_dev, width), jnp.float32)], axis=0
     )
     grad_layer_low = grad_layer.astype(bfloat)
     grad_down = matmul_tn(activated, grad_layer_low)
     grad_pre = act_pull(matmul_nt(grad_layer_low, down_weight))[0].astype(bfloat)
-    grad_up = whole_to_tiles(matmul_tn(hidden_two, grad_pre), dp_size, seq_size)
+    grad_up = matmul_tn(hidden_two, grad_pre)
     grad_norm_two, grad_gain_two, grad_shift_two = norm_backward(
         matmul_nt(grad_pre, up_weight), normed_two, inverse_two, gain_two
     )
     grad_after = grad_layer + grad_norm_two
     grad_after_low = grad_after.astype(bfloat)
-    grad_out_weight = whole_to_tiles(matmul_tn(mixed, grad_after_low), dp_size, seq_size)
+    grad_out_weight = matmul_tn(mixed, grad_after_low)
     grad_mixed = matmul_nt(grad_after_low, out_weight).astype(bfloat)
     grad_heads = split_heads(grad_mixed, HEADS)
 
@@ -267,24 +674,32 @@
     grad_qkv = jnp.concatenate(
         [join_heads(grad_query), own_key_grad, own_value_grad], axis=1
     ).astype(bfloat)
-    grad_qkv_weight = whole_to_tiles(matmul_tn(hidden_one, grad_qkv), dp_size, seq_size)
+    grad_qkv_weight = matmul_tn(hidden_one, grad_qkv)
     grad_norm_one, grad_gain_one, grad_shift_one = norm_backward(
         matmul_nt(grad_qkv, qkv_weight), normed_one, inverse_one, gain_one
     )
     grad_tokens = grad_after + grad_norm_one
-    block_sums = (
-        lax.psum_scatter(grad_qkv_weight, ("dp", "seq"), scatter_dimension=0, tiled=True),
-        lax.psum_scatter(grad_out_weight, ("dp", "seq"), scatter_dimension=0, tiled=True),
-        lax.psum_scatter(grad_up, ("dp", "seq"), scatter_dimension=0, tiled=True),
-        lax.psum_scatter(grad_down, ("dp", "seq"), scatter_dimension=0, tiled=True),
-        lax.psum_scatter(grad_unpatch, ("dp", "seq"), scatter_dimension=0, tiled=True),
-        lax.psum_scatter(grad_gain_one, ("dp", "seq"), scatter_dimension=0, tiled=True),
-        lax.psum_scatter(grad_shift_one, ("dp", "seq"), scatter_dimension=0, tiled=True),
-        lax.psum_scatter(grad_gain_two, ("dp", "seq"), scatter_dimension=0, tiled=True),
-        lax.psum_scatter(grad_shift_two, ("dp", "seq"), scatter_dimension=0, tiled=True),
-    )
-    sum_qkv, sum_out, sum_up, sum_down, sum_unpatch = block_sums[:5]
-    sum_gain_one, sum_shift_one, sum_gain_two, sum_shift_two = block_sums[5:]
+    whole_grads = [
+        grad.astype(bfloat).reshape(m.shape(n, seq_size))
+        for m, grad in zip(matrices, (grad_qkv_weight, grad_out_weight, grad_up, grad_down, grad_unpatch))
+    ]
+    small_parts = [grad_gain_one, grad_shift_one, grad_gain_two, grad_shift_two]
+    small_parts += [grad_w_one, grad_b_one, grad_w_two, grad_b_two]
+    flat = jnp.concatenate([part.reshape(-1) for part in small_parts])
+    lanes = 128
+    padded = -(-flat.shape[0] // (8 * lanes)) * 8 * lanes
+    small = jnp.pad(flat, (0, padded - flat.shape[0])).reshape(-1, lanes)
+    *block_sums, small_sums = scatter_grads(n, seq_size, matrices, whole_grads, small)
+    flat_sums, at, sums = small_sums.reshape(-1), 0, []
+    for part in small_parts:
+        sums.append(flat_sums[at : at + part.size].reshape(part.shape))
+        at += part.size
+    own = width // (dp_size * seq_size)
+    sum_qkv, sum_out, sum_up, sum_down, sum_unpatch = block_sums
+    sum_gain_one, sum_shift_one, sum_gain_two, sum_shift_two = [
+        lax.dynamic_slice(part, (device * own,), (own,)) for part in sums[:4]
+    ]
+    decoder_sums = sums[4:]
     return (
         density[None],
         color_value.T[None],

time: 2190 us -> 1010 us (0.46)
  waiting for transfers between devices: 1510 us -> 247 us
  Pallas kernels: 0 us -> 297 us
  local copies, waits for them, and re-layouts: 216 us -> 113 us
  blocking collectives: 83.5 us -> 0 us
    reduce_scatter x7 -> x0, waiting for transfers between devices: 1150 us -> none  [the longest x1 366 us: shards(): lax.psum_scatter(grad_up, ('dp', 'seq'), scatter_dimension=0, tiled=True)]
    pallas_call x0 -> x2, Pallas kernels: none -> 297 us  [the longest x1 149 us: scatter_grads(): pl.pallas_call(functools.partial(scatter_kernel, n, seq_size, matrices),...]
    all_gather x5 -> x0, waiting for transfers between devices: 166 us -> none  [the longest x1 60.2 us: shards(): lax.all_gather(w_unpatch.astype(bfloat), ('dp', 'seq'), axis=0, tiled=True)]
    unnamed x2 -> x0, blocking collectives: 83.5 us -> none
    reshape x7 -> x4, local copies, waits for them, and re-layouts: 65.9 us -> 0.87 us  [the longest x1 0.62 us: shards(): small = jnp.pad(flat, (0, padded - flat.shape[0])).reshape(-1, lanes)]
    unnamed x16 -> x8, waiting for transfers between devices: 0.78 us -> 52.1 us
    transpose x2 -> x0, local copies, waits for them, and re-layouts: 26.9 us -> none  [whole_to_tiles(): whole.reshape(groups, tile_rows, parts, tile_cols).transpose(0, 2, 1, 3)]
  transfers between devices with their start and end apart: 16 -> 6, of which waited for: 15 -> 6; matrix products, arithmetic and copies ran while one was open for 13% -> 4% of each run, Pallas kernels for 0% -> 0%
where the time goes in v1:
time: 1010 us; the launch traced here: 1000 us
  Pallas kernels  297 us (29%)
  waiting for transfers between devices  247 us (24%)
  matrix products  236 us (23%)
  local copies, waits for them, and re-layouts  113 us (11%)
  other arithmetic  94.2 us (9%)
  between operations  15.1 us (1%)
    pallas_call x1, Pallas kernels, scatter_grads(): pl.pallas_call(functools.partial(scatter_kernel, n, seq_size, matrices),...  149 us
    pallas_call x1, Pallas kernels, gather_weights(): pl.pallas_call(functools.partial(gather_kernel, n, seq_size, matrices), o...  148 us
    dot_general x53, matrix products, matmul_nt(): lax.dot_general(left, right, (((1,), (1,)), ((), ())), preferred_element_...  87.2 us
    dot_general x37, matrix products, matmul_tn(): lax.dot_general(left, right, (((0,), (0,)), ((), ())), preferred_element_...  75.5 us
    dot_general x37, matrix products, matmul(): return jnp.dot(left, right, preferred_element_type=jnp.float32)  66.7 us
    all_gather x1, waiting for transfers between devices, shards(): texels = lax.all_gather(own_texels, 'seq', axis=0, tiled=True)  61.3 us
    reduce_scatter x1, waiting for transfers between devices, shards(): lax.psum_scatter(grad_table.reshape(texels.shape).astype(jnp.bfloat16), '...  59 us
    unnamed x8, waiting for transfers between devices  52.1 us
  transfers between devices with their start and end apart: 6, of which 6 were waited for; matrix products, arithmetic and copies ran while one was open for 4% of the time, Pallas kernels for 0%

profile of v1, /device:TPU:0, one launch (start us, length us, event | category | flops | bytes accessed | tf_op | source)
XLA Modules:
  0.0 1004.0 jit_solution(12505551067839142546)
XLA Ops:
  9.1 147.9 %shard_map.297 = (bf16[2,2,2,128,3072]{4,3,2,1,0:T(8,128)(2,1)}, bf16[2,2,2,128,1024]{4,3,2,1,0:T(8,128)(2,1)}, bf16[2,2,2,128,4096]{4,3,2,1,0:T(8,128)(2,1)}, b...) custom-call(f32[128,768]{1,0:T(8,128)} %refs_0_.1, ...), custom_call_target="tpu_custom_call" | custom-call | tf_op jit(solution)/shard_map/pallas_call | solution.py:221
  160.7 4.5 convolution_convert_fusion.3
  167.8 40.3 %all-gather.4.cloned.1.call-done = bf16[896,1024]{1,0:T(8,128)(2,1)} async-done(((bf16[224,1024]{1,0:T(8,128)(2,1)}), bf16[896,1024]{1,0:T(8,128)(2,1)}) %all-gather.4.cloned.1.call-update) | async-done | bytes 1835024 | tf_op jit(solution)/shard_map/all_gather | solution.py:555
  208.2 3.8 copy.79
  212.0 4.6 copy.82
  216.6 34.0 %all-gather.6.cloned.1.call-done = bf16[896,1024]{1,0:T(8,128)(2,1)} async-done(((bf16[224,1024]{1,0:T(8,128)(2,1)}), bf16[896,1024]{1,0:T(8,128)(2,1)}) %all-gather.6.cloned.1.call-update) | async-done | bytes 1835024 | tf_op jit(solution)/shard_map/all_gather | solution.py:556
  250.6 3.8 copy.80
  254.4 4.6 copy.83
  259.0 59.3 %while.28 = (s32[]{:T(128)}, bf16[16,224,64]{1,2,0:T(8,128)(2,1)S(1)}, f32[16,224]{1,0:T(8,128)S(1)}, bf16[16,224,64]{2,1,0:T(8,128)(2,1)S(1)}, bf16[16,896,64]{...) while((s32[]{:T(128)}, ...), condition=%wide.region_5.6_spmd.clone, body=%wide.region_2.5_spmd.clone.sunk | while | flops 53001760 | bytes 3003365 | solution.py:577
  318.4 2.9 fusion.141
  321.6 14.1 %multiply_convert_fusion.1 = (bf16[224,4096]{1,0:T(8,128)(2,1)S(1)}, f32[224,4096]{1,0:T(8,128)}, f32[224,4096]{1,0:T(8,128)}) fusion(bf16[1024,4096]{1,0:T(8,128)(2,1)} %bitcast.311, f32[224,1024]{1,0:T(8,128)S(1)} %get-tuple-element.354, f32[1024]{0:T(1024)S(1)} %bitcast.293, f32[1024]{0:T(1024)S(1)} %bitcast.289, f32[224]{0:T(256)S(1)} %add_rsqrt_fusion, ...), kind=kOutput, calls=%fused_computation.100 | convolution fusion | flops 1939832832 | bytes 18491136 | tf_op jit(solution)/shard_map/dot_general | solution.py:442
  335.7 2.1 fusion.143
  338.7 1.9 convolution_convert_fusion.5
  341.9 61.3 %all-gather.8.cloned.1.call-done = bf16[768,2048]{1,0:T(8,128)(2,1)} async-done(((bf16[192,2048]{1,0:T(8,128)(2,1)}), bf16[768,2048]{1,0:T(8,128)(2,1)}) %all-gather.8.cloned.1.call-update) | async-done | bytes 3145744 | tf_op jit(solution)/shard_map/all_gather | solution.py:588
  403.2 15.4 %reshape.626 = bf16[49152,32]{1,0:T(8,128)(2,1)} reshape(bf16[768,2048]{1,0:T(8,128)(2,1)} %all-gather.8.cloned.1.call-done) | data formatting | bytes 6291456 | tf_op jit(solution)/shard_map/reshape | solution.py:589
  418.6 22.7 %gather_fusion = bf16[6144,32]{1,0:T(8,128)(2,1)S(1)} fusion(bf16[49152,32]{1,0:T(8,128)(2,1)} %reshape.626, s32[6144]{0:T(1024)S(1)} %broadcast_clamp_fusion), kind=kCustom, calls=%fused_computation | custom fusion | bytes 811008 | tf_op jit(solution)/shard_map/jit(_take)/gather | solution.py:600
  448.0 2.3 copy.99
  450.3 43.5 %scatter_custom_fusion = f32[49152,32]{1,0:T(8,128)} fusion(s32[6144]{0:T(1024)S(1)} %bitcast.299, f32[6144,32]{1,0:T(8,128)} %bitcast.278, f32[]{:T(128)} %constant.266.clone.1), kind=kCustom, calls=%fused_computation.90 | custom fusion | flops 196608 | bytes 6291968 | tf_op jit(solution)/shard_map/scatter-add | solution.py:621
  493.9 13.1 %convert_element_type.109 = bf16[49152,32]{1,0:T(8,128)(2,1)} convert(f32[49152,32]{1,0:T(8,128)} %scatter_custom_fusion) | non-fusion elementwise | flops 1572864 | bytes 9437184 | tf_op jit(solution)/shard_map/convert_element_type | solution.py:624
  507.0 17.3 %convert_element_type.110 = bf16[768,2048]{1,0:T(8,128)(2,1)} reshape(bf16[49152,32]{1,0:T(8,128)(2,1)} %convert_element_type.109) | data formatting | bytes 6291456 | tf_op jit(solution)/shard_map/convert_element_type | solution.py:624
  524.4 59.0 %reduce-scatter.8.cloned.1.call-done = bf16[192,2048]{1,0:T(8,128)(2,1)} async-done(((bf16[768,2048]{1,0:T(8,128)(2,1)}), bf16[192,2048]{1,0:T(8,128)(2,1)}) %reduce-scatter.8.cloned.1.call-update) | async-done | bytes 786448 | tf_op jit(solution)/shard_map/reduce_scatter | solution.py:623
  583.4 4.1 fusion.145
  587.5 9.5 add_convert_fusion
  597.1 3.0 multiply_reduce_fusion.1
  603.5 129.2 %while.29 = (s32[]{:T(128)}, bf16[16,224,64]{1,2,0:T(8,128)(2,1)S(1)}, bf16[16,896,64]{1,2,0:T(8,128)(2,1)}, bf16[16,896,64]{1,2,0:T(8,128)(2,1)}, bf16[16,224,6...) while((s32[]{:T(128)}, ...), condition=%wide.region_14.15_spmd.clone, body=%wide.region_12.14_spmd.clone.sunk | while | flops 130344480 | bytes 7425269 | solution.py:663
  607.1 1.7 fusion.211
  631.3 1.7 fusion.211
  639.4 1.7 fusion.211
  647.5 1.7 fusion.211
  687.8 1.7 fusion.211
  695.9 1.7 fusion.211
  712.1 1.7 fusion.211
  728.2 1.7 fusion.211
  732.8 4.0 copy.100
  736.9 4.0 copy.102
  741.0 1.8 fusion.98
  746.0 3.1 convolution_convert_fusion.6
  749.1 3.3 convolution_convert_fusion.4
  752.5 5.6 convolution_convert_fusion
  758.1 5.7 convolution_convert_fusion.1
  763.8 12.6 %reduce-scatter.10.cloned.1.call-done = bf16[224,1024]{1,0:T(8,128)(2,1)} async-done(((bf16[896,1024]{1,0:T(8,128)(2,1)}), bf16[224,1024]{1,0:T(8,128)(2,1)}) %reduce-scatter.10.cloned.1.call-update) | async-done | bytes 458768
  776.5 2.0 copy.101
  778.5 38.7 %reduce-scatter.12.cloned.1.call-done = bf16[224,1024]{1,0:T(8,128)(2,1)} async-done(((bf16[896,1024]{1,0:T(8,128)(2,1)}), bf16[224,1024]{1,0:T(8,128)(2,1)}) %reduce-scatter.12.cloned.1.call-update) | async-done | bytes 458768
  817.2 2.0 copy.103
  819.2 5.6 multiply_reduce_fusion.2
  824.8 4.7 convolution_convert_fusion.2
  830.3 148.8 %shard_map.298 = (f32[128,768]{1,0:T(8,128)}, f32[128,256]{1,0:T(8,128)}, f32[128,1024]{1,0:T(8,128)}, f32[128,1024]{1,0:T(8,128)}, f32[128,512]{1,0:T(8,128)}, /*index=5*/f32[88,128]{1,0:T(8,128)}) custom-call(bf16[2,2,2,128,3072]{4,3,2,1,0:T(8,128)(2,1)} %bitcast.272, bf16[2,2,2,128,1024]{4,3,2,1,0:T(8,128)(2,1)} %bitcast.267, ...), custom_call_target="tpu_custom_call" | custom-call | tf_op jit(solution)/shard_map/pallas_call | solution.py:399
  979.1 3.4 slice.92
  (375 shorter events, 212.7 us)
Async XLA Ops:
  7.2 436.5 %copy-start = (f32[96,64]{0,1:T(8,128)S(1)}, f32[96,64]{0,1:T(8,128)}, u32[]{:S(2)}) copy-start(f32[96,64]{0,1:T(8,128)} %param.32) | copy-start | bytes 73732
  7.2 153.5 %copy-start.3 = (f32[1,224,1024]{2,1,0:T(8,128)S(1)}, f32[1,224,1024]{2,1,0:T(8,128)}, u32[]{:S(2)}) copy-start(f32[1,224,1024]{2,1,0:T(8,128)} %param.22) | copy-start | bytes 2752516
  7.2 200.9 %all-gather.4.cloned.1.call-start = ((), (), s32[]{:S(2)}) async-start(), calls=%async_computation.3 | async-start | bytes 2293760 | tf_op jit(solution)/shard_map/all_gather | solution.py:555
  8.4 0.6 copy-start.27
  166.2 84.4 %all-gather.6.cloned.1.call-start = ((), (), s32[]{:S(2)}) async-start(), calls=%async_computation.4 | async-start | bytes 2293760 | tf_op jit(solution)/shard_map/all_gather | solution.py:556
  167.0 236.2 %all-gather.8.cloned.1.call-start = ((), (), s32[]{:S(2)}) async-start(), calls=%async_computation.5 | async-start | bytes 3932160 | tf_op jit(solution)/shard_map/all_gather | solution.py:588
  318.3 17.3 %copy-start.9 = (bf16[16,224,64]{1,2,0:T(8,128)(2,1)}, bf16[16,224,64]{1,2,0:T(8,128)(2,1)S(1)}, u32[]{:S(2)}) copy-start(bf16[16,224,64]{1,2,0:T(8,128)(2,1)S(1)} %get-tuple-element.122) | copy-start | bytes 1376260
  318.4 17.3 %copy-start.12 = (bf16[16,224,64]{2,1,0:T(8,128)(2,1)}, bf16[16,224,64]{2,1,0:T(8,128)(2,1)S(1)}, u32[]{:S(2)}) copy-start(bf16[16,224,64]{2,1,0:T(8,128)(2,1)S(1)} %get-tuple-element.582) | copy-start | bytes 1376260
  318.4 17.3 %slice-start.2 = ((s8[8388608]{0:T(1024)(128)(4,1)}), s8[4194304]{0:T(1024)(128)(4,1)S(1)}, s32[]{:S(2)}) async-start(s8[8388608]{0:T(1024)(128)(4,1)} %bitcast.316), calls=%async_computation.11 | async-start | bytes 8388608
  321.6 14.1 %slice-start.3 = ((s8[8388608]{0:T(1024)(128)(4,1)}), s8[4194304]{0:T(1024)(128)(4,1)S(1)}, s32[]{:S(2)}) async-start(s8[8388608]{0:T(1024)(128)(4,1)} %bitcast.316), calls=%async_computation.12 | async-start | bytes 8388608
  335.7 2.2 copy-start.10
  335.7 3.0 copy-start.2
  337.8 3.0 copy-start.29
  338.0 0.7 copy-start.7
  340.7 242.7 %reduce-scatter.8.cloned.1.call-start = ((), (), s32[]{:S(2)}) async-start(), calls=%async_computation.6 | async-start | bytes 3932160 | tf_op jit(solution)/shard_map/reduce_scatter | solution.py:623
  418.6 25.1 %copy-start.34 = (f32[64]{0:T(128)S(1)}, f32[64]{0:T(128)}, u32[]{:S(2)}) copy-start(f32[64]{0:T(128)} %param.33) | copy-start | bytes 772
  443.6 1.5 copy-start.19
  443.7 1.5 copy-start.32
  443.7 1.5 copy-start.33
  443.7 1.9 copy-start.30
  443.7 2.0 copy-start.31
  445.2 2.3 copy-start.14
  445.2 2.3 copy-start.15
  446.6 0.9 copy-start.16
  524.3 252.1 %reduce-scatter.10.cloned.1.call-start = ((), (), s32[]{:S(2)}) async-start(), calls=%async_computation.7 | async-start | bytes 2293760
  583.4 13.7 %slice-start = ((s8[8388608]{0:T(1024)(128)(4,1)}), s8[4194304]{0:T(1024)(128)(4,1)S(1)}, s32[]{:S(2)}) async-start(s8[8388608]{0:T(1024)(128)(4,1)} %bitcast.312), calls=%async_computation.9 | async-start | bytes 8388608
  587.5 12.6 %copy-start.5 = (f32[192,1024]{1,0:T(8,128)}, f32[192,1024]{1,0:T(8,128)S(1)}, u32[]{:S(2)}) copy-start(f32[192,1024]{1,0:T(8,128)S(1)} %fusion.145) | copy-start | bytes 2359300
  587.5 9.5 slice-start.1
  597.1 3.0 copy-start.17
  600.1 1.6 copy-start.4
  732.8 8.2 copy-start.20
  736.9 80.3 %reduce-scatter.12.cloned.1.call-start = ((), (), s32[]{:S(2)}) async-start(), calls=%async_computation.8 | async-start | bytes 2293760
  740.9 8.2 copy-start.8
  744.6 4.5 copy-start.13
  749.1 3.3 copy-start.6
  749.1 3.3 copy-start.11
  752.5 5.6 copy-start.18
  758.1 61.1 %copy-start.21 = (bf16[16,224,64]{1,2,0:T(8,128)(2,1)S(1)}, bf16[16,224,64]{1,2,0:T(8,128)(2,1)}, u32[]{:S(2)}) copy-start(bf16[16,224,64]{1,2,0:T(8,128)(2,1)} %copy-done.20) | copy-start | bytes 1376260
  819.2 5.6 copy-start.24
  819.2 5.6 copy-start.25
  979.1 13.9 %copy-start.28 = (f32[128,256]{1,0:T(8,128)S(1)}, f32[128,256]{1,0:T(8,128)}, u32[]{:S(2)}) copy-start(f32[128,256]{1,0:T(8,128)} %get-tuple-element.558) | copy-start | bytes 393220
  979.1 15.3 %copy-start.22 = (f32[128,1024]{1,0:T(8,128)S(1)}, f32[128,1024]{1,0:T(8,128)}, u32[]{:S(2)}) copy-start(f32[128,1024]{1,0:T(8,128)} %get-tuple-element.562) | copy-start | bytes 1572868
  988.6 3.6 copy-start.26
  988.6 5.0 copy-start.23
  990.9 5.9 copy-start.1
Sparse Core Ops, SparseCore 0:
  166.3 41.7 all-gather.3
  210.3 40.2 all-gather.5
  340.8 62.3 all-gather.7
  524.4 58.8 reduce-scatter.7
  737.0 39.4 reduce-scatter.9
  778.6 38.5 reduce-scatter.11

commit v2 on v1

--- a/solution.py
+++ b/solution.py
@@ -1,4 +1,5 @@
 import functools
+import math
 
 import jax
 import jax.numpy as jnp
@@ -17,6 +18,7 @@
 NEGATIVE = -1e30
 VMEM_LIMIT = 56 * 2**20
 AHEAD = 3
+LAG = 2
 
 
 MESH = pl.DeviceIdType.MESH
@@ -47,10 +49,10 @@
         size = self.size(axis)
         return lax.rem(self.me(axis) + (size - step), size)
 
-    def enter(self):
+    def enter(self, axes=(0, 1, 2, 3)):
         barrier = pltpu.get_barrier_semaphore()
         count = 0
-        for axis in range(4):
+        for axis in axes:
             for step in range(1, self.size(axis)):
                 pl.semaphore_signal(
                     barrier, inc=1, device_id=self.peer(axis, step)[1], device_id_type=MESH
@@ -89,23 +91,35 @@
         return (count, size, self.cols) if self.by_rows else (size, count * self.cols)
 
 
-def small_sum(place, value, slots, send, recv):
-    for stage, axis in enumerate((2, 1, 0, 3)):
-        me = place.me(axis)
-        slots[stage, me] = value
-        copies = []
-        for step in range(1, place.size(axis)):
-            ref = slots.at[stage, me]
-            copy = remote(
-                ref, ref, send.at[stage, step - 1], recv.at[stage, step - 1], place.peer(axis, step)[1]
-            )
-            copy.start()
-            copies.append(copy)
+def small_stage(place, value, slots, send, recv, stage, axis):
+    me = place.me(axis)
+    slots[stage, me] = value
+    copies = []
+    for step in range(1, place.size(axis)):
+        ref = slots.at[stage, me]
+        copy = remote(
+            ref, ref, send.at[stage, step - 1], recv.at[stage, step - 1], place.peer(axis, step)[1]
+        )
+        copy.start()
+        copies.append(copy)
+
+    def end():
         for copy in copies:
             copy.wait()
-        value = slots[stage, 0]
+        total = slots[stage, 0]
         for other in range(1, place.size(axis)):
-            value = value + slots[stage, other]
+            total = total + slots[stage, other]
+        return total
+
+    return end
+
+
+def small_sum(place, value, slots, send, recv, between=None):
+    for stage, axis in enumerate((2, 1, 0, 3)):
+        end = small_stage(place, value, slots, send, recv, stage, axis)
+        if between is not None:
+            between()
+        value = end()
     return value
 
 
@@ -171,71 +185,6 @@
 def gather_sems(n, seq_size, chunks):
     sem = pltpu.SemaphoreType.DMA
     return [sem((chunks, seq_size - 1))] * 2 + [sem((chunks, 4, n - 1))] * 2 + [sem((chunks, n - 1))] * 2
-
-
-def gather_kernel(n, seq_size, matrices, *refs):
-    count = len(matrices)
-    shards, gains, wholes, gains_out = refs[:count], refs[count], refs[count + 1 : 2 * count + 1], refs[2 * count + 1]
-    rest = refs[2 * count + 2 :]
-    bufs, (slots, small_send, small_recv, out_sem), sems = rest[:count], rest[count : count + 4], rest[count + 4 :]
-    place = Place(n, seq_size)
-    for matrix, shard, buf in zip(matrices, shards, bufs):
-        if matrix.by_rows:
-            buf[place.i + (place.seq,)] = shard[...].astype(jnp.bfloat16)
-        else:
-            at = pl.ds(pl.multiple_of(place.seq * matrix.cols, 128), matrix.cols)
-            buf[place.i + (slice(None), at)] = shard[...].astype(jnp.bfloat16)
-    place.enter()
-    gather = Gather(place, matrices, bufs, sems)
-    total = len(gather.chunks)
-    for k in range(AHEAD):
-        gather.along_seq(k)
-    gains_out[...] = small_sum(place, gains[...], slots, small_send, small_recv)
-    outs = []
-    for t in range(total + 6):
-        if t < total:
-            gather.hop(t, 0)
-            if t + AHEAD < total:
-                gather.along_seq(t + AHEAD)
-        if 0 <= t - 2 < total:
-            gather.hop(t - 2, 1)
-        if 0 <= t - 4 < total:
-            gather.third(t - 4)
-        if 0 <= t - 6 < total:
-            gather.arrived(t - 6)
-            w, matrix, part = gather.chunks[t - 6]
-            index = (slice(None),) * 3 + matrix.tail(part, 0, seq_size)
-            copy = pltpu.make_async_copy(bufs[w].at[index], wholes[w].at[index], out_sem.at[t - 6])
-            copy.start()
-            outs.append(copy)
-    gather.finish()
-    for copy in outs:
-        copy.wait()
-
-
-def gather_weights(n, seq_size, matrices, shards, gains):
-    chunks = sum(m.parts for m in matrices)
-    vmem, any_space = pl.BlockSpec(memory_space=pltpu.VMEM), pl.BlockSpec(memory_space=pl.ANY)
-    shapes = [m.shape(n, seq_size) for m in matrices]
-    largest = max(n, seq_size)
-    return pl.pallas_call(
-        functools.partial(gather_kernel, n, seq_size, matrices),
-        out_shape=[jax.ShapeDtypeStruct(s, jnp.bfloat16) for s in shapes]
-        + [jax.ShapeDtypeStruct(gains.shape, jnp.float32)],
-        in_specs=[vmem] * (len(matrices) + 1),
-        out_specs=[any_space] * len(matrices) + [vmem],
-        scratch_shapes=[pltpu.VMEM(s, jnp.bfloat16) for s in shapes]
-        + [
-            pltpu.VMEM((4, largest) + gains.shape, jnp.float32),
-            pltpu.SemaphoreType.DMA((4, largest - 1)),
-            pltpu.SemaphoreType.DMA((4, largest - 1)),
-            pltpu.SemaphoreType.DMA((chunks,)),
-        ]
-        + gather_sems(n, seq_size, chunks),
-        compiler_params=pltpu.CompilerParams(
-            collective_id=0, has_side_effects=True, vmem_limit_bytes=VMEM_LIMIT
-        ),
-    )(*shards, gains)
 
 
 class Scatter:
@@ -429,6 +378,430 @@
     )(*grads, small)
 
 
+def gelu_parts(x):
+    cdf = 0.5 + 0.5 * lax.erf(x * (0.5**0.5))
+    return x * cdf, cdf + x * (jnp.exp(-0.5 * x * x) * (2.0 * math.pi) ** -0.5)
+
+
+def split_low(x):
+    high = x.astype(jnp.bfloat16)
+    return high, (x - high.astype(jnp.float32)).astype(jnp.bfloat16)
+
+
+def texel_place(texel, seq_size, me):
+    side, quarter = PRES * PATCH, PRES * PRES // seq_size
+    row, col = texel // side, texel % side
+    token = row // PATCH * PRES + col // PATCH
+    a, b = row % PATCH, col % PATCH
+    fold = PATCH // 2
+    mine = token // quarter == me
+    key = jnp.where(mine, a // 2 * quarter + token % quarter, -1)
+    return key, a % 2 * PATCH + b, fold
+
+
+def decode_kernel(
+    n,
+    seq_size,
+    tile,
+    texels,
+    index,
+    w1,
+    b1,
+    w2,
+    b2,
+    d_density,
+    d_color,
+    density,
+    color,
+    grad_texels,
+    g_w1,
+    g_b1,
+    g_w2,
+    g_b2,
+    tables,
+    grad_tables,
+    features,
+    part_out,
+    part_in,
+    own_part,
+    grad_all,
+    sems,
+):
+    send_sem, recv_sem, back_send, back_recv = sems
+    place = Place(n, seq_size)
+    bfloat, f32 = jnp.bfloat16, jnp.float32
+    samples = index.shape[2]
+    quarter = PRES * PRES // seq_size
+    width = texels.shape[1]
+    groups = 2 * PATCH
+    cols = groups * CH
+    depth = width // cols * quarter
+    hidden = w1.shape[1]
+    place.enter((3,))
+    for p in range(3):
+        own = texels[p * quarter : (p + 1) * quarter].astype(f32)
+        stacked = jnp.concatenate([own[:, i * cols : (i + 1) * cols] for i in range(width // cols)], axis=0)
+        tables[p] = stacked.T.astype(bfloat)
+    w1_high, w1_low = split_low(w1[...])
+    w1_stack = jnp.concatenate([w1_high, w1_low], axis=1)
+    tiles = samples // tile
+
+    def one_hot(source, at, p):
+        texel = index[source, pl.ds(p, 1), at]
+        key, group, _ = texel_place(texel, seq_size, place.seq)
+        rows = lax.broadcasted_iota(jnp.int32, (depth, tile), 0)
+        return (rows == key).astype(f32).astype(bfloat), group
+
+    def forward(source):
+        @pl.loop(0, tiles)
+        def _(t):
+            at = pl.ds(pl.multiple_of(t * tile, tile), tile)
+            picked = []
+            for p in range(3):
+                hot, group = one_hot(source, at, p)
+                spread = matmul(tables[p], hot)
+                total = jnp.where(group == 0, spread[:CH], 0.0)
+                for g in range(1, groups):
+                    total = total + jnp.where(group == g, spread[g * CH : (g + 1) * CH], 0.0)
+                picked.append(total)
+            feature = jnp.concatenate(picked, axis=0).astype(bfloat)
+            features[source, :, at] = feature
+            both = matmul_tn(w1_stack, feature)
+            part = both[:hidden] + both[hidden:]
+            own_part[:, at] = part
+            part_out[source, :, at] = part.astype(bfloat)
+
+    copies = []
+    for step in range(1, seq_size):
+        to, device = place.peer(3, step)
+        forward(to)
+        copy = remote(part_out.at[to], part_in.at[step - 1], send_sem.at[step - 1], recv_sem.at[step - 1], device)
+        copy.start()
+        copies.append(copy)
+    forward(place.seq)
+    pre = own_part[...] + b1[...]
+    for step, copy in enumerate(copies):
+        copy.wait_recv()
+        pre = pre + part_in[step].astype(f32)
+    act, slope = gelu_parts(pre)
+    highest = lax.Precision.HIGHEST
+    out = lax.dot_general(
+        w2[...], act, (((0,), (0,)), ((), ())), precision=highest, preferred_element_type=f32
+    ) + b2[...]
+    gate = 1.0 / (1.0 + jnp.exp(-out))
+    first = out[:1]
+    density[...] = jnp.maximum(first, 0.0) + jnp.log1p(jnp.exp(-jnp.abs(first)))
+    color[...] = gate[1:4]
+    grad_out = jnp.concatenate(
+        [
+            d_density[...] * gate[:1],
+            d_color[...] * gate[1:4] * (1.0 - gate[1:4]),
+            jnp.zeros((w2.shape[1] - 4, samples), f32),
+        ],
+        axis=0,
+    )
+    grad_pre = jnp.dot(w2[...], grad_out, precision=highest, preferred_element_type=f32) * slope
+    me = place.seq
+    grad_all[me] = grad_pre.astype(bfloat)
+    backs = []
+    for step in range(1, seq_size):
+        ref = grad_all.at[me]
+        copy = remote(ref, ref, back_send.at[step - 1], back_recv.at[step - 1], place.peer(3, step)[1])
+        copy.start()
+        backs.append(copy)
+    g_w2[...] = lax.dot_general(
+        grad_out, act, (((1,), (1,)), ((), ())), precision=highest, preferred_element_type=f32
+    )
+    g_b2[...] = jnp.sum(grad_out, axis=1, keepdims=True)
+    g_b1[...] = jnp.sum(grad_pre, axis=1, keepdims=True)
+    g_w1[...] = jnp.zeros(g_w1.shape, f32)
+    grad_tables[...] = jnp.zeros(grad_tables.shape, f32)
+
+    def backward(source):
+        @pl.loop(0, tiles)
+        def _(t):
+            at = pl.ds(pl.multiple_of(t * tile, tile), tile)
+            grad = grad_all[source, :, at]
+            g_w1[...] += matmul_nt(features[source, :, at], grad)
+            grad_feature = matmul(w1_high, grad) + matmul(w1_low, grad)
+            for p in range(3):
+                hot, group = one_hot(source, at, p)
+                mine = grad_feature[p * CH : (p + 1) * CH]
+                spread = jnp.concatenate(
+                    [jnp.where(group == g, mine, 0.0) for g in range(groups)], axis=0
+                ).astype(bfloat)
+                grad_tables[p] += matmul_nt(spread, hot)
+
+    backward(me)
+    for step, copy in enumerate(backs):
+        copy.wait_recv()
+        backward(place.source(3, step + 1))
+    for p in range(3):
+        back = grad_tables[p].T
+        for i in range(width // cols):
+            grad_texels[p * quarter : (p + 1) * quarter, i * cols : (i + 1) * cols] = back[
+                i * quarter : (i + 1) * quarter
+            ].astype(bfloat)
+    for copy in copies + backs:
+        copy.wait_send()
+
+
+def decode(n, seq_size, texels, index, dec_w1, dec_b1, dec_w2, dec_b2, d_density, d_color):
+    bfloat, f32 = jnp.bfloat16, jnp.float32
+    samples, hidden = index.shape[2], dec_w1.shape[1]
+    rows = 8
+    w2 = jnp.pad(dec_w2, ((0, 0), (0, rows - dec_w2.shape[1])))
+    b2 = jnp.pad(dec_b2, (0, rows - dec_b2.shape[0]))[:, None]
+    quarter = PRES * PRES // seq_size
+    cols = 2 * PATCH * CH
+    depth = texels.shape[1] // cols * quarter
+    vmem = pl.BlockSpec(memory_space=pltpu.VMEM)
+    sem = pltpu.SemaphoreType.DMA((seq_size - 1,))
+
+    def kernel(*refs):
+        decode_kernel(n, seq_size, min(512, samples), *refs[:-4], refs[-4:])
+
+    return pl.pallas_call(
+        kernel,
+        out_shape=[
+            jax.ShapeDtypeStruct((1, samples), f32),
+            jax.ShapeDtypeStruct((3, samples), f32),
+            jax.ShapeDtypeStruct(texels.shape, bfloat),
+            jax.ShapeDtypeStruct(dec_w1.shape, f32),
+            jax.ShapeDtypeStruct((hidden, 1), f32),
+            jax.ShapeDtypeStruct((rows, hidden), f32),
+            jax.ShapeDtypeStruct((rows, 1), f32),
+        ],
+        in_specs=[vmem] * 8,
+        out_specs=[vmem] * 7,
+        scratch_shapes=[
+            pltpu.VMEM((3, cols, depth), bfloat),
+            pltpu.VMEM((3, cols, depth), f32),
+            pltpu.VMEM((seq_size, 3 * CH, samples), bfloat),
+            pltpu.VMEM((seq_size, hidden, samples), bfloat),
+            pltpu.VMEM((seq_size - 1, hidden, samples), bfloat),
+            pltpu.VMEM((hidden, samples), f32),
+            pltpu.VMEM((seq_size, hidden, samples), bfloat),
+            sem,
+            sem,
+            sem,
+            sem,
+        ],
+        compiler_params=pltpu.CompilerParams(
+            collective_id=2, has_side_effects=True, vmem_limit_bytes=VMEM_LIMIT
+        ),
+        cost_estimate=pl.CostEstimate(flops=16 * 10**9, bytes_accessed=4 * 10**6, transcendentals=0),
+    )(texels, index, dec_w1, dec_b1[:, None], w2, b2, d_density, d_color)
+
+
+def columns(ref, first, count):
+    block = ref[..., pl.ds(first, count)]
+    return block.reshape(-1, count)
+
+
+def normalize(values):
+    center = values - jnp.mean(values, axis=-1, keepdims=True)
+    inverse = lax.rsqrt(jnp.mean(center * center, axis=-1, keepdims=True) + EPSILON)
+    return center * inverse, inverse
+
+
+def forward_kernel(n, seq_size, matrices, *refs):
+    count = len(matrices)
+    refs = list(refs)
+
+    def take(k):
+        taken = refs[:k]
+        del refs[:k]
+        return taken
+
+    shards = take(count)
+    tokens, gains, index, valid = take(4)
+    wholes = take(count)
+    gains_out, index_out, hidden_all, query, keys, values, mixed = take(7)
+    normed_one, inverse_one, normed_two, inverse_two, hidden_two, act, slope, planes, texels = take(9)
+    bufs = take(count)
+    after, index_send, index_recv, hidden_send, hidden_recv, slots, small_send, small_recv, out_sem = take(9)
+    bfloat, f32 = jnp.bfloat16, jnp.float32
+    place = Place(n, seq_size)
+    for matrix, shard, buf in zip(matrices, shards, bufs):
+        if matrix.by_rows:
+            buf[place.i + (place.seq,)] = shard[...].astype(bfloat)
+        else:
+            at = pl.ds(pl.multiple_of(place.seq * matrix.cols, 128), matrix.cols)
+            buf[place.i + (slice(None), at)] = shard[...].astype(bfloat)
+    index_out[place.seq] = index[...]
+    place.enter()
+    gather = Gather(place, matrices, bufs, refs)
+    total = len(gather.chunks)
+    outs = []
+    state = [0]
+
+    def advance():
+        t = state[0]
+        state[0] += 1
+        if t < total:
+            gather.hop(t, 0)
+            if t + AHEAD < total:
+                gather.along_seq(t + AHEAD)
+        if 0 <= t - LAG < total:
+            gather.hop(t - LAG, 1)
+        if 0 <= t - 2 * LAG < total:
+            gather.third(t - 2 * LAG)
+        k = t - 3 * LAG
+        if 0 <= k < total:
+            gather.arrived(k)
+            w, matrix, part = gather.chunks[k]
+            at = (slice(None),) * 3 + matrix.tail(part, 0, seq_size)
+            copy = pltpu.make_async_copy(bufs[w].at[at], wholes[w].at[at], out_sem.at[k])
+            copy.start()
+            outs.append(copy)
+
+    def advance_to(weight):
+        last = max(k for k, (w, _, _) in enumerate(gather.chunks) if w == weight)
+        while state[0] <= last + 3 * LAG:
+            advance()
+
+    def spread(ref, send, recv):
+        copies = []
+        for step in range(1, seq_size):
+            copy = remote(ref, ref, send.at[step - 1], recv.at[step - 1], place.peer(3, step)[1])
+            copy.start()
+            copies.append(copy)
+        return copies
+
+    for k in range(AHEAD):
+        gather.along_seq(k)
+    later = spread(index_out.at[place.seq], index_send, index_recv)
+    normed, inverse = normalize(tokens[...])
+    normed_one[...] = normed
+    inverse_one[...] = inverse
+    gain_sum = small_sum(place, gains[...], slots, small_send, small_recv, advance)
+    gains_out[...] = gain_sum.astype(bfloat).astype(f32)
+    hidden_all[place.seq] = (normed_one[...] * gains_out[0:1] + gains_out[1:2]).astype(bfloat)
+    hidden_copies = spread(hidden_all.at[place.seq], hidden_send, hidden_recv)
+    w_qkv, w_out, w_up, w_down, w_unpatch = bufs
+    width = tokens.shape[1]
+    tile = 512
+    advance_to(0)
+    for at in range(0, width, tile):
+        query[:, at : at + tile] = matmul(hidden_all[place.seq], columns(w_qkv, at, tile)).astype(bfloat)
+    for copy in hidden_copies:
+        copy.wait_recv()
+    hidden = hidden_all[...].reshape(-1, width)
+
+    @pl.loop(0, width // tile)
+    def _(t):
+        at = pl.multiple_of(t * tile, tile)
+        keys[:, pl.ds(at, tile)] = matmul(hidden, columns(w_qkv, at + width, tile)).astype(bfloat)
+        values[:, pl.ds(at, tile)] = matmul(hidden, columns(w_qkv, at + 2 * width, tile)).astype(bfloat)
+
+    advance()
+    pair = 2 * width // HEADS
+    scale = (width // HEADS) ** (-0.5)
+    rows = tokens.shape[0]
+    first = lax.broadcasted_iota(jnp.int32, (rows, pair), 1) < pair // 2
+    pairs, segments = HEADS // 2, 4
+    for segment in range(segments):
+
+        @pl.loop(segment * pairs // segments, (segment + 1) * pairs // segments)
+        def _(p):
+            at = pl.ds(pl.multiple_of(p * pair, pair), pair)
+            query_two, key_two, value_two = query[:, at].astype(f32) * scale, keys[:, at], values[:, at]
+            made = []
+            for mine in (first, ~first):
+                scores = matmul_nt(jnp.where(mine, query_two, 0.0).astype(bfloat), key_two)
+                scores = jnp.where(valid[...] > 0.0, scores, NEGATIVE)
+                expo = jnp.exp(scores - jnp.max(scores, axis=-1, keepdims=True))
+                probs = expo * (1.0 / jnp.sum(expo, axis=-1, keepdims=True))
+                made.append(matmul(probs.astype(bfloat), value_two))
+            mixed[:, at] = jnp.where(first, made[0], made[1]).astype(bfloat)
+
+        advance()
+    advance_to(1)
+    for at in range(0, width, tile):
+        after[:, at : at + tile] = tokens[:, at : at + tile] + matmul(mixed[...], columns(w_out, at, tile))
+    normed, inverse = normalize(after[...])
+    normed_two[...] = normed
+    inverse_two[...] = inverse
+    hidden_two[...] = (normed * gains_out[2:3] + gains_out[3:4]).astype(bfloat)
+    advance_to(2)
+
+    @pl.loop(0, act.shape[1] // tile)
+    def _(t):
+        at = pl.multiple_of(t * tile, tile)
+        value, rate = gelu_parts(matmul(hidden_two[...], columns(w_up, at, tile)))
+        act[:, pl.ds(at, tile)] = value.astype(bfloat)
+        slope[:, pl.ds(at, tile)] = rate.astype(bfloat)
+
+    advance_to(3)
+    deep = act.shape[1] // n
+    for i in range(n):
+        block = w_down[i].reshape(deep, width)
+        for at in range(0, width, tile):
+            after[:, at : at + tile] += matmul(act[:, i * deep : (i + 1) * deep], block[:, at : at + tile])
+    planes[...] = after[: planes.shape[0]].astype(bfloat)
+    advance_to(4)
+    while state[0] < total + 3 * LAG:
+        advance()
+    for at in range(0, texels.shape[1], tile):
+        texels[:, at : at + tile] = matmul(planes[...], columns(w_unpatch, at, tile)).astype(bfloat)
+    gather.finish()
+    for copy in later:
+        copy.wait()
+    for copy in hidden_copies:
+        copy.wait_send()
+    for copy in outs:
+        copy.wait()
+
+
+def forward_layer(n, seq_size, matrices, shards, tokens, gains, index, valid):
+    chunks = sum(m.parts for m in matrices)
+    vmem, any_space = pl.BlockSpec(memory_space=pltpu.VMEM), pl.BlockSpec(memory_space=pl.ANY)
+    shapes = [m.shape(n, seq_size) for m in matrices]
+    largest = max(n, seq_size)
+    bfloat, f32 = jnp.bfloat16, jnp.float32
+    rows, width = tokens.shape
+    plane_rows = 3 * PRES * PRES // seq_size
+    ff = matrices[2].cols * seq_size
+    results = [
+        ((8, width), f32),
+        ((seq_size,) + index.shape, jnp.int32),
+        ((seq_size, rows, width), bfloat),
+        ((rows, width), bfloat),
+        ((seq_size * rows, width), bfloat),
+        ((seq_size * rows, width), bfloat),
+        ((rows, width), bfloat),
+        ((rows, width), f32),
+        ((rows, 1), f32),
+        ((rows, width), f32),
+        ((rows, 1), f32),
+        ((rows, width), bfloat),
+        ((rows, ff), bfloat),
+        ((rows, ff), bfloat),
+        ((plane_rows, width), bfloat),
+        ((plane_rows, matrices[4].cols * seq_size), bfloat),
+    ]
+    sem = pltpu.SemaphoreType.DMA
+    made = pl.pallas_call(
+        functools.partial(forward_kernel, n, seq_size, matrices),
+        out_shape=[jax.ShapeDtypeStruct(s, bfloat) for s in shapes]
+        + [jax.ShapeDtypeStruct(s, t) for s, t in results],
+        in_specs=[vmem] * (len(matrices) + 4),
+        out_specs=[any_space] * len(matrices) + [vmem] * len(results),
+        scratch_shapes=[pltpu.VMEM(s, bfloat) for s in shapes]
+        + [pltpu.VMEM((rows, width), f32)]
+        + [sem((seq_size - 1,))] * 4
+        + [pltpu.VMEM((4, largest) + gains.shape, f32)]
+        + [sem((4, largest - 1))] * 2
+        + [sem((chunks,))]
+        + gather_sems(n, seq_size, chunks),
+        compiler_params=pltpu.CompilerParams(
+            collective_id=0, has_side_effects=True, vmem_limit_bytes=VMEM_LIMIT
+        ),
+    )(*shards, tokens, gains, index, valid)
+    return made[: len(matrices)], made[len(matrices) :]
+
+
 def weight_list(shards):
     names = ("qkv", "out", "up", "down", "unpatch")
     parts = (4, 1, 4, 4, 2)
@@ -451,30 +824,6 @@
 def matmul_nt(left, right):
     return lax.dot_general(
         left, right, (((1,), (1,)), ((), ())), preferred_element_type=jnp.float32
-    )
-
-
-def exact(left, right):
-    return jnp.dot(left, right, precision=lax.Precision.HIGHEST, preferred_element_type=jnp.float32)
-
-
-def exact_tn(left, right):
-    return lax.dot_general(
-        left,
-        right,
-        (((0,), (0,)), ((), ())),
-        precision=lax.Precision.HIGHEST,
-        preferred_element_type=jnp.float32,
-    )
-
-
-def exact_nt(left, right):
-    return lax.dot_general(
-        left,
-        right,
-        (((1,), (1,)), ((), ())),
-        precision=lax.Precision.HIGHEST,
-        preferred_element_type=jnp.float32,
     )
 
 
@@ -541,94 +890,29 @@
     gains = jnp.stack([ln1_gain, ln1_bias, ln2_gain, ln2_bias])
     spread = jnp.zeros((8, width), jnp.float32)
     spread = lax.dynamic_update_slice(spread, gains, (0, device * gains.shape[1]))
-    *wholes, gains_all = gather_weights(n, seq_size, matrices, shards_of, spread)
-    qkv_weight, out_weight, up_weight, down_weight, unpatch_weight = [
-        w.reshape(-1, w.shape[-1]) for w in wholes
-    ]
-    gain_one, shift_one, gain_two, shift_two = [
-        lax.reduce_precision(gains_all[i], 8, 7) for i in range(4)
-    ]
-    norm_one, normed_one, inverse_one = norm_forward(rows_in, gain_one, shift_one)
-    hidden_one = norm_one.astype(bfloat)
-    qkv = matmul(hidden_one, qkv_weight).astype(bfloat)
-    keys_all, values_all = (
-        lax.all_gather(qkv[:, width : 2 * width], "seq", axis=0, tiled=True),
-        lax.all_gather(qkv[:, 2 * width :], "seq", axis=0, tiled=True),
-    )
     position = jnp.arange(seq_size * tok_dev, dtype=jnp.int32)
     owner = position // tok_dev
     offset = position % tok_dev
     key_valid = (offset < plane_dev) | (
         owner * (tok_dev - plane_dev) + offset - plane_dev < counts[0]
     )
-    query_heads = split_heads(qkv[:, :width], HEADS)
+    wholes, made = forward_layer(
+        n, seq_size, matrices, shards_of, rows_in, spread, sample_texels[0], key_valid.astype(jnp.float32)[None]
+    )
+    gains_all, index_all, hidden_all, query, keys_all, values_all, mixed = made[:7]
+    normed_one, inverse_one, normed_two, inverse_two, hidden_two, activated, slope, plane_rows, own_texels = made[7:]
+    qkv_weight, out_weight, up_weight, down_weight, unpatch_weight = [
+        w.reshape(-1, w.shape[-1]) for w in wholes
+    ]
+    gain_one, gain_two = gains_all[0], gains_all[2]
+    hidden_one = lax.dynamic_index_in_dim(hidden_all, lax.axis_index("seq"), 0, keepdims=False)
+    density, color_value, own_grad_texels, grad_w_one, grad_b_one, grad_w_two, grad_b_two = decode(
+        n, seq_size, own_texels, index_all, dec_w1, dec_b1, dec_w2, dec_b2, d_density, d_color[0]
+    )
+    grad_b_one, grad_w_two, grad_b_two = grad_b_one[:, 0], grad_w_two[:4].T, grad_b_two[:4, 0]
+    query_heads = split_heads(query, HEADS)
     key_heads = split_heads(keys_all, HEADS)
     value_heads = split_heads(values_all, HEADS)
-
-    def head_forward(parts):
-        query_h, key_h, value_h = parts
-        scores = jnp.where(key_valid[None, :], matmul_nt(query_h, key_h) * scale, NEGATIVE)
-        peak = jnp.max(scores, axis=-1, keepdims=True)
-        expo = jnp.exp(scores - peak)
-        total = jnp.sum(expo, axis=-1, keepdims=True)
-        probs = (expo / total).astype(bfloat)
-        return (matmul(probs, value_h), peak[:, 0] + jnp.log(total[:, 0]))
-
-    head_out, log_norm = lax.map(head_forward, (query_heads, key_heads, value_heads))
-    mixed = join_heads(head_out).astype(bfloat)
-    after_attn = rows_in + matmul(mixed, out_weight)
-    norm_two, normed_two, inverse_two = norm_forward(after_attn, gain_two, shift_two)
-    hidden_two = norm_two.astype(bfloat)
-    pre_act = matmul(hidden_two, up_weight)
-    act_value, act_pull = jax.vjp(gelu_exact, pre_act)
-    activated = act_value.astype(bfloat)
-    layer_out = after_attn + matmul(activated, down_weight)
-    plane_rows = layer_out[:plane_dev].astype(bfloat)
-    own_texels = matmul(plane_rows, unpatch_weight).astype(bfloat)
-    texels = lax.all_gather(own_texels, "seq", axis=0, tiled=True)
-    table = texels.reshape(-1, CH)
-    texel = sample_texels[0]
-    samples = texel.shape[1]
-    side = PRES * PATCH
-    row_pos = texel // side
-    col_pos = texel % side
-    token = row_pos // PATCH * PRES + col_pos // PATCH
-    sub_pos = row_pos % PATCH * PATCH + col_pos % PATCH
-    plane = jnp.arange(3, dtype=jnp.int32)[:, None]
-    grid_row = token // quarter * plane_dev + plane * quarter + token % quarter
-    flat_rows = (grid_row * (PATCH * PATCH) + sub_pos).reshape(-1)
-    picked = jnp.take(table, flat_rows, axis=0).astype(jnp.float32)
-    features = picked.reshape(3, samples, CH).transpose(1, 0, 2).reshape(samples, 3 * CH)
-    dec_pre = exact(features, dec_w1) + dec_b1
-    dec_hidden, dec_pull = jax.vjp(gelu_exact, dec_pre)
-    dec_out = exact(dec_hidden, dec_w2) + dec_b2
-    density = jax.nn.softplus(dec_out[:, 0])
-    color_value = jax.nn.sigmoid(dec_out[:, 1:])
-    grad_dec_out = jnp.concatenate(
-        [
-            (d_density[0] * jax.nn.sigmoid(dec_out[:, 0]))[:, None],
-            d_color[0].T * color_value * (1.0 - color_value),
-        ],
-        axis=1,
-    )
-    grad_w_two = exact_tn(dec_hidden, grad_dec_out)
-    grad_b_two = jnp.sum(grad_dec_out, axis=0)
-    grad_dec_pre = dec_pull(exact_nt(grad_dec_out, dec_w2))[0]
-    grad_w_one = exact_tn(features, grad_dec_pre)
-    grad_b_one = jnp.sum(grad_dec_pre, axis=0)
-    grad_features = exact_nt(grad_dec_pre, dec_w1)
-    spread_grads = grad_features.reshape(samples, 3, CH).transpose(1, 0, 2).reshape(-1, CH)
-    grad_table = jnp.zeros(table.shape, jnp.float32).at[flat_rows].add(spread_grads)
-    own_grad_texels = (
-        lax.psum_scatter(
-            grad_table.reshape(texels.shape).astype(jnp.bfloat16),
-            "seq",
-            scatter_dimension=0,
-            tiled=True,
-        )
-        .astype(jnp.float32)
-        .astype(bfloat)
-    )
     grad_planes = matmul_nt(own_grad_texels, unpatch_weight)
     grad_unpatch = matmul_tn(plane_rows, own_grad_texels)
     grad_layer = jnp.concatenate(
@@ -636,7 +920,7 @@
     )
     grad_layer_low = grad_layer.astype(bfloat)
     grad_down = matmul_tn(activated, grad_layer_low)
-    grad_pre = act_pull(matmul_nt(grad_layer_low, down_weight))[0].astype(bfloat)
+    grad_pre = (matmul_nt(grad_layer_low, down_weight) * slope.astype(jnp.float32)).astype(bfloat)
     grad_up = matmul_tn(hidden_two, grad_pre)
     grad_norm_two, grad_gain_two, grad_shift_two = norm_backward(
         matmul_nt(grad_pre, up_weight), normed_two, inverse_two, gain_two
@@ -648,9 +932,9 @@
     grad_heads = split_heads(grad_mixed, HEADS)
 
     def head_backward(parts):
-        query_h, key_h, value_h, norm_h, grad_h = parts
-        scores = matmul_nt(query_h, key_h) * scale
-        probs = jnp.where(key_valid[None, :], jnp.exp(scores - norm_h[:, None]), 0.0)
+        query_h, key_h, value_h, grad_h = parts
+        scores = jnp.where(key_valid[None, :], matmul_nt(query_h, key_h) * scale, NEGATIVE)
+        probs = jax.nn.softmax(scores, axis=-1)
         grad_value = matmul_tn(probs.astype(bfloat), grad_h)
         grad_probs = matmul_nt(grad_h, value_h)
         grad_scores = (
@@ -661,7 +945,7 @@
         return (grad_query, grad_key, grad_value)
 
     grad_query, grad_key, grad_value = lax.map(
-        head_backward, (query_heads, key_heads, value_heads, log_norm, grad_heads)
+        head_backward, (query_heads, key_heads, value_heads, grad_heads)
     )
     own_key_grad, own_value_grad = (
         lax.psum_scatter(
@@ -701,8 +985,8 @@
     ]
     decoder_sums = sums[4:]
     return (
-        density[None],
-        color_value.T[None],
+        density,
+        color_value[None],
         grad_tokens[None],
         sum_gain_one,
         sum_shift_one,

time: 1010 us -> 731 us (0.72)
  waiting for transfers between devices: 247 us -> 56.9 us
  Pallas kernels: 297 us -> 394 us
  matrix products: 236 us -> 170 us
  other arithmetic: 94.2 us -> 28.7 us
  local copies, waits for them, and re-layouts: 113 us -> 53.8 us
    all_gather x3 -> x0, waiting for transfers between devices: 136 us -> none  [the longest x1 61.3 us: shards(): texels = lax.all_gather(own_texels, 'seq', axis=0, tiled=True)]
    pallas_call x1 -> x2, Pallas kernels: 148 us -> 245 us  [the longest x1 188 us: forward_layer(): pl.pallas_call(functools.partial(forward_kernel, n, seq_size, matrices),...]
    reduce_scatter x1 -> x0, waiting for transfers between devices: 59 us -> none  [shards(): lax.psum_scatter(grad_table.reshape(texels.shape).astype(jnp.bfloat16), '...]
    scatter-add x1 -> x0, other arithmetic: 43.5 us -> none  [shards(): jnp.zeros(table.shape, jnp.float32).at[flat_rows].add(spread_grads)]
    dot_general x37 -> x16, matrix products: 66.7 us -> 28.4 us  [matmul(): return jnp.dot(left, right, preferred_element_type=jnp.float32)]
    gather x2 -> x0, local copies, waits for them, and re-layouts: 24 us -> none  [shards(): picked = jnp.take(table, flat_rows, axis=0).astype(jnp.float32)]
    dot_general x53 -> x37, matrix products: 87.2 us -> 64.1 us  [matmul_nt(): lax.dot_general(left, right, (((1,), (1,)), ((), ())), preferred_element_...]
    reshape x3 -> x0, local copies, waits for them, and re-layouts: 18.2 us -> none  [the longest x1 15.4 us: shards(): table = texels.reshape(-1, CH)]
  transfers between devices with their start and end apart: 6 -> 2, of which waited for: 6 -> 2; matrix products, arithmetic and copies ran while one was open for 4% -> 4% of each run, Pallas kernels for 0% -> 0%
where the time goes in v2:
time: 731 us; the launch traced here: 719 us
  Pallas kernels  394 us (54%)
  matrix products  170 us (23%)
  waiting for transfers between devices  56.9 us (8%)
  local copies, waits for them, and re-layouts  53.8 us (7%)
  other arithmetic  28.7 us (4%)
  between operations  15.5 us (2%)
    pallas_call x1, Pallas kernels, forward_layer(): pl.pallas_call(functools.partial(forward_kernel, n, seq_size, matrices),...  188 us
    pallas_call x1, Pallas kernels, scatter_grads(): pl.pallas_call(functools.partial(scatter_kernel, n, seq_size, matrices),...  149 us
    dot_general x37, matrix products, matmul_tn(): lax.dot_general(left, right, (((0,), (0,)), ((), ())), preferred_element_...  77.5 us
    dot_general x37, matrix products, matmul_nt(): lax.dot_general(left, right, (((1,), (1,)), ((), ())), preferred_element_...  64.1 us
    unnamed x4, waiting for transfers between devices  56.9 us
    pallas_call x1, Pallas kernels, decode(): pl.pallas_call(kernel, out_shape=[jax.ShapeDtypeStruct((1, samples), f32)...  56.8 us
    dot_general x16, matrix products, matmul(): return jnp.dot(left, right, preferred_element_type=jnp.float32)  28.4 us
    unnamed x63, local copies, waits for them, and re-layouts  24 us
  transfers between devices with their start and end apart: 2, of which 2 were waited for; matrix products, arithmetic and copies ran while one was open for 4% of the time, Pallas kernels for 0%

profile of v2, /device:TPU:0, one launch (start us, length us, event | category | flops | bytes accessed | tf_op | source)
XLA Modules:
  0.0 718.9 jit_solution(14729755224909829682)
XLA Ops:
  18.5 188.1 %shard_map.297 = (bf16[2,2,2,128,3072]{4,3,2,1,0:T(8,128)(2,1)}, bf16[2,2,2,128,1024]{4,3,2,1,0:T(8,128)(2,1)}, bf16[2,2,2,128,4096]{4,3,2,1,0:T(8,128)(2,1)}, b...) custom-call(f32[128,768]{1,0:T(8,128)} %refs_0_.1, ...), custom_call_target="tpu_custom_call" | custom-call | tf_op jit(solution)/shard_map/pallas_call | solution.py:785
  207.5 56.8 %shard_map.298 = (f32[1,2048]{1,0:T(1,128)}, f32[3,2048]{1,0:T(4,128)}, bf16[192,2048]{1,0:T(8,128)(2,1)}, f32[96,64]{1,0:T(8,128)}, f32[64,1]{1,0:T(8,128)}, /*index=5*/f32[8,64]{1,0:T(8,128)}, f32[8,1]{1,0:T(8,128)}) custom-call(bf16[192,2048]{1,0:T(8,128)(2,1)} %get-tuple-element.99.refs_0_, s32[4,3,2048]{2,1,0:T(4,128)} %get-tuple-element.100.refs_1_, ...), custom_call_target="tpu_custom_call" | custom-call | flops 16000000000 | bytes 4000000 | tf_op jit(solution)/shard_map/pallas_call | solution.py:564
  264.3 2.8 fusion.58
  267.2 6.2 fusion.43
  273.4 4.5 multiply_reduce_fusion.1
  279.5 1.9 pad_add_fusion
  283.2 2.0 copy.67
  285.2 3.8 copy.66
  289.0 3.8 copy.68
  292.8 2.0 copy.65
  294.8 145.3 %while.15 = (s32[]{:T(128)}, bf16[16,224,64]{1,2,0:T(8,128)(2,1)}, bf16[16,896,64]{1,2,0:T(8,128)(2,1)}, bf16[16,896,64]{1,2,0:T(8,128)(2,1)}, bf16[16,224,64]{1...) while((s32[]{:T(128)}, bf16[16,224,64]{1,2,0:T(8,128)(2,1)}, ...), condition=%wide.region_6.7_spmd.clone, body=%wide.region_2.6_spmd.clone.sunk | while | flops 131949664 | bytes 7840233 | solution.py:947
  297.1 1.8 fusion.97
  302.1 1.8 fusion.95
  311.2 1.8 fusion.95
  315.3 1.8 fusion.97
  320.3 1.8 fusion.95
  324.3 1.8 fusion.97
  329.4 1.8 fusion.95
  347.5 1.8 fusion.95
  351.6 1.8 fusion.97
  356.6 1.8 fusion.95
  365.7 1.8 fusion.95
  369.7 1.8 fusion.97
  374.8 1.8 fusion.95
  383.9 1.8 fusion.95
  387.9 1.8 fusion.97
  392.9 1.8 fusion.95
  397.0 1.8 fusion.97
  402.0 1.8 fusion.95
  406.1 1.8 fusion.97
  415.2 1.8 fusion.97
  420.2 1.8 fusion.95
  429.3 1.8 fusion.95
  433.3 1.8 fusion.97
  438.3 1.8 fusion.95
  440.1 3.8 copy.77
  444.0 4.0 copy.79
  456.5 3.1 convolution_convert_fusion.4
  459.5 3.3 convolution_convert_fusion.3
  462.9 5.6 convolution_convert_fusion
  468.5 5.6 convolution_convert_fusion.1
  474.1 17.2 %reduce-scatter.7.cloned.1.call-done = bf16[224,1024]{1,0:T(8,128)(2,1)} async-done(((bf16[896,1024]{1,0:T(8,128)(2,1)}), bf16[224,1024]{1,0:T(8,128)(2,1)}) %reduce-scatter.7.cloned.1.call-update) | async-done | bytes 458768
  492.5 39.7 %reduce-scatter.9.cloned.1.call-done = bf16[224,1024]{1,0:T(8,128)(2,1)} async-done(((bf16[896,1024]{1,0:T(8,128)(2,1)}), bf16[224,1024]{1,0:T(8,128)(2,1)}) %reduce-scatter.9.cloned.1.call-update) | async-done | bytes 458768
  533.5 6.2 multiply_reduce_fusion.2
  540.4 5.7 convolution_convert_fusion.2
  546.1 148.8 %shard_map.299 = (f32[128,768]{1,0:T(8,128)}, f32[128,256]{1,0:T(8,128)}, f32[128,1024]{1,0:T(8,128)}, f32[128,1024]{1,0:T(8,128)}, f32[128,512]{1,0:T(8,128)}, /*index=5*/f32[88,128]{1,0:T(8,128)}) custom-call(bf16[2,2,2,128,3072]{4,3,2,1,0:T(8,128)(2,1)} %bitcast.159, bf16[2,2,2,128,1024]{4,3,2,1,0:T(8,128)(2,1)} %bitcast.157, ...), custom_call_target="tpu_custom_call" | custom-call | tf_op jit(solution)/shard_map/pallas_call | solution.py:348
  694.9 2.3 slice.66
  704.9 2.4 add_bitcast_fusion
  (206 shorter events, 140.8 us)
Async XLA Ops:
  7.2 484.1 %reduce-scatter.7.cloned.1.call-start = ((), (), s32[]{:S(2)}) async-start(), calls=%async_computation.2 | async-start | bytes 2293760
  17.9 0.6 copy-start.13
  207.5 56.8 %copy-start = (bf16[2,2,2,128,2048]{4,3,2,1,0:T(8,128)(2,1)S(1)}, bf16[2,2,2,128,2048]{4,3,2,1,0:T(8,128)(2,1)}, u32[]{:S(2)}) copy-start(bf16[2,2,2,128,2048]{4,3,2,1,0:T(8,128)(2,1)} %get-tuple-element.104) | copy-start | bytes 12582916
  264.3 2.8 copy-start.4
  264.3 9.1 %slice-start = ((s8[8388608]{0:T(1024)(128)(4,1)}), s8[4194304]{0:T(1024)(128)(4,1)S(1)}, s32[]{:S(2)}) async-start(s8[8388608]{0:T(1024)(128)(4,1)} %bitcast.182), calls=%async_computation.4 | async-start | bytes 8388608
  267.2 6.2 copy-start.6
  267.2 6.2 slice-start.1
  279.5 2.2 copy-start.3
  444.0 88.2 %reduce-scatter.9.cloned.1.call-start = ((), (), s32[]{:S(2)}) async-start(), calls=%async_computation.3 | async-start | bytes 2293760
  448.0 0.7 copy-start.20
  455.1 4.5 copy-start.2
  455.1 4.5 copy-start.7
  459.5 3.3 copy-start.1
  462.9 5.6 copy-start.8
  474.1 59.3 %copy-start.5 = (f32[224,1024]{1,0:T(8,128)S(1)}, f32[224,1024]{1,0:T(8,128)}, u32[]{:S(2)}) copy-start(f32[224,1024]{1,0:T(8,128)} %get-tuple-element.119) | copy-start | bytes 2752516
  533.4 6.2 copy-start.15
  533.4 6.2 copy-start.17
  533.5 6.2 copy-start.18
  533.5 6.2 copy-start.19
  704.9 2.5 copy-start.16
  704.9 3.1 copy-start.11
  704.9 3.8 copy-start.14
  704.9 4.5 copy-start.10
  707.3 2.8 copy-start.9
  707.3 3.6 copy-start.12
Sparse Core Ops, SparseCore 0:
  444.1 47.1 reduce-scatter.6
  493.6 38.5 reduce-scatter.8

commit v3 on v2

--- a/solution.py
+++ b/solution.py
@@ -16,7 +16,7 @@
 
 EPSILON = 1e-05
 NEGATIVE = -1e30
-VMEM_LIMIT = 56 * 2**20
+VMEM_LIMIT = 58 * 2**20
 AHEAD = 3
 LAG = 2
 
@@ -187,197 +187,6 @@
     return [sem((chunks, seq_size - 1))] * 2 + [sem((chunks, 4, n - 1))] * 2 + [sem((chunks, n - 1))] * 2
 
 
-class Scatter:
-    def __init__(self, place, matrices, wholes, refs, far, hops, near, outs, sems):
-        self.place, self.wholes, self.refs = place, wholes, refs
-        self.far, self.hops, self.near, self.outs = far, hops, near, outs
-        self.chunks = [(w, m, p) for w, m in enumerate(matrices) for p in range(m.parts)]
-        self.seq_send, self.seq_recv, self.hop_send, self.hop_recv, self.far_send, self.far_recv = sems
-        self.copies = {}
-
-    def _send(self, key, axis, region_to, slot, send, recv):
-        made = []
-        for step in range(1, self.place.size(axis)):
-            to, device = self.place.peer(axis, step)
-            copy = remote(region_to(to), slot(step - 1), send.at[step - 1], recv.at[step - 1], device)
-            copy.start()
-            made.append(copy)
-        self.copies[key] = made
-
-    def _take(self, key):
-        for copy in self.copies[key]:
-            copy.wait_recv()
-
-    def _index(self, k, index, first, count):
-        w, matrix, part = self.chunks[k]
-        return index + matrix.tail(part, first, count)
-
-    def third(self, k):
-        w, matrix, part = self.chunks[k]
-        p, every = self.place, slice(None)
-        tail = matrix.tail(part, 0, p.seq_size)
-        self._send(
-            (k, 3),
-            2,
-            lambda to: self.wholes[w].at[(every, every, to) + tail],
-            lambda s: self.far[w].at[(s, every, every) + tail],
-            self.far_send.at[k],
-            self.far_recv.at[k],
-        )
-
-    def hop(self, k, number):
-        w, matrix, part = self.chunks[k]
-        p, half, n = self.place, self.place.seq_size // 2, self.place.n
-        ref = self.refs[w]
-        if number == 0:
-            self._take((k, 3))
-            tail = matrix.tail(part, 0, p.seq_size)
-
-            @pl.loop(0, n * n)
-            def _(at):
-                a, b = lax.div(at, n), lax.rem(at, n)
-                value = ref[(a, b) + tail].astype(jnp.float32)
-                for s in range(n - 1):
-                    value = value + self.far[w][(s, a, b) + tail].astype(jnp.float32)
-                ref[(a, b) + tail] = value.astype(jnp.bfloat16)
-
-        else:
-            for h in (0, 1):
-                self._take((k, 1, h))
-                tail, local = matrix.tail(part, h * half, half), matrix.tail(part, 0, half)
-                for a in range(n):
-                    index = (p.i[0], a) if h == 0 else (a, p.i[1])
-                    value = ref[index + tail].astype(jnp.float32)
-                    for s in range(n - 1):
-                        value = value + self.hops[w][(h, s, a) + local].astype(jnp.float32)
-                    ref[index + tail] = value.astype(jnp.bfloat16)
-        for h in (0, 1):
-            axis = h if number == 0 else 1 - h
-            tail, local = matrix.tail(part, h * half, half), matrix.tail(part, 0, half)
-            other = slice(None) if number == 0 else p.i[1 - axis]
-            at = 2 * number + h
-
-            def region_to(to, axis=axis, other=other, tail=tail):
-                index = (to, other) if axis == 0 else (other, to)
-                return ref.at[index + tail]
-
-            def slot(s, h=h, local=local):
-                return self.hops[w].at[(h, s, pl.ds(0, n) if number == 0 else n) + local]
-
-            self._send((k, 1 + number, h), axis, region_to, slot, self.hop_send.at[k, at], self.hop_recv.at[k, at])
-
-    def along_seq(self, k):
-        w, matrix, part = self.chunks[k]
-        p, half, n = self.place, self.place.seq_size // 2, self.place.n
-        ref = self.refs[w]
-        for h in (0, 1):
-            self._take((k, 2, h))
-            tail, local = matrix.tail(part, h * half, half), matrix.tail(part, 0, half)
-            value = ref[p.i[:2] + tail].astype(jnp.float32)
-            for s in range(n - 1):
-                value = value + self.hops[w][(h, s, n) + local].astype(jnp.float32)
-            ref[p.i[:2] + tail] = value.astype(jnp.bfloat16)
-        size = matrix.rows // matrix.parts
-        self._send(
-            (k, 0),
-            3,
-            lambda to: ref.at[p.i[:2] + matrix.tail(part, to, 1)],
-            lambda s: self.near[w].at[(s,) + matrix.tail(part, 0, 1)],
-            self.seq_send.at[k],
-            self.seq_recv.at[k],
-        )
-
-    def arrived(self, k):
-        w, matrix, part = self.chunks[k]
-        p = self.place
-        self._take((k, 0))
-        value = self.refs[w][p.i[:2] + matrix.tail(part, p.seq, 1)].astype(jnp.float32)
-        for s in range(p.seq_size - 1):
-            value = value + self.near[w][(s,) + matrix.tail(part, 0, 1)].astype(jnp.float32)
-        size = matrix.rows // matrix.parts
-        self.outs[w][pl.ds(part * size, size)] = value.reshape(size, matrix.cols)
-
-    def finish(self):
-        for made in self.copies.values():
-            for copy in made:
-                copy.wait_send()
-
-
-def scatter_kernel(n, seq_size, matrices, *refs):
-    count = len(matrices)
-    grads, small, outs, small_out = refs[:count], refs[count], refs[count + 1 : 2 * count + 1], refs[2 * count + 1]
-    rest = refs[2 * count + 2 :]
-    bufs, far, hops, near = [rest[i * count : (i + 1) * count] for i in range(4)]
-    slots, small_send, small_recv, in_sem = rest[4 * count : 4 * count + 4]
-    sems = rest[4 * count + 4 :]
-    place = Place(n, seq_size)
-    scatter = Scatter(place, matrices, grads, bufs, far, hops, near, outs, sems)
-    total = len(scatter.chunks)
-    loads = []
-    for k, (w, matrix, part) in enumerate(scatter.chunks):
-        tail, every = matrix.tail(part, 0, seq_size), (slice(None),) * 2
-        copy = pltpu.make_async_copy(
-            grads[w].at[every + (place.i[2],) + tail], bufs[w].at[every + tail], in_sem.at[k]
-        )
-        copy.start()
-        loads.append(copy)
-    place.enter()
-    for t in range(total + 8):
-        if t < total:
-            scatter.third(t)
-        if 0 <= t - 2 < total:
-            loads[t - 2].wait()
-            scatter.hop(t - 2, 0)
-        if 0 <= t - 4 < total:
-            scatter.hop(t - 4, 1)
-        if 0 <= t - 6 < total:
-            scatter.along_seq(t - 6)
-        if 0 <= t - 8 < total:
-            scatter.arrived(t - 8)
-        if t == 8:
-            small_out[...] = small_sum(place, small[...], slots, small_send, small_recv)
-    scatter.finish()
-
-
-def scatter_grads(n, seq_size, matrices, grads, small):
-    chunks = sum(m.parts for m in matrices)
-    vmem, any_space = pl.BlockSpec(memory_space=pltpu.VMEM), pl.BlockSpec(memory_space=pl.ANY)
-    shapes = [m.shape(n, seq_size) for m in matrices]
-    largest = max(n, seq_size)
-    bfloat = jnp.bfloat16
-    return pl.pallas_call(
-        functools.partial(scatter_kernel, n, seq_size, matrices),
-        out_shape=[jax.ShapeDtypeStruct((m.rows, m.cols), jnp.float32) for m in matrices]
-        + [jax.ShapeDtypeStruct(small.shape, jnp.float32)],
-        in_specs=[any_space] * len(matrices) + [vmem],
-        out_specs=[vmem] * (len(matrices) + 1),
-        scratch_shapes=[pltpu.VMEM((n, n) + s[3:], bfloat) for s in shapes]
-        + [pltpu.VMEM((n - 1, n, n) + s[3:], bfloat) for s in shapes]
-        + [
-            pltpu.VMEM(
-                (2, n - 1, n + 1)
-                + ((seq_size // 2, m.rows, m.cols) if m.by_rows else (m.rows, seq_size // 2 * m.cols)),
-                bfloat,
-            )
-            for m in matrices
-        ]
-        + [
-            pltpu.VMEM((seq_size - 1,) + ((1, m.rows, m.cols) if m.by_rows else (m.rows, m.cols)), bfloat)
-            for m in matrices
-        ]
-        + [
-            pltpu.VMEM((4, largest) + small.shape, jnp.float32),
-            pltpu.SemaphoreType.DMA((4, largest - 1)),
-            pltpu.SemaphoreType.DMA((4, largest - 1)),
-            pltpu.SemaphoreType.DMA((chunks,)),
-        ]
-        + gather_sems(n, seq_size, chunks),
-        compiler_params=pltpu.CompilerParams(
-            collective_id=1, has_side_effects=True, vmem_limit_bytes=VMEM_LIMIT
-        ),
-    )(*grads, small)
-
-
 def gelu_parts(x):
     cdf = 0.5 + 0.5 * lax.erf(x * (0.5**0.5))
     return x * cdf, cdf + x * (jnp.exp(-0.5 * x * x) * (2.0 * math.pi) ** -0.5)
@@ -399,9 +208,9 @@
     return key, a % 2 * PATCH + b, fold
 
 
-def decode_kernel(
-    n,
-    seq_size,
+def decode_both(
+    place,
+    grad_texels,
     tile,
     texels,
     index,
@@ -413,7 +222,6 @@
     d_color,
     density,
     color,
-    grad_texels,
     g_w1,
     g_b1,
     g_w2,
@@ -425,10 +233,12 @@
     part_in,
     own_part,
     grad_all,
-    sems,
+    send_sem,
+    recv_sem,
+    back_send,
+    back_recv,
 ):
-    send_sem, recv_sem, back_send, back_recv = sems
-    place = Place(n, seq_size)
+    seq_size = place.seq_size
     bfloat, f32 = jnp.bfloat16, jnp.float32
     samples = index.shape[2]
     quarter = PRES * PRES // seq_size
@@ -437,7 +247,6 @@
     cols = groups * CH
     depth = width // cols * quarter
     hidden = w1.shape[1]
-    place.enter((3,))
     for p in range(3):
         own = texels[p * quarter : (p + 1) * quarter].astype(f32)
         stacked = jnp.concatenate([own[:, i * cols : (i + 1) * cols] for i in range(width // cols)], axis=0)
@@ -539,42 +348,218 @@
     for p in range(3):
         back = grad_tables[p].T
         for i in range(width // cols):
-            grad_texels[p * quarter : (p + 1) * quarter, i * cols : (i + 1) * cols] = back[
-                i * quarter : (i + 1) * quarter
-            ].astype(bfloat)
+            block = back[i * quarter : (i + 1) * quarter].astype(bfloat)
+            grad_texels[p * quarter : (p + 1) * quarter, i * cols : (i + 1) * cols] = block
     for copy in copies + backs:
         copy.wait_send()
 
 
-def decode(n, seq_size, texels, index, dec_w1, dec_b1, dec_w2, dec_b2, d_density, d_color):
+def core_columns(ref, n, segment, to):
+    width = ref.shape[1]
+    parts = width // (n * segment)
+    if segment % 128 == 0:
+        places = [pl.multiple_of((q * n + to) * segment, 128) for q in range(parts)]
+        return jnp.concatenate([ref[:, pl.ds(at, segment)] for at in places], axis=1).T
+    place = lax.broadcasted_iota(jnp.int32, (width, width // n), 1)
+    source = (lax.div(place, segment) * n + to) * segment + lax.rem(place, segment)
+    pick = lax.broadcasted_iota(jnp.int32, (width, width // n), 0) == source
+    return matmul(ref[...], pick.astype(jnp.float32).astype(jnp.bfloat16)).astype(jnp.bfloat16).T
+
+
+class Exchange:
+    def __init__(self, place, send, recv):
+        self.place, self.send, self.recv = place, send, recv
+        self.made, self.used = [], 0
+
+    def _start(self, source_of, buf):
+        copies, p = [], self.place
+        for step in range(1, p.size(2)):
+            to, device = p.peer(2, step)
+            sems = (self.send.at[self.used, step - 1], self.recv.at[self.used, step - 1])
+            copy = remote(source_of(step, to), buf.at[p.i[2]], *sems, device)
+            copy.start()
+            copies.append(copy)
+        self.used += 1
+        self.made += copies
+
+        def wait():
+            for copy in copies:
+                copy.wait_recv()
+
+        return wait
+
+    def columns(self, ref, segment, split, buf):
+        p = self.place
+        for step in range(1, p.size(2)):
+            split[step - 1] = core_columns(ref, p.n, segment, p.peer(2, step)[0])
+        wait = self._start(lambda step, to: split.at[step - 1], buf)
+        buf[p.i[2]] = core_columns(ref, p.n, segment, p.i[2])
+        return wait
+
+    def rows(self, buf):
+        return self._start(lambda step, to: buf.at[self.place.i[2]], buf)
+
+    def finish(self):
+        for copy in self.made:
+            copy.wait_send()
+
+
+def weight_grad(left, right, grad, first=0, tile=512):
+    shape, width = grad.shape[:-1], right.shape[-1]
+    for at in range(0, width, tile):
+        size = min(tile, width - at)
+        block = matmul(left[0], right[0, :, at : at + size])
+        for i in range(1, left.shape[0]):
+            block = block + matmul(left[i], right[i, :, at : at + size])
+        grad[..., first + at : first + at + size] = block.astype(jnp.bfloat16).reshape(shape + (size,))
+
+
+def norm_back(grad, normed, inverse, gain):
+    scaled = grad * gain
+    inner = scaled - jnp.mean(scaled, axis=-1, keepdims=True)
+    inner = inner - normed * jnp.mean(scaled * normed, axis=-1, keepdims=True)
+    return inner * inverse
+
+
+def feed_back(place, matrices, refs):
+    (planes, act, slope, hidden_two, normed_two, inverse_two, gains, weights) = refs[:8]
+    (grads_out, grad_after, norm_grads, bufs) = refs[8:12]
+    (planes_split, planes_all, act_split, act_all, hidden_split, hidden_all) = refs[12:18]
+    (texels_all, layer_all, pre_all, layer, load_sem, out_sem, send, recv) = refs[18:26]
+    grads = [buf.at[0] for buf in bufs]
+    n = place.n
+    bfloat, f32 = jnp.bfloat16, jnp.float32
+    up, down, unpatch = matrices
+    w_up, w_down, w_unpatch = bufs
+    exchange = Exchange(place, send, recv)
+    me = place.i[2]
+    loads, waits = [], []
+
+    def start():
+        for k in (2, 1, 0):
+            copy = pltpu.make_async_copy(weights[k], bufs[k], load_sem.at[k])
+            copy.start()
+            loads.append(copy)
+
+    def start_remote():
+        waits.append(exchange.columns(planes, unpatch.rows, planes_split, planes_all))
+        waits.append(exchange.columns(act, place.seq_size * down.rows, act_split, act_all))
+        waits.append(exchange.columns(hidden_two, up.rows, hidden_split, hidden_all))
+
+    outs = []
+
+    def put(k):
+        copy = pltpu.make_async_copy(grads[k], grads_out[k], out_sem.at[k])
+        copy.start()
+        outs.append(copy)
+
+    def end():
+        got_texels = exchange.rows(texels_all)
+        loads[0].wait()
+        grad_texels = texels_all[me]
+        step = layer.shape[1] // n
+        for i in range(n):
+            block = w_unpatch[i].reshape(step, -1)
+            layer[:, i * step : (i + 1) * step] = matmul_nt(grad_texels, block)
+        layer_all[me] = layer[...].astype(bfloat)
+        got_layer = exchange.rows(layer_all)
+        loads[1].wait()
+        step = act.shape[1] // (n * n)
+        for i in range(n):
+            for j in range(n):
+                block = w_down[i, j].reshape(step, -1)
+                at = (i * n + j) * step
+                value = matmul_nt(layer_all[me], block) * slope[:, at : at + step].astype(f32)
+                pre_all[me, :, at : at + step] = value.astype(bfloat)
+        got_pre = exchange.rows(pre_all)
+        waits[0]()
+        got_texels()
+        weight_grad(planes_all, texels_all, grads[2])
+        put(2)
+        loads[2].wait()
+        step = layer.shape[1] // n
+        pieces = []
+        for i in range(n):
+            block = w_up[i].reshape(step, -1)
+            pieces.append(matmul_nt(pre_all[me], block))
+        grad = jnp.concatenate(pieces, axis=1)
+        normed = normed_two[...]
+        norm_grads[0:1] = jnp.sum(grad * normed, axis=0, keepdims=True)
+        norm_grads[1:2] = jnp.sum(grad, axis=0, keepdims=True)
+        grad_after[...] = layer[...] + norm_back(grad, normed, inverse_two[...], gains[2:3])
+        waits[1]()
+        got_layer()
+        weight_grad(act_all, layer_all, grads[1])
+        put(1)
+        waits[2]()
+        got_pre()
+        weight_grad(hidden_all, pre_all, grads[0])
+        put(0)
+        exchange.finish()
+        for copy in outs:
+            copy.wait()
+
+    return start, start_remote, end
+
+
+def middle_kernel(n, seq_size, matrices, *refs):
+    refs = list(refs)
+
+    def take(k):
+        taken = refs[:k]
+        del refs[:k]
+        return taken
+
+    decode_in, feed_in, weights = take(8), take(7), take(3)
+    density, color, g_w1, g_b1, g_w2, g_b2, grad_after, norm_grads = take(8)
+    grads_out, bufs, decode_scratch = take(3), take(3), take(11)
+    place = Place(n, seq_size)
+    feed = list(feed_in) + [weights, grads_out, grad_after, norm_grads, bufs] + refs
+    texels_all = refs[6]
+    start, start_remote, end = feed_back(place, matrices, feed)
+    start()
+    place.enter((2, 3))
+    start_remote()
+    tile = min(512, decode_in[1].shape[2])
+    outs = (density, color, g_w1, g_b1, g_w2, g_b2)
+    decode_both(place, texels_all.at[place.i[2]], tile, *decode_in, *outs, *decode_scratch)
+    end()
+
+
+def middle(n, seq_size, matrices, decode_in, feed_in, weights):
+    texels, index, dec_w1, dec_b1, dec_w2, dec_b2, d_density, d_color = decode_in
+    planes, act, slope, hidden_two, normed_two, inverse_two, gains = feed_in
     bfloat, f32 = jnp.bfloat16, jnp.float32
     samples, hidden = index.shape[2], dec_w1.shape[1]
-    rows = 8
-    w2 = jnp.pad(dec_w2, ((0, 0), (0, rows - dec_w2.shape[1])))
-    b2 = jnp.pad(dec_b2, (0, rows - dec_b2.shape[0]))[:, None]
+    slots = 8
+    w2 = jnp.pad(dec_w2, ((0, 0), (0, slots - dec_w2.shape[1])))
+    b2 = jnp.pad(dec_b2, (0, slots - dec_b2.shape[0]))[:, None]
     quarter = PRES * PRES // seq_size
     cols = 2 * PATCH * CH
     depth = texels.shape[1] // cols * quarter
-    vmem = pl.BlockSpec(memory_space=pltpu.VMEM)
-    sem = pltpu.SemaphoreType.DMA((seq_size - 1,))
-
-    def kernel(*refs):
-        decode_kernel(n, seq_size, min(512, samples), *refs[:-4], refs[-4:])
-
+    vmem, any_space = pl.BlockSpec(memory_space=pltpu.VMEM), pl.BlockSpec(memory_space=pl.ANY)
+    sem = pltpu.SemaphoreType.DMA
+    rows, width = normed_two.shape
+    ff, core_ff = act.shape[1], act.shape[1] // n
+    shapes = [m.shape(n, seq_size) for m in matrices]
+    halves = [(n, n) + s[3:] for s in shapes]
     return pl.pallas_call(
-        kernel,
+        functools.partial(middle_kernel, n, seq_size, matrices),
         out_shape=[
             jax.ShapeDtypeStruct((1, samples), f32),
             jax.ShapeDtypeStruct((3, samples), f32),
-            jax.ShapeDtypeStruct(texels.shape, bfloat),
             jax.ShapeDtypeStruct(dec_w1.shape, f32),
             jax.ShapeDtypeStruct((hidden, 1), f32),
-            jax.ShapeDtypeStruct((rows, hidden), f32),
-            jax.ShapeDtypeStruct((rows, 1), f32),
-        ],
-        in_specs=[vmem] * 8,
-        out_specs=[vmem] * 7,
-        scratch_shapes=[
+            jax.ShapeDtypeStruct((slots, hidden), f32),
+            jax.ShapeDtypeStruct((slots, 1), f32),
+            jax.ShapeDtypeStruct((rows, width), f32),
+            jax.ShapeDtypeStruct((2, width), f32),
+        ]
+        + [jax.ShapeDtypeStruct(s, bfloat) for s in halves],
+        in_specs=[vmem] * 15 + [any_space] * 3,
+        out_specs=[vmem] * 8 + [any_space] * 3,
+        scratch_shapes=[pltpu.VMEM(s, bfloat) for s in shapes]
+        + [
             pltpu.VMEM((3, cols, depth), bfloat),
             pltpu.VMEM((3, cols, depth), f32),
             pltpu.VMEM((seq_size, 3 * CH, samples), bfloat),
@@ -582,16 +567,328 @@
             pltpu.VMEM((seq_size - 1, hidden, samples), bfloat),
             pltpu.VMEM((hidden, samples), f32),
             pltpu.VMEM((seq_size, hidden, samples), bfloat),
-            sem,
-            sem,
-            sem,
-            sem,
-        ],
+        ]
+        + [sem((seq_size - 1,))] * 4
+        + [
+            pltpu.VMEM((n - 1, width // n, rows), bfloat),
+            pltpu.VMEM((n, width // n, rows), bfloat),
+            pltpu.VMEM((n - 1, core_ff, rows), bfloat),
+            pltpu.VMEM((n, core_ff, rows), bfloat),
+            pltpu.VMEM((n - 1, width // n, rows), bfloat),
+            pltpu.VMEM((n, width // n, rows), bfloat),
+            pltpu.VMEM((n,) + texels.shape, bfloat),
+            pltpu.VMEM((n, rows, width), bfloat),
+            pltpu.VMEM((n, rows, ff), bfloat),
+            pltpu.VMEM((rows, width), f32),
+            sem((3,)),
+            sem((3,)),
+        ]
+        + [sem((8, n - 1))] * 2,
         compiler_params=pltpu.CompilerParams(
             collective_id=2, has_side_effects=True, vmem_limit_bytes=VMEM_LIMIT
         ),
-        cost_estimate=pl.CostEstimate(flops=16 * 10**9, bytes_accessed=4 * 10**6, transcendentals=0),
-    )(texels, index, dec_w1, dec_b1[:, None], w2, b2, d_density, d_color)
+    )(texels, index, dec_w1, dec_b1[:, None], w2, b2, d_density, d_color, *feed_in, *weights)
+
+
+class Scatter:
+    def __init__(self, place, matrices, sources, kept, hops, near, outs, sems):
+        self.place, self.sources, self.kept = place, sources, kept
+        self.hops, self.near, self.outs = hops, near, outs
+        self.chunks = [(w, m, p) for w, m in enumerate(matrices) for p in range(m.parts)]
+        self.load_sem, self.seq_send, self.seq_recv, self.hop_send, self.hop_recv = sems
+        self.copies, self.loads = {}, {}
+
+    def _send(self, key, axis, region_to, slot, send, recv):
+        made = []
+        for step in range(1, self.place.size(axis)):
+            to, device = self.place.peer(axis, step)
+            copy = remote(region_to(to), slot(step - 1), send.at[step - 1], recv.at[step - 1], device)
+            copy.start()
+            made.append(copy)
+        self.copies[key] = made
+
+    def _take(self, key):
+        for copy in self.copies[key]:
+            copy.wait_recv()
+
+    def hop(self, k, number):
+        w, matrix, part = self.chunks[k]
+        p, half, n = self.place, self.place.seq_size // 2, self.place.n
+        kept, every = self.kept[w], slice(None)
+        local = matrix.tail(part, 0, half)
+        if number == 0:
+            for h in (0, 1):
+                index = (p.i[0], every) if h == 0 else (every, p.i[1])
+                source = self.sources[w].at[index + matrix.tail(part, h * half, half)]
+                copy = pltpu.make_async_copy(source, kept.at[(h, every) + local], self.load_sem.at[k, h])
+                copy.start()
+                self.loads[k, h] = copy
+        else:
+            for h in (0, 1):
+                self.loads[k, h].wait()
+                self._take((k, 1, h))
+                for a in range(n):
+                    value = kept[(h, a) + local].astype(jnp.float32)
+                    for s in range(n - 1):
+                        value = value + self.hops[w][(h, s, a) + local].astype(jnp.float32)
+                    kept[(h, a) + local] = value.astype(jnp.bfloat16)
+        for h in (0, 1):
+            axis = h if number == 0 else 1 - h
+            tail, at = matrix.tail(part, h * half, half), 2 * number + h
+
+            def region_to(to, h=h, tail=tail):
+                if number == 1:
+                    return kept.at[(h, to) + local]
+                return self.sources[w].at[((to, every) if h == 0 else (every, to)) + tail]
+
+            def slot(s, h=h):
+                return self.hops[w].at[(h, s, pl.ds(0, n) if number == 0 else n) + local]
+
+            self._send((k, 1 + number, h), axis, region_to, slot, self.hop_send.at[k, at], self.hop_recv.at[k, at])
+
+    def _block(self, matrix, part, j):
+        p, half = self.place, self.place.seq_size // 2
+        h = lax.div(j, half)
+        return (h, p.i[1] + h * (p.i[0] - p.i[1])) + matrix.tail(part, lax.rem(j, half), 1)
+
+    def along_seq(self, k):
+        w, matrix, part = self.chunks[k]
+        p, half, n = self.place, self.place.seq_size // 2, self.place.n
+        kept = self.kept[w]
+        local = matrix.tail(part, 0, half)
+        for h in (0, 1):
+            self._take((k, 2, h))
+            value = kept[(h, p.i[1 - h]) + local].astype(jnp.float32)
+            for s in range(n - 1):
+                value = value + self.hops[w][(h, s, n) + local].astype(jnp.float32)
+            kept[(h, p.i[1 - h]) + local] = value.astype(jnp.bfloat16)
+        self._send(
+            (k, 0),
+            3,
+            lambda to: kept.at[self._block(matrix, part, to)],
+            lambda s: self.near[w].at[(s,) + matrix.tail(part, 0, 1)],
+            self.seq_send.at[k],
+            self.seq_recv.at[k],
+        )
+
+    def arrived(self, k):
+        w, matrix, part = self.chunks[k]
+        p = self.place
+        self._take((k, 0))
+        value = self.kept[w][self._block(matrix, part, p.seq)].astype(jnp.float32)
+        for s in range(p.seq_size - 1):
+            value = value + self.near[w][(s,) + matrix.tail(part, 0, 1)].astype(jnp.float32)
+        size = matrix.rows // matrix.parts
+        self.outs[w][pl.ds(part * size, size)] = value.reshape(size, matrix.cols)
+
+    def finish(self):
+        for made in self.copies.values():
+            for copy in made:
+                copy.wait_send()
+
+
+def backward_kernel(n, seq_size, matrices, *refs):
+    count = len(matrices)
+    refs = list(refs)
+
+    def take(k):
+        taken = refs[:k]
+        del refs[:k]
+        return taken
+
+    grad_after, mixed, query, normed_one, inverse_one, gains, valid, small = take(8)
+    w_out_in, w_qkv_in, keys_in, values_in, hidden_all_in = take(5)
+    early = take(count - 2)
+    outs = take(count)
+    g_tokens, small_out = take(2)
+    w_out, w_qkv, work = take(3)
+    g_out, g_qkv = w_out.at[0], w_qkv.at[0]
+    kept, hops, near = take(count), take(count), take(count)
+    mixed_split, mixed_all, after_all, hidden_split, hidden_core, own_split, own_core = take(7)
+    query_all, grad_all, hidden_in = take(3)
+    grad_mixed, load_sem, core_send, core_recv, hidden_send, hidden_recv = take(6)
+    slots, small_send, small_recv = take(3)
+    sems = refs
+    bfloat, f32 = jnp.bfloat16, jnp.float32
+    place = Place(n, seq_size)
+    me = place.i[2]
+    loads = []
+    rows, width = query.shape
+    token_rows = normed_one.shape[0]
+    keys, values = grad_all.at[me, :, pl.ds(0, width)], grad_all.at[me, :, pl.ds(width, width)]
+    for k, (source, target) in enumerate(
+        ((hidden_all_in, work), (w_out_in, w_out), (keys_in, keys), (values_in, values), (w_qkv_in, w_qkv))
+    ):
+        copy = pltpu.make_async_copy(source, target, load_sem.at[k])
+        copy.start()
+        loads.append(copy)
+    place.enter()
+    scatter = Scatter(place, matrices, list(early) + [g_out, g_qkv], kept, hops, near, outs, sems)
+    total = len(scatter.chunks)
+    state = [0]
+
+    def advance():
+        t = state[0]
+        state[0] += 1
+        if t < total:
+            scatter.hop(t, 0)
+        if 0 <= t - LAG < total:
+            scatter.hop(t - LAG, 1)
+        if 0 <= t - 2 * LAG < total:
+            scatter.along_seq(t - 2 * LAG)
+        if 0 <= t - 3 * LAG < total:
+            scatter.arrived(t - 3 * LAG)
+
+    advance()
+    advance()
+    exchange = Exchange(place, core_send, core_recv)
+    out_matrix, qkv_matrix = matrices[-2:]
+    got_mixed = exchange.columns(mixed, out_matrix.rows, mixed_split, mixed_all)
+    after_all[me] = grad_after[...].astype(bfloat)
+    got_after = exchange.rows(after_all)
+    loads[0].wait()
+    own = work.at[pl.ds(pl.multiple_of(place.seq * token_rows, 16), rows)]
+    got_own = exchange.columns(own, qkv_matrix.rows, own_split, own_core)
+    got_hidden = exchange.columns(work, qkv_matrix.rows, hidden_split, hidden_core)
+    loads[1].wait()
+    step = width // n
+    for i in range(n):
+        block = w_out[i].reshape(step, width)
+        grad_mixed[:, i * step : (i + 1) * step] = matmul_nt(after_all[me], block).astype(bfloat)
+    got_mixed()
+    got_after()
+    weight_grad(mixed_all, after_all, g_out)
+    loads[2].wait()
+    loads[3].wait()
+    pair = 2 * width // HEADS
+    scale = (width // HEADS) ** (-0.5)
+    first = lax.broadcasted_iota(jnp.int32, (rows, pair), 1) < pair // 2
+    pairs, segments = HEADS // 2, 4
+    for segment in range(segments):
+
+        @pl.loop(segment * pairs // segments, (segment + 1) * pairs // segments)
+        def _(p):
+            at = pl.ds(pl.multiple_of(p * pair, pair), pair)
+            query_two, grad_two = query[:, at].astype(f32) * scale, grad_mixed[:, at].astype(f32)
+            later = pl.ds(pl.multiple_of(width + p * pair, pair), pair)
+            key_two, value_two = grad_all[me, :, at], grad_all[me, :, later]
+            key_turned = key_two.T
+            grad_key, grad_value, turned = 0.0, 0.0, []
+            for h, mine in enumerate((first, ~first)):
+                query_h = jnp.where(mine, query_two, 0.0).astype(bfloat)
+                grad_h = jnp.where(mine, grad_two, 0.0).astype(bfloat)
+                scores = jnp.where(valid[...] > 0.0, matmul_nt(key_two, query_h), NEGATIVE)
+                expo = jnp.exp(scores - jnp.max(scores, axis=0, keepdims=True))
+                probs = expo * (1.0 / jnp.sum(expo, axis=0, keepdims=True))
+                grad_value = grad_value + matmul(probs.astype(bfloat), grad_h)
+                grad_probs = matmul_nt(value_two, grad_h)
+                inner = jnp.sum(probs * grad_probs, axis=0, keepdims=True)
+                grad_scores = (probs * (grad_probs - inner)).astype(bfloat)
+                grad_key = grad_key + matmul(grad_scores, query_h)
+                grad_query = matmul(key_turned, grad_scores)
+                turned.append(grad_query[h * (pair // 2) : (h + 1) * (pair // 2)])
+            query_all[me, :, at] = (jnp.concatenate(turned, axis=0) * scale).T.astype(bfloat)
+            grad_all[me, :, at] = grad_key.astype(bfloat)
+            grad_all[me, :, later] = grad_value.astype(bfloat)
+
+        advance()
+    got_grad = exchange.rows(grad_all)
+    got_query = exchange.rows(query_all)
+    loads[4].wait()
+    for i in range(n):
+        block = w_qkv[i].reshape(step, 3 * width)
+        work[:, i * step : (i + 1) * step] = matmul_nt(grad_all[me], block[:, width:]).astype(bfloat)
+    pieces = [matmul_nt(query_all[me], w_qkv[i].reshape(step, 3 * width)[:, :width]) for i in range(n)]
+    from_query = jnp.concatenate(pieces, axis=1)
+    hidden_copies = []
+    for s in range(1, seq_size):
+        to, device = place.peer(3, s)
+        source = work.at[pl.ds(pl.multiple_of(to * token_rows, 16), token_rows)]
+        copy = remote(source, hidden_in.at[s - 1], hidden_send.at[s - 1], hidden_recv.at[s - 1], device)
+        copy.start()
+        hidden_copies.append(copy)
+    advance()
+    got_grad()
+    got_query()
+    got_hidden()
+    got_own()
+    weight_grad(own_core, query_all, g_qkv)
+    weight_grad(hidden_core, grad_all, g_qkv, width)
+    advance()
+    grad = work[pl.ds(pl.multiple_of(place.seq * token_rows, 16), token_rows)].astype(f32)
+    rest = jnp.zeros((token_rows - rows, width), f32)
+    grad = grad + jnp.concatenate([from_query, rest], axis=0)
+    advance()
+    for s, copy in enumerate(hidden_copies):
+        copy.wait_recv()
+        grad = grad + hidden_in[s].astype(f32)
+    normed = normed_one[...]
+    g_tokens[...] = norm_back(grad, normed, inverse_one[...], gains[0:1])
+    g_tokens[0:rows] += grad_after[...]
+    gain_row = jnp.sum(grad * normed, axis=0, keepdims=True)
+    shift_row = jnp.sum(grad, axis=0, keepdims=True)
+    slots_in = jnp.concatenate([gain_row, shift_row, small[2:]], axis=0)
+    small_out[...] = small_sum(place, slots_in, slots, small_send, small_recv, advance)
+    while state[0] < total + 3 * LAG:
+        advance()
+    scatter.finish()
+    exchange.finish()
+    for copy in hidden_copies:
+        copy.wait_send()
+
+
+def half_tail(matrix, seq_size):
+    half = seq_size // 2
+    if matrix.by_rows:
+        return (half, matrix.rows, matrix.cols)
+    return (matrix.rows, half * matrix.cols)
+
+
+def backward_attention(n, seq_size, matrices, inputs, loaded, early):
+    grad_after, mixed, query, normed_one, inverse_one, gains, valid, small = inputs
+    bfloat, f32 = jnp.bfloat16, jnp.float32
+    vmem, any_space = pl.BlockSpec(memory_space=pltpu.VMEM), pl.BlockSpec(memory_space=pl.ANY)
+    shapes = [m.shape(n, seq_size) for m in matrices]
+    chunks = sum(m.parts for m in matrices)
+    rows, width = query.shape
+    all_rows = loaded[2].shape[0]
+    largest = max(n, seq_size)
+    sem = pltpu.SemaphoreType.DMA
+    return pl.pallas_call(
+        functools.partial(backward_kernel, n, seq_size, matrices),
+        out_shape=[jax.ShapeDtypeStruct((m.rows, m.cols), f32) for m in matrices]
+        + [jax.ShapeDtypeStruct(normed_one.shape, f32), jax.ShapeDtypeStruct(small.shape, f32)],
+        in_specs=[vmem] * len(inputs) + [any_space] * (len(loaded) + len(early)),
+        out_specs=[vmem] * (len(matrices) + 2),
+        scratch_shapes=[pltpu.VMEM(x.shape, bfloat) for x in loaded[:3]]
+        + [pltpu.VMEM((2, n) + half_tail(m, seq_size), bfloat) for m in matrices]
+        + [pltpu.VMEM((2, n - 1, n + 1) + half_tail(m, seq_size), bfloat) for m in matrices]
+        + [pltpu.VMEM((seq_size - 1,) + ((1, m.rows, m.cols) if m.by_rows else (m.rows, m.cols)), bfloat) for m in matrices]
+        + [
+            pltpu.VMEM((n - 1, width // n, rows), bfloat),
+            pltpu.VMEM((n, width // n, rows), bfloat),
+            pltpu.VMEM((n, rows, width), bfloat),
+            pltpu.VMEM((n - 1, width // n, all_rows), bfloat),
+            pltpu.VMEM((n, width // n, all_rows), bfloat),
+            pltpu.VMEM((n - 1, width // n, rows), bfloat),
+            pltpu.VMEM((n, width // n, rows), bfloat),
+            pltpu.VMEM((n, rows, width), bfloat),
+            pltpu.VMEM((n, all_rows, 2 * width), bfloat),
+            pltpu.VMEM((seq_size - 1,) + normed_one.shape, bfloat),
+            pltpu.VMEM((rows, width), bfloat),
+            sem((len(loaded),)),
+        ]
+        + [sem((8, n - 1))] * 2
+        + [sem((seq_size - 1,))] * 2
+        + [pltpu.VMEM((4, largest) + small.shape, f32)]
+        + [sem((4, largest - 1))] * 2
+        + [sem((chunks, 2))]
+        + [sem((chunks, seq_size - 1))] * 2
+        + [sem((chunks, 4, n - 1))] * 2,
+        compiler_params=pltpu.CompilerParams(
+            collective_id=1, has_side_effects=True, vmem_limit_bytes=VMEM_LIMIT
+        ),
+    )(*inputs, *loaded, *early)
 
 
 def columns(ref, first, count):
@@ -684,21 +981,22 @@
     tile = 512
     advance_to(0)
     for at in range(0, width, tile):
-        query[:, at : at + tile] = matmul(hidden_all[place.seq], columns(w_qkv, at, tile)).astype(bfloat)
+        own = hidden_all[place.seq, pl.ds(0, query.shape[0])]
+        query[:, at : at + tile] = matmul(own, columns(w_qkv, at, tile)).astype(bfloat)
     for copy in hidden_copies:
         copy.wait_recv()
-    hidden = hidden_all[...].reshape(-1, width)
 
     @pl.loop(0, width // tile)
     def _(t):
         at = pl.multiple_of(t * tile, tile)
+        hidden = hidden_all[...].reshape(-1, width)
         keys[:, pl.ds(at, tile)] = matmul(hidden, columns(w_qkv, at + width, tile)).astype(bfloat)
         values[:, pl.ds(at, tile)] = matmul(hidden, columns(w_qkv, at + 2 * width, tile)).astype(bfloat)
 
     advance()
     pair = 2 * width // HEADS
     scale = (width // HEADS) ** (-0.5)
-    rows = tokens.shape[0]
+    rows = query.shape[0]
     first = lax.broadcasted_iota(jnp.int32, (rows, pair), 1) < pair // 2
     pairs, segments = HEADS // 2, 4
     for segment in range(segments):
@@ -719,7 +1017,7 @@
         advance()
     advance_to(1)
     for at in range(0, width, tile):
-        after[:, at : at + tile] = tokens[:, at : at + tile] + matmul(mixed[...], columns(w_out, at, tile))
+        after[:, at : at + tile] = tokens[:rows, at : at + tile] + matmul(mixed[...], columns(w_out, at, tile))
     normed, inverse = normalize(after[...])
     normed_two[...] = normed
     inverse_two[...] = inverse
@@ -739,7 +1037,7 @@
         block = w_down[i].reshape(deep, width)
         for at in range(0, width, tile):
             after[:, at : at + tile] += matmul(act[:, i * deep : (i + 1) * deep], block[:, at : at + tile])
-    planes[...] = after[: planes.shape[0]].astype(bfloat)
+    planes[...] = after[...].astype(bfloat)
     advance_to(4)
     while state[0] < total + 3 * LAG:
         advance()
@@ -767,17 +1065,17 @@
         ((8, width), f32),
         ((seq_size,) + index.shape, jnp.int32),
         ((seq_size, rows, width), bfloat),
-        ((rows, width), bfloat),
+        ((plane_rows, width), bfloat),
         ((seq_size * rows, width), bfloat),
         ((seq_size * rows, width), bfloat),
-        ((rows, width), bfloat),
+        ((plane_rows, width), bfloat),
         ((rows, width), f32),
         ((rows, 1), f32),
-        ((rows, width), f32),
-        ((rows, 1), f32),
-        ((rows, width), bfloat),
-        ((rows, ff), bfloat),
-        ((rows, ff), bfloat),
+        ((plane_rows, width), f32),
+        ((plane_rows, 1), f32),
+        ((plane_rows, width), bfloat),
+        ((plane_rows, ff), bfloat),
+        ((plane_rows, ff), bfloat),
         ((plane_rows, width), bfloat),
         ((plane_rows, matrices[4].cols * seq_size), bfloat),
     ]
@@ -789,7 +1087,7 @@
         in_specs=[vmem] * (len(matrices) + 4),
         out_specs=[any_space] * len(matrices) + [vmem] * len(results),
         scratch_shapes=[pltpu.VMEM(s, bfloat) for s in shapes]
-        + [pltpu.VMEM((rows, width), f32)]
+        + [pltpu.VMEM((plane_rows, width), f32)]
         + [sem((seq_size - 1,))] * 4
         + [pltpu.VMEM((4, largest) + gains.shape, f32)]
         + [sem((4, largest - 1))] * 2
@@ -851,6 +1149,10 @@
 
 def join_heads(stacked):
     return stacked.transpose(1, 0, 2).reshape(stacked.shape[1], stacked.shape[0] * stacked.shape[2])
+
+
+def split_at(values, count):
+    return values[:count], values[count:]
 
 
 def shards(
@@ -901,89 +1203,43 @@
     )
     gains_all, index_all, hidden_all, query, keys_all, values_all, mixed = made[:7]
     normed_one, inverse_one, normed_two, inverse_two, hidden_two, activated, slope, plane_rows, own_texels = made[7:]
-    qkv_weight, out_weight, up_weight, down_weight, unpatch_weight = [
-        w.reshape(-1, w.shape[-1]) for w in wholes
-    ]
-    gain_one, gain_two = gains_all[0], gains_all[2]
-    hidden_one = lax.dynamic_index_in_dim(hidden_all, lax.axis_index("seq"), 0, keepdims=False)
-    density, color_value, own_grad_texels, grad_w_one, grad_b_one, grad_w_two, grad_b_two = decode(
-        n, seq_size, own_texels, index_all, dec_w1, dec_b1, dec_w2, dec_b2, d_density, d_color[0]
+    qkv, out, up, down, unpatch = matrices
+    (density, color_value, grad_w_one, grad_b_one, grad_w_two, grad_b_two, grad_after, norm_grads), grads = split_at(
+        middle(
+            n,
+            seq_size,
+            (up, down, unpatch),
+            (own_texels, index_all, dec_w1, dec_b1, dec_w2, dec_b2, d_density, d_color[0]),
+            (plane_rows, activated, slope, hidden_two, normed_two, inverse_two, gains_all),
+            wholes[2:],
+        ),
+        8,
     )
-    grad_b_one, grad_w_two, grad_b_two = grad_b_one[:, 0], grad_w_two[:4].T, grad_b_two[:4, 0]
-    query_heads = split_heads(query, HEADS)
-    key_heads = split_heads(keys_all, HEADS)
-    value_heads = split_heads(values_all, HEADS)
-    grad_planes = matmul_nt(own_grad_texels, unpatch_weight)
-    grad_unpatch = matmul_tn(plane_rows, own_grad_texels)
-    grad_layer = jnp.concatenate(
-        [grad_planes, jnp.zeros((tok_dev - plane_dev, width), jnp.float32)], axis=0
+    decoder = (grad_w_one, grad_b_one[:, 0], grad_w_two[:4].T, grad_b_two[:4, 0])
+    flat = jnp.concatenate([part.reshape(-1) for part in decoder])
+    lines = -(-(flat.shape[0] + 4 * width) // (8 * width)) * 8
+    flat = jnp.pad(flat, (0, (lines - 4) * width - flat.shape[0])).reshape(-1, width)
+    small = jnp.concatenate([jnp.zeros((2, width), jnp.float32), norm_grads, flat], axis=0)
+    valid = key_valid.astype(jnp.float32)[:, None]
+    block_sums, (grad_tokens, small_sums) = split_at(
+        backward_attention(
+            n,
+            seq_size,
+            (unpatch, down, up, out, qkv),
+            (grad_after, mixed, query, normed_one, inverse_one, gains_all, valid, small),
+            (wholes[1], wholes[0], keys_all, values_all, hidden_all.reshape(-1, width)),
+            (grads[2], grads[1], grads[0]),
+        ),
+        5,
     )
-    grad_layer_low = grad_layer.astype(bfloat)
-    grad_down = matmul_tn(activated, grad_layer_low)
-    grad_pre = (matmul_nt(grad_layer_low, down_weight) * slope.astype(jnp.float32)).astype(bfloat)
-    grad_up = matmul_tn(hidden_two, grad_pre)
-    grad_norm_two, grad_gain_two, grad_shift_two = norm_backward(
-        matmul_nt(grad_pre, up_weight), normed_two, inverse_two, gain_two
-    )
-    grad_after = grad_layer + grad_norm_two
-    grad_after_low = grad_after.astype(bfloat)
-    grad_out_weight = matmul_tn(mixed, grad_after_low)
-    grad_mixed = matmul_nt(grad_after_low, out_weight).astype(bfloat)
-    grad_heads = split_heads(grad_mixed, HEADS)
-
-    def head_backward(parts):
-        query_h, key_h, value_h, grad_h = parts
-        scores = jnp.where(key_valid[None, :], matmul_nt(query_h, key_h) * scale, NEGATIVE)
-        probs = jax.nn.softmax(scores, axis=-1)
-        grad_value = matmul_tn(probs.astype(bfloat), grad_h)
-        grad_probs = matmul_nt(grad_h, value_h)
-        grad_scores = (
-            probs * (grad_probs - jnp.sum(probs * grad_probs, axis=-1, keepdims=True))
-        ).astype(bfloat)
-        grad_query = matmul(grad_scores, key_h) * scale
-        grad_key = matmul_tn(grad_scores, query_h) * scale
-        return (grad_query, grad_key, grad_value)
-
-    grad_query, grad_key, grad_value = lax.map(
-        head_backward, (query_heads, key_heads, value_heads, grad_heads)
-    )
-    own_key_grad, own_value_grad = (
-        lax.psum_scatter(
-            join_heads(grad_key).astype(jnp.bfloat16), "seq", scatter_dimension=0, tiled=True
-        ).astype(jnp.float32),
-        lax.psum_scatter(
-            join_heads(grad_value).astype(jnp.bfloat16), "seq", scatter_dimension=0, tiled=True
-        ).astype(jnp.float32),
-    )
-    grad_qkv = jnp.concatenate(
-        [join_heads(grad_query), own_key_grad, own_value_grad], axis=1
-    ).astype(bfloat)
-    grad_qkv_weight = matmul_tn(hidden_one, grad_qkv)
-    grad_norm_one, grad_gain_one, grad_shift_one = norm_backward(
-        matmul_nt(grad_qkv, qkv_weight), normed_one, inverse_one, gain_one
-    )
-    grad_tokens = grad_after + grad_norm_one
-    whole_grads = [
-        grad.astype(bfloat).reshape(m.shape(n, seq_size))
-        for m, grad in zip(matrices, (grad_qkv_weight, grad_out_weight, grad_up, grad_down, grad_unpatch))
-    ]
-    small_parts = [grad_gain_one, grad_shift_one, grad_gain_two, grad_shift_two]
-    small_parts += [grad_w_one, grad_b_one, grad_w_two, grad_b_two]
-    flat = jnp.concatenate([part.reshape(-1) for part in small_parts])
-    lanes = 128
-    padded = -(-flat.shape[0] // (8 * lanes)) * 8 * lanes
-    small = jnp.pad(flat, (0, padded - flat.shape[0])).reshape(-1, lanes)
-    *block_sums, small_sums = scatter_grads(n, seq_size, matrices, whole_grads, small)
-    flat_sums, at, sums = small_sums.reshape(-1), 0, []
-    for part in small_parts:
-        sums.append(flat_sums[at : at + part.size].reshape(part.shape))
+    flat_sums, at, decoder_sums = small_sums[4:].reshape(-1), 0, []
+    for part in decoder:
+        decoder_sums.append(flat_sums[at : at + part.size].reshape(part.shape))
         at += part.size
     own = width // (dp_size * seq_size)
-    sum_qkv, sum_out, sum_up, sum_down, sum_unpatch = block_sums
-    sum_gain_one, sum_shift_one, sum_gain_two, sum_shift_two = [
-        lax.dynamic_slice(part, (device * own,), (own,)) for part in sums[:4]
-    ]
-    decoder_sums = sums[4:]
+    sum_unpatch, sum_down, sum_up, sum_out, sum_qkv = block_sums
+    norm_sums = lax.dynamic_slice(small_sums, (0, device * own), (4, own))
+    sum_gain_one, sum_shift_one, sum_gain_two, sum_shift_two = [norm_sums[i] for i in range(4)]
     return (
         density,
         color_value[None],

time: 731 us -> 464 us (0.63)
  matrix products: 170 us -> 0 us
  waiting for transfers between devices: 56.9 us -> 0 us
  Pallas kernels: 394 us -> 429 us
  local copies, waits for them, and re-layouts: 53.8 us -> 21.9 us
  other arithmetic: 28.7 us -> 4.69 us
  between operations: 15.5 us -> 2.01 us
    dot_general x90 -> x0, matrix products: 170 us -> none  [the longest x37 77.5 us: matmul_tn(): lax.dot_general(left, right, (((0,), (0,)), ((), ())), preferred_element_...]
    unnamed x4 -> x0, waiting for transfers between devices: 56.9 us -> none
    pallas_call x2, Pallas kernels: 206 us -> 241 us  [the longest x1 166 us: backward_attention(): pl.pallas_call(functools.partial(backward_kernel, n, seq_size, matrices),...]
    unnamed x63 -> x40, local copies, waits for them, and re-layouts: 24 us -> 11 us
    or x16 -> x0, other arithmetic: 10.6 us -> none  [shards(): (offset < plane_dev) | (owner * (tok_dev - plane_dev) + offset - plane_de...]
    pallas_call x3 -> x0, local copies, waits for them, and re-layouts: 9.61 us -> none  [forward_layer(): pl.pallas_call(functools.partial(forward_kernel, n, seq_size, matrices),...]
  transfers between devices with their start and end apart: 2 -> 0, of which waited for: 2 -> 0; matrix products, arithmetic and copies ran while one was open for 4% -> 0% of each run, Pallas kernels for 0% -> 0%
where the time goes in v3:
time: 464 us; the launch traced here: 457 us
  Pallas kernels  429 us (92%)
  local copies, waits for them, and re-layouts  21.9 us (5%)
  other arithmetic  4.69 us (1%)
    pallas_call x1, Pallas kernels, forward_layer(): pl.pallas_call(functools.partial(forward_kernel, n, seq_size, matrices),...  188 us
    pallas_call x1, Pallas kernels, backward_attention(): pl.pallas_call(functools.partial(backward_kernel, n, seq_size, matrices),...  166 us
    pallas_call x1, Pallas kernels, middle(): pl.pallas_call(functools.partial(middle_kernel, n, seq_size, matrices), o...  75 us
    unnamed x40, local copies, waits for them, and re-layouts  11 us

profile of v3, /device:TPU:0, one launch (start us, length us, event | category | flops | bytes accessed | tf_op | source)
XLA Modules:
  0.0 457.3 jit_solution(12437232485163487881)
XLA Ops:
  0.6 0.0 copy-start.10
  0.7 0.0 copy-start.7
  0.7 0.0 copy-start.8
  0.7 0.0 copy-start.11
  0.7 0.0 copy-start.12
  0.7 0.7 pad_maximum_fusion.1
  1.4 0.4 dynamic_update_slice.3.refs_6_
  1.8 0.0 copy-start.5
  2.5 0.6 or_convert_fusion.refs_8_
  3.1 1.4 copy.63
  4.5 187.6 %shard_map.297 = (bf16[2,2,2,128,3072]{4,3,2,1,0:T(8,128)(2,1)}, bf16[2,2,2,128,1024]{4,3,2,1,0:T(8,128)(2,1)}, bf16[2,2,2,128,4096]{4,3,2,1,0:T(8,128)(2,1)}, b...) custom-call(f32[128,768]{1,0:T(8,128)} %refs_0_.1, ...), custom_call_target="tpu_custom_call" | custom-call | tf_op jit(solution)/shard_map/pallas_call | solution.py:1083
  192.1 0.0 copy-done.10
  192.1 0.1 copy.49
  192.2 0.6 pad.12.refs_4_
  192.8 0.7 copy.50.refs_2_
  193.5 0.6 copy.62
  194.2 0.7 copy.51.refs_3_
  194.9 0.7 copy.52.refs_5_
  195.6 75.0 %shard_map.298 = (f32[1,2048]{1,0:T(1,128)}, f32[3,2048]{1,0:T(4,128)}, f32[96,64]{1,0:T(8,128)}, f32[64,1]{1,0:T(8,128)}, f32[8,64]{1,0:T(8,128)}, /*index=5*/f...) custom-call(bf16[192,2048]{1,0:T(8,128)(2,1)} %get-tuple-element.55., ...), custom_call_target="tpu_custom_call" | custom-call | tf_op jit(solution)/shard_map/pallas_call | solution.py:546
  270.6 0.7 slice_bitcast_fusion
  271.3 0.1 copy.54
  271.4 0.1 reshape.190
  271.5 0.9 reshape.189
  272.4 0.9 reduce
  273.2 0.8 slice_reduce_fusion
  274.0 0.1 concatenate.6
  274.2 1.4 pad_maximum_fusion.refs_7_
  275.6 1.1 fusion.11.refs_6_
  276.6 166.1 %shard_map.299 = (f32[128,512]{1,0:T(8,128)}, f32[128,1024]{1,0:T(8,128)}, f32[128,1024]{1,0:T(8,128)}, f32[128,256]{1,0:T(8,128)}, f32[128,768]{1,0:T(8,128)}, /*index=5*/f32[224,1024]{1,0:T(8,128)}, f32[16,1024]{1,0:T(8,128)}) custom-call(f32[192,1024]{1,0:T(8,128)} %get-tuple-element.69.refs_0_, bf16[192,1024]{1,0:T(8,128)(2,1)} %get-tuple-element.70.refs_1_, ...), custom_call_target="tpu_custom_call" | custom-call | tf_op jit(solution)/shard_map/pallas_call | solution.py:857
  442.8 0.9 slice.45
  443.8 1.6 slice.47
  445.4 0.7 copy.57
  446.1 0.5 slice.50
  446.6 0.6 slice.52
  447.2 0.8 slice.44
  448.0 0.1 reshape.193
  448.1 0.7 copy.56
  448.8 0.7 constant_dynamic-slice_fusion
  449.5 0.5 slice_bitcast_fusion.1
  450.1 0.6 copy.55
  450.7 0.6 copy.73
  451.3 0.9 copy.74
  452.2 0.0 copy-done.3
  452.2 0.7 copy.75
  453.0 1.6 copy.76
  454.5 0.8 copy.77
  455.3 0.8 copy.78
  456.1 0.7 copy.79
  (26 shorter events, 0.1 us)
Async XLA Ops:
  0.6 191.4 %copy-start.10 = (f32[64,4]{0,1:T(4,128)S(1)}, f32[64,4]{0,1:T(4,128)}, u32[]{:S(2)}) copy-start(f32[64,4]{0,1:T(4,128)} %param.30) | copy-start | bytes 3076
  0.7 192.2 %copy-start.7 = (f32[96,64]{0,1:T(8,128)S(1)}, f32[96,64]{0,1:T(8,128)}, u32[]{:S(2)}) copy-start(f32[96,64]{0,1:T(8,128)} %param.28) | copy-start | bytes 73732
  0.7 192.9 %copy-start.8 = (f32[1,3,2048]{2,0,1:T(1,128)S(1)}, f32[1,3,2048]{2,0,1:T(1,128)}, u32[]{:S(2)}) copy-start(f32[1,3,2048]{2,0,1:T(1,128)} %param.35) | copy-start | bytes 73732
  0.7 193.5 %copy-start.11 = (f32[64]{0:T(128)S(1)}, f32[64]{0:T(128)}, u32[]{:S(2)}) copy-start(f32[64]{0:T(128)} %param.29) | copy-start | bytes 772
  0.7 194.2 %copy-start.12 = (f32[4]{0:T(128)S(1)}, f32[4]{0:T(128)}, u32[]{:S(2)}) copy-start(f32[4]{0:T(128)} %param.31) | copy-start | bytes 52
  1.8 2.6 copy-start.5
  442.8 7.3 %copy-start.6 = (f32[3,2048]{1,0:T(4,128)S(1)}, f32[3,2048]{1,0:T(4,128)}, u32[]{:S(2)}) copy-start(f32[3,2048]{1,0:T(4,128)} %get-tuple-element.68) | copy-start | bytes 73732
  442.8 7.9 %copy-start.9 = (f32[1,2048]{1,0:T(1,128)S(1)}, f32[1,2048]{1,0:T(1,128)}, u32[]{:S(2)}) copy-start(f32[1,2048]{1,0:T(1,128)} %get-tuple-element.162) | copy-start | bytes 24580
  442.8 8.5 %copy-start = (f32[224,1024]{1,0:T(8,128)S(1)}, f32[224,1024]{1,0:T(8,128)}, u32[]{:S(2)}) copy-start(f32[224,1024]{1,0:T(8,128)} %get-tuple-element.87) | copy-start | bytes 2752516
  442.8 9.4 %copy-start.3 = (f32[128,768]{1,0:T(8,128)S(1)}, f32[128,768]{1,0:T(8,128)}, u32[]{:S(2)}) copy-start(f32[128,768]{1,0:T(8,128)} %get-tuple-element.167) | copy-start | bytes 1179652
  445.4 9.2 %copy-start.2 = (f32[128,1024]{1,0:T(8,128)S(1)}, f32[128,1024]{1,0:T(8,128)}, u32[]{:S(2)}) copy-start(f32[128,1024]{1,0:T(8,128)} %get-tuple-element.171) | copy-start | bytes 1572868
  448.0 7.3 %copy-start.1 = (f32[128,1024]{1,0:T(8,128)S(1)}, f32[128,1024]{1,0:T(8,128)}, u32[]{:S(2)}) copy-start(f32[128,1024]{1,0:T(8,128)} %get-tuple-element.172) | copy-start | bytes 1572868
  451.3 4.8 %copy-start.4 = (f32[128,512]{1,0:T(8,128)S(1)}, f32[128,512]{1,0:T(8,128)}, u32[]{:S(2)}) copy-start(f32[128,512]{1,0:T(8,128)} %get-tuple-element.173) | copy-start | bytes 786436

commit v4 on v3

--- a/solution.py
+++ b/solution.py
@@ -17,7 +17,7 @@
 EPSILON = 1e-05
 NEGATIVE = -1e30
 VMEM_LIMIT = 58 * 2**20
-AHEAD = 3
+AHEAD = 4
 LAG = 2
 
 
@@ -65,6 +65,96 @@
     return pltpu.make_async_remote_copy(
         src_ref=src, dst_ref=dst, send_sem=send, recv_sem=recv, device_id=device, device_id_type=MESH
     )
+
+
+class Line:
+    def __init__(self, place):
+        z = place.seq
+        assert place.seq_size == 4
+        self.dp, self.me = place.dp, z
+        self.pair, self.far, self.opposite = z + 1 - 2 * lax.rem(z, 2), lax.rem(z + 2, 4), 3 - z
+        self.middle = z * (3 - z) == 2
+        self.end = z * (3 - z) == 0
+
+    def _copy(self, source, target, send, recv, to):
+        return remote(source, target, send, recv, (self.dp, to))
+
+    def gather_start(self, region, send, recv):
+        own = region(self.me)
+        self._copy(own, own, send.at[0], recv.at[0], self.pair).start()
+        self._copy(own, own, send.at[1], recv.at[1], self.far).start()
+
+        @pl.when(self.middle)
+        def _():
+            self._copy(own, own, send.at[2], recv.at[2], self.opposite).start()
+
+    def gather_relay(self, region, send, recv):
+        block = region(self.far)
+        self._copy(block, block, send.at[1], recv.at[1], self.far).wait_recv()
+
+        @pl.when(self.middle)
+        def _():
+            self._copy(block, block, send.at[3], recv.at[2], self.pair).start()
+
+    def gather_take(self, region, send, recv, which=("pair", "opposite")):
+        for i, name, j in ((0, "pair", self.pair), (2, "opposite", self.opposite)):
+            if name in which:
+                self._copy(region(j), region(j), send.at[i], recv.at[i], self.pair).wait_recv()
+
+    def gather_finish(self, region, send, recv):
+        own = region(self.me)
+        for i in (0, 1):
+            self._copy(own, own, send.at[i], recv.at[i], self.pair).wait_send()
+
+        @pl.when(self.middle)
+        def _():
+            for i in (2, 3):
+                self._copy(own, own, send.at[i], recv.at[2], self.pair).wait_send()
+
+    def sum_start(self, region, slot, send, recv, which=("opposite", "far", "pair")):
+        if "opposite" in which:
+            block = region(self.opposite)
+
+            @pl.when(self.middle)
+            def _():
+                self._copy(block, slot(2), send.at[2], recv.at[2], self.opposite).start()
+
+            @pl.when(self.end)
+            def _():
+                self._copy(block, slot(3), send.at[2], recv.at[3], self.pair).start()
+
+        if "far" in which:
+
+            @pl.when(self.end)
+            def _():
+                self._copy(region(self.far), slot(1), send.at[1], recv.at[1], self.far).start()
+
+        if "pair" in which:
+            self._copy(region(self.pair), slot(0), send.at[0], recv.at[0], self.pair).start()
+
+    def sum_relay(self, region, slot, send, recv, add):
+        @pl.when(self.middle)
+        def _():
+            block = region(self.far)
+            self._copy(block, slot(3), send.at[2], recv.at[3], self.pair).wait_recv()
+            add(self.far)
+            self._copy(block, slot(1), send.at[1], recv.at[1], self.far).start()
+
+    def sum_take(self, region, slot, send, recv):
+        for i in (0, 1):
+            self._copy(region(self.me), slot(i), send.at[i], recv.at[i], self.pair).wait_recv()
+
+        @pl.when(self.middle)
+        def _():
+            self._copy(region(self.me), slot(2), send.at[2], recv.at[2], self.pair).wait_recv()
+
+    def sum_of(self, own, slots):
+        total = own.astype(jnp.float32) + slots(0).astype(jnp.float32) + slots(1).astype(jnp.float32)
+        return total + jnp.where(self.middle, slots(2).astype(jnp.float32), 0.0)
+
+    def sum_finish(self, region, slot, send, recv):
+        for i in (0, 1, 2):
+            self._copy(region(self.me), slot(0), send.at[i], recv.at[0], self.pair).wait_send()
 
 
 class Matrix:
@@ -114,18 +204,19 @@
     return end
 
 
-def small_sum(place, value, slots, send, recv, between=None):
+def small_sum(place, parts, between=None):
+    values = [part[0] for part in parts]
     for stage, axis in enumerate((2, 1, 0, 3)):
-        end = small_stage(place, value, slots, send, recv, stage, axis)
+        ends = [small_stage(place, v, *part[1:], stage, axis) for v, part in zip(values, parts)]
         if between is not None:
             between()
-        value = end()
-    return value
+        values = [end() for end in ends]
+    return values
 
 
 class Gather:
     def __init__(self, place, matrices, refs, sems):
-        self.place, self.refs = place, refs
+        self.place, self.refs, self.line = place, refs, Line(place)
         self.chunks = [(w, m, p) for w, m in enumerate(matrices) for p in range(m.parts)]
         self.seq_send, self.seq_recv, self.hop_send, self.hop_recv, self.far_send, self.far_recv = sems
         self.copies = {}
@@ -146,14 +237,19 @@
         w, matrix, part = self.chunks[k]
         return self.refs[w].at[index + matrix.tail(part, first, count)]
 
+    def _along(self, k):
+        return lambda j: self.region(k, self.place.i, j, 1), self.seq_send.at[k], self.seq_recv.at[k]
+
     def along_seq(self, k):
-        p = self.place
-        self._send((k, 0), 3, self.region(k, p.i, p.seq, 1), self.seq_send.at[k], self.seq_recv.at[k])
+        self.line.gather_start(*self._along(k))
+
+    def relay(self, k):
+        self.line.gather_relay(*self._along(k))
 
     def hop(self, k, number):
         p, half = self.place, self.place.seq_size // 2
         if number == 0:
-            self._take((k, 0))
+            self.line.gather_take(*self._along(k))
         else:
             self._take((k, 1, 0))
             self._take((k, 1, 1))
@@ -177,6 +273,8 @@
         self._take((k, 3))
 
     def finish(self):
+        for k in range(len(self.chunks)):
+            self.line.gather_finish(*self._along(k))
         for made in self.copies.values():
             for copy in made:
                 copy.wait_send()
@@ -184,7 +282,7 @@
 
 def gather_sems(n, seq_size, chunks):
     sem = pltpu.SemaphoreType.DMA
-    return [sem((chunks, seq_size - 1))] * 2 + [sem((chunks, 4, n - 1))] * 2 + [sem((chunks, n - 1))] * 2
+    return [sem((chunks, 4)), sem((chunks, 3))] + [sem((chunks, 4, n - 1))] * 2 + [sem((chunks, n - 1))] * 2
 
 
 def gelu_parts(x):
@@ -222,10 +320,7 @@
     d_color,
     density,
     color,
-    g_w1,
-    g_b1,
-    g_w2,
-    g_b2,
+    grads,
     tables,
     grad_tables,
     features,
@@ -240,23 +335,24 @@
 ):
     seq_size = place.seq_size
     bfloat, f32 = jnp.bfloat16, jnp.float32
-    samples = index.shape[2]
+    samples = index.shape[3]
     quarter = PRES * PRES // seq_size
     width = texels.shape[1]
     groups = 2 * PATCH
     cols = groups * CH
     depth = width // cols * quarter
-    hidden = w1.shape[1]
+    hidden, inputs = w1.shape
+    line = Line(place)
     for p in range(3):
         own = texels[p * quarter : (p + 1) * quarter].astype(f32)
         stacked = jnp.concatenate([own[:, i * cols : (i + 1) * cols] for i in range(width // cols)], axis=0)
         tables[p] = stacked.T.astype(bfloat)
     w1_high, w1_low = split_low(w1[...])
-    w1_stack = jnp.concatenate([w1_high, w1_low], axis=1)
+    w1_stack = jnp.concatenate([w1_high, w1_low], axis=0)
     tiles = samples // tile
 
     def one_hot(source, at, p):
-        texel = index[source, pl.ds(p, 1), at]
+        texel = index[source, p, :, at]
         key, group, _ = texel_place(texel, seq_size, place.seq)
         rows = lax.broadcasted_iota(jnp.int32, (depth, tile), 0)
         return (rows == key).astype(f32).astype(bfloat), group
@@ -275,55 +371,55 @@
                 picked.append(total)
             feature = jnp.concatenate(picked, axis=0).astype(bfloat)
             features[source, :, at] = feature
-            both = matmul_tn(w1_stack, feature)
+            both = matmul(w1_stack, feature)
             part = both[:hidden] + both[hidden:]
             own_part[:, at] = part
             part_out[source, :, at] = part.astype(bfloat)
 
-    copies = []
-    for step in range(1, seq_size):
-        to, device = place.peer(3, step)
-        forward(to)
-        copy = remote(part_out.at[to], part_in.at[step - 1], send_sem.at[step - 1], recv_sem.at[step - 1], device)
-        copy.start()
-        copies.append(copy)
+    forward_line = (lambda j: part_out.at[j], lambda i: part_in.at[i], send_sem, recv_sem)
+    for name, j in (("opposite", line.opposite), ("far", line.far), ("pair", line.pair)):
+        forward(j)
+        line.sum_start(*forward_line, which=(name,))
+
+    def add(j):
+        part_out[j] = (part_out[j].astype(f32) + part_in[3].astype(f32)).astype(bfloat)
+
+    line.sum_relay(*forward_line, add)
     forward(place.seq)
-    pre = own_part[...] + b1[...]
-    for step, copy in enumerate(copies):
-        copy.wait_recv()
-        pre = pre + part_in[step].astype(f32)
+    highest = lax.Precision.HIGHEST
+    tn, nt = (((0,), (0,)), ((), ())), (((1,), (1,)), ((), ()))
+    ones = jnp.ones((8, samples), f32)
+
+    def eight(x):
+        return jnp.concatenate([x, jnp.zeros((8 - x.shape[0], x.shape[1]), f32)], axis=0)
+
+    def dot(left, right, dims):
+        return lax.dot_general(left, right, dims, precision=highest, preferred_element_type=f32)
+
+    shift = dot(eight(b1[...]), ones, tn)
+    line.sum_take(*forward_line)
+    pre = line.sum_of(own_part[...], lambda i: part_in[i]) + shift
     act, slope = gelu_parts(pre)
-    highest = lax.Precision.HIGHEST
-    out = lax.dot_general(
-        w2[...], act, (((0,), (0,)), ((), ())), precision=highest, preferred_element_type=f32
-    ) + b2[...]
+    out = jnp.dot(w2[...], act, precision=highest, preferred_element_type=f32) + dot(eight(b2[...]), ones, tn)
     gate = 1.0 / (1.0 + jnp.exp(-out))
     first = out[:1]
     density[...] = jnp.maximum(first, 0.0) + jnp.log1p(jnp.exp(-jnp.abs(first)))
-    color[...] = gate[1:4]
-    grad_out = jnp.concatenate(
-        [
-            d_density[...] * gate[:1],
-            d_color[...] * gate[1:4] * (1.0 - gate[1:4]),
-            jnp.zeros((w2.shape[1] - 4, samples), f32),
-        ],
-        axis=0,
-    )
-    grad_pre = jnp.dot(w2[...], grad_out, precision=highest, preferred_element_type=f32) * slope
+    rows = [d_density[...] * gate[:1]]
+    for p in range(3):
+        own = gate[p + 1 : p + 2]
+        color[p] = own
+        rows.append(d_color[p] * own * (1.0 - own))
+    grad_out = jnp.concatenate(rows, axis=0)
+    grad_pre = dot(eight(w2[...]), eight(grad_out), tn) * slope
     me = place.seq
     grad_all[me] = grad_pre.astype(bfloat)
-    backs = []
-    for step in range(1, seq_size):
-        ref = grad_all.at[me]
-        copy = remote(ref, ref, back_send.at[step - 1], back_recv.at[step - 1], place.peer(3, step)[1])
-        copy.start()
-        backs.append(copy)
-    g_w2[...] = lax.dot_general(
-        grad_out, act, (((1,), (1,)), ((), ())), precision=highest, preferred_element_type=f32
-    )
-    g_b2[...] = jnp.sum(grad_out, axis=1, keepdims=True)
-    g_b1[...] = jnp.sum(grad_pre, axis=1, keepdims=True)
-    g_w1[...] = jnp.zeros(g_w1.shape, f32)
+    back_line = (lambda j: grad_all.at[j], back_send, back_recv)
+    line.gather_start(*back_line)
+    grads[...] = jnp.zeros(grads.shape, f32)
+    outs = w2.shape[0]
+    grads[hidden : hidden + outs, :hidden] = dot(grad_out, act, nt)
+    grads[hidden + 8 : hidden + 9, :hidden] = dot(ones, grad_pre, nt)[:1]
+    grads[hidden + 16 : hidden + 17, :outs] = dot(ones, grad_out, nt)[:1]
     grad_tables[...] = jnp.zeros(grad_tables.shape, f32)
 
     def backward(source):
@@ -331,8 +427,8 @@
         def _(t):
             at = pl.ds(pl.multiple_of(t * tile, tile), tile)
             grad = grad_all[source, :, at]
-            g_w1[...] += matmul_nt(features[source, :, at], grad)
-            grad_feature = matmul(w1_high, grad) + matmul(w1_low, grad)
+            grads[:hidden, :inputs] += matmul_nt(grad, features[source, :, at])
+            grad_feature = matmul_tn(w1_high, grad) + matmul_tn(w1_low, grad)
             for p in range(3):
                 hot, group = one_hot(source, at, p)
                 mine = grad_feature[p * CH : (p + 1) * CH]
@@ -342,16 +438,19 @@
                 grad_tables[p] += matmul_nt(spread, hot)
 
     backward(me)
-    for step, copy in enumerate(backs):
-        copy.wait_recv()
-        backward(place.source(3, step + 1))
+    line.gather_relay(*back_line)
+    backward(line.far)
+    line.gather_take(*back_line, which=("pair",))
+    backward(line.pair)
+    line.gather_take(*back_line, which=("opposite",))
+    backward(line.opposite)
     for p in range(3):
         back = grad_tables[p].T
         for i in range(width // cols):
             block = back[i * quarter : (i + 1) * quarter].astype(bfloat)
             grad_texels[p * quarter : (p + 1) * quarter, i * cols : (i + 1) * cols] = block
-    for copy in copies + backs:
-        copy.wait_send()
+    line.sum_finish(*forward_line)
+    line.gather_finish(*back_line)
 
 
 def core_columns(ref, n, segment, to):
@@ -422,10 +521,10 @@
 
 
 def feed_back(place, matrices, refs):
-    (planes, act, slope, hidden_two, normed_two, inverse_two, gains, weights) = refs[:8]
+    (planes, hidden_two, inverse_two, gains, act_in, slope_in, normed_in, weights) = refs[:8]
     (grads_out, grad_after, norm_grads, bufs) = refs[8:12]
     (planes_split, planes_all, act_split, act_all, hidden_split, hidden_all) = refs[12:18]
-    (texels_all, layer_all, pre_all, layer, load_sem, out_sem, send, recv) = refs[18:26]
+    (texels_all, layer_all, pre_all, layer, act, slope, normed_two, load_sem, out_sem, send, recv) = refs[18:29]
     grads = [buf.at[0] for buf in bufs]
     n = place.n
     bfloat, f32 = jnp.bfloat16, jnp.float32
@@ -436,13 +535,15 @@
     loads, waits = [], []
 
     def start():
-        for k in (2, 1, 0):
-            copy = pltpu.make_async_copy(weights[k], bufs[k], load_sem.at[k])
+        pairs = [(act_in, act)] + [(weights[k], bufs[k]) for k in (2, 1, 0)] + [(slope_in, slope), (normed_in, normed_two)]
+        for k, (source, target) in enumerate(pairs):
+            copy = pltpu.make_async_copy(source, target, load_sem.at[k])
             copy.start()
             loads.append(copy)
 
     def start_remote():
         waits.append(exchange.columns(planes, unpatch.rows, planes_split, planes_all))
+        loads[0].wait()
         waits.append(exchange.columns(act, place.seq_size * down.rows, act_split, act_all))
         waits.append(exchange.columns(hidden_two, up.rows, hidden_split, hidden_all))
 
@@ -455,7 +556,7 @@
 
     def end():
         got_texels = exchange.rows(texels_all)
-        loads[0].wait()
+        loads[1].wait()
         grad_texels = texels_all[me]
         step = layer.shape[1] // n
         for i in range(n):
@@ -463,7 +564,8 @@
             layer[:, i * step : (i + 1) * step] = matmul_nt(grad_texels, block)
         layer_all[me] = layer[...].astype(bfloat)
         got_layer = exchange.rows(layer_all)
-        loads[1].wait()
+        loads[2].wait()
+        loads[4].wait()
         step = act.shape[1] // (n * n)
         for i in range(n):
             for j in range(n):
@@ -476,7 +578,8 @@
         got_texels()
         weight_grad(planes_all, texels_all, grads[2])
         put(2)
-        loads[2].wait()
+        loads[3].wait()
+        loads[5].wait()
         step = layer.shape[1] // n
         pieces = []
         for i in range(n):
@@ -511,7 +614,7 @@
         return taken
 
     decode_in, feed_in, weights = take(8), take(7), take(3)
-    density, color, g_w1, g_b1, g_w2, g_b2, grad_after, norm_grads = take(8)
+    density, color, decoder_grads, grad_after, norm_grads = take(5)
     grads_out, bufs, decode_scratch = take(3), take(3), take(11)
     place = Place(n, seq_size)
     feed = list(feed_in) + [weights, grads_out, grad_after, norm_grads, bufs] + refs
@@ -520,20 +623,17 @@
     start()
     place.enter((2, 3))
     start_remote()
-    tile = min(512, decode_in[1].shape[2])
-    outs = (density, color, g_w1, g_b1, g_w2, g_b2)
+    tile = min(512, decode_in[1].shape[3])
+    outs = (density, color, decoder_grads)
     decode_both(place, texels_all.at[place.i[2]], tile, *decode_in, *outs, *decode_scratch)
     end()
 
 
 def middle(n, seq_size, matrices, decode_in, feed_in, weights):
-    texels, index, dec_w1, dec_b1, dec_w2, dec_b2, d_density, d_color = decode_in
-    planes, act, slope, hidden_two, normed_two, inverse_two, gains = feed_in
+    texels, index, w1, b1, w2, b2, d_density, d_color = decode_in
+    planes, hidden_two, inverse_two, gains, act, slope, normed_two = feed_in
     bfloat, f32 = jnp.bfloat16, jnp.float32
-    samples, hidden = index.shape[2], dec_w1.shape[1]
-    slots = 8
-    w2 = jnp.pad(dec_w2, ((0, 0), (0, slots - dec_w2.shape[1])))
-    b2 = jnp.pad(dec_b2, (0, slots - dec_b2.shape[0]))[:, None]
+    samples, hidden = index.shape[3], w1.shape[0]
     quarter = PRES * PRES // seq_size
     cols = 2 * PATCH * CH
     depth = texels.shape[1] // cols * quarter
@@ -547,28 +647,25 @@
         functools.partial(middle_kernel, n, seq_size, matrices),
         out_shape=[
             jax.ShapeDtypeStruct((1, samples), f32),
-            jax.ShapeDtypeStruct((3, samples), f32),
-            jax.ShapeDtypeStruct(dec_w1.shape, f32),
-            jax.ShapeDtypeStruct((hidden, 1), f32),
-            jax.ShapeDtypeStruct((slots, hidden), f32),
-            jax.ShapeDtypeStruct((slots, 1), f32),
+            jax.ShapeDtypeStruct((3, 1, samples), f32),
+            jax.ShapeDtypeStruct((hidden + 24, 128), f32),
             jax.ShapeDtypeStruct((rows, width), f32),
             jax.ShapeDtypeStruct((2, width), f32),
         ]
         + [jax.ShapeDtypeStruct(s, bfloat) for s in halves],
-        in_specs=[vmem] * 15 + [any_space] * 3,
-        out_specs=[vmem] * 8 + [any_space] * 3,
+        in_specs=[vmem] * 12 + [any_space] * 6,
+        out_specs=[vmem] * 5 + [any_space] * 3,
         scratch_shapes=[pltpu.VMEM(s, bfloat) for s in shapes]
         + [
             pltpu.VMEM((3, cols, depth), bfloat),
             pltpu.VMEM((3, cols, depth), f32),
             pltpu.VMEM((seq_size, 3 * CH, samples), bfloat),
             pltpu.VMEM((seq_size, hidden, samples), bfloat),
-            pltpu.VMEM((seq_size - 1, hidden, samples), bfloat),
+            pltpu.VMEM((4, hidden, samples), bfloat),
             pltpu.VMEM((hidden, samples), f32),
             pltpu.VMEM((seq_size, hidden, samples), bfloat),
         ]
-        + [sem((seq_size - 1,))] * 4
+        + [sem((3,)), sem((4,)), sem((4,)), sem((3,))]
         + [
             pltpu.VMEM((n - 1, width // n, rows), bfloat),
             pltpu.VMEM((n, width // n, rows), bfloat),
@@ -580,20 +677,23 @@
             pltpu.VMEM((n, rows, width), bfloat),
             pltpu.VMEM((n, rows, ff), bfloat),
             pltpu.VMEM((rows, width), f32),
-            sem((3,)),
+            pltpu.VMEM((rows, ff), bfloat),
+            pltpu.VMEM((rows, ff), bfloat),
+            pltpu.VMEM((rows, width), f32),
+            sem((6,)),
             sem((3,)),
         ]
         + [sem((8, n - 1))] * 2,
         compiler_params=pltpu.CompilerParams(
             collective_id=2, has_side_effects=True, vmem_limit_bytes=VMEM_LIMIT
         ),
-    )(texels, index, dec_w1, dec_b1[:, None], w2, b2, d_density, d_color, *feed_in, *weights)
+    )(*decode_in, *feed_in, *weights)
 
 
 class Scatter:
     def __init__(self, place, matrices, sources, kept, hops, near, outs, sems):
         self.place, self.sources, self.kept = place, sources, kept
-        self.hops, self.near, self.outs = hops, near, outs
+        self.hops, self.near, self.outs, self.line = hops, near, outs, Line(place)
         self.chunks = [(w, m, p) for w, m in enumerate(matrices) for p in range(m.parts)]
         self.load_sem, self.seq_send, self.seq_recv, self.hop_send, self.hop_recv = sems
         self.copies, self.loads = {}, {}
@@ -662,26 +762,36 @@
             for s in range(n - 1):
                 value = value + self.hops[w][(h, s, n) + local].astype(jnp.float32)
             kept[(h, p.i[1 - h]) + local] = value.astype(jnp.bfloat16)
-        self._send(
-            (k, 0),
-            3,
-            lambda to: kept.at[self._block(matrix, part, to)],
-            lambda s: self.near[w].at[(s,) + matrix.tail(part, 0, 1)],
-            self.seq_send.at[k],
-            self.seq_recv.at[k],
-        )
+        self.line.sum_start(*self._along(k))
+
+    def _along(self, k):
+        w, matrix, part = self.chunks[k]
+        kept, near, own = self.kept[w], self.near[w], matrix.tail(part, 0, 1)
+        region, slot = lambda j: kept.at[self._block(matrix, part, j)], lambda i: near.at[(i,) + own]
+        return region, slot, self.seq_send.at[k], self.seq_recv.at[k]
+
+    def relay(self, k):
+        w, matrix, part = self.chunks[k]
+        kept, own = self.kept[w], matrix.tail(part, 0, 1)
+
+        def add(j):
+            at = self._block(matrix, part, j)
+            kept[at] = (kept[at].astype(jnp.float32) + self.near[w][(3,) + own].astype(jnp.float32)).astype(jnp.bfloat16)
+
+        self.line.sum_relay(*self._along(k), add)
 
     def arrived(self, k):
         w, matrix, part = self.chunks[k]
-        p = self.place
-        self._take((k, 0))
-        value = self.kept[w][self._block(matrix, part, p.seq)].astype(jnp.float32)
-        for s in range(p.seq_size - 1):
-            value = value + self.near[w][(s,) + matrix.tail(part, 0, 1)].astype(jnp.float32)
+        own = matrix.tail(part, 0, 1)
+        self.line.sum_take(*self._along(k))
+        value = self.kept[w][self._block(matrix, part, self.place.seq)]
+        value = self.line.sum_of(value, lambda i: self.near[w][(i,) + own])
         size = matrix.rows // matrix.parts
         self.outs[w][pl.ds(part * size, size)] = value.reshape(size, matrix.cols)
 
     def finish(self):
+        for k in range(len(self.chunks)):
+            self.line.sum_finish(*self._along(k))
         for made in self.copies.values():
             for copy in made:
                 copy.wait_send()
@@ -696,18 +806,19 @@
         del refs[:k]
         return taken
 
-    grad_after, mixed, query, normed_one, inverse_one, gains, valid, small = take(8)
+    grad_after, mixed, query, normed_one, inverse_one, gains, norm_grads, decoder_grads, scene_count = take(9)
     w_out_in, w_qkv_in, keys_in, values_in, hidden_all_in = take(5)
     early = take(count - 2)
     outs = take(count)
-    g_tokens, small_out = take(2)
+    g_tokens, *norm_outs = take(5)
+    g_w1, g_b1, g_w2, g_b2 = take(4)
     w_out, w_qkv, work = take(3)
     g_out, g_qkv = w_out.at[0], w_qkv.at[0]
     kept, hops, near = take(count), take(count), take(count)
     mixed_split, mixed_all, after_all, hidden_split, hidden_core, own_split, own_core = take(7)
     query_all, grad_all, hidden_in = take(3)
     grad_mixed, load_sem, core_send, core_recv, hidden_send, hidden_recv = take(6)
-    slots, small_send, small_recv = take(3)
+    norm_part, decoder_part = take(3), take(3)
     sems = refs
     bfloat, f32 = jnp.bfloat16, jnp.float32
     place = Place(n, seq_size)
@@ -736,9 +847,12 @@
             scatter.hop(t - LAG, 1)
         if 0 <= t - 2 * LAG < total:
             scatter.along_seq(t - 2 * LAG)
-        if 0 <= t - 3 * LAG < total:
-            scatter.arrived(t - 3 * LAG)
-
+        if 0 <= t - 2 * LAG - 1 < total:
+            scatter.relay(t - 2 * LAG - 1)
+        if 0 <= t - 3 * LAG - 1 < total:
+            scatter.arrived(t - 3 * LAG - 1)
+
+    line = Line(place)
     advance()
     advance()
     exchange = Exchange(place, core_send, core_recv)
@@ -760,6 +874,7 @@
     weight_grad(mixed_all, after_all, g_out)
     loads[2].wait()
     loads[3].wait()
+    valid = key_valid(scene_count, seq_size, rows, token_rows, 0)
     pair = 2 * width // HEADS
     scale = (width // HEADS) ** (-0.5)
     first = lax.broadcasted_iota(jnp.int32, (rows, pair), 1) < pair // 2
@@ -777,7 +892,7 @@
             for h, mine in enumerate((first, ~first)):
                 query_h = jnp.where(mine, query_two, 0.0).astype(bfloat)
                 grad_h = jnp.where(mine, grad_two, 0.0).astype(bfloat)
-                scores = jnp.where(valid[...] > 0.0, matmul_nt(key_two, query_h), NEGATIVE)
+                scores = jnp.where(valid, matmul_nt(key_two, query_h), NEGATIVE)
                 expo = jnp.exp(scores - jnp.max(scores, axis=0, keepdims=True))
                 probs = expo * (1.0 / jnp.sum(expo, axis=0, keepdims=True))
                 grad_value = grad_value + matmul(probs.astype(bfloat), grad_h)
@@ -800,41 +915,56 @@
         work[:, i * step : (i + 1) * step] = matmul_nt(grad_all[me], block[:, width:]).astype(bfloat)
     pieces = [matmul_nt(query_all[me], w_qkv[i].reshape(step, 3 * width)[:, :width]) for i in range(n)]
     from_query = jnp.concatenate(pieces, axis=1)
-    hidden_copies = []
-    for s in range(1, seq_size):
-        to, device = place.peer(3, s)
-        source = work.at[pl.ds(pl.multiple_of(to * token_rows, 16), token_rows)]
-        copy = remote(source, hidden_in.at[s - 1], hidden_send.at[s - 1], hidden_recv.at[s - 1], device)
-        copy.start()
-        hidden_copies.append(copy)
+    hidden_line = (
+        lambda j: work.at[pl.ds(pl.multiple_of(j * token_rows, 16), token_rows)],
+        lambda i: hidden_in.at[i],
+        hidden_send,
+        hidden_recv,
+    )
+    line.sum_start(*hidden_line)
     advance()
     got_grad()
     got_query()
     got_hidden()
     got_own()
     weight_grad(own_core, query_all, g_qkv)
+
+    def add(j):
+        at = pl.ds(pl.multiple_of(j * token_rows, 16), token_rows)
+        work[at] = (work[at].astype(f32) + hidden_in[3].astype(f32)).astype(bfloat)
+
+    line.sum_relay(*hidden_line, add)
     weight_grad(hidden_core, grad_all, g_qkv, width)
     advance()
-    grad = work[pl.ds(pl.multiple_of(place.seq * token_rows, 16), token_rows)].astype(f32)
+    advance()
+    line.sum_take(*hidden_line)
+    grad = line.sum_of(work[pl.ds(pl.multiple_of(place.seq * token_rows, 16), token_rows)], lambda i: hidden_in[i])
     rest = jnp.zeros((token_rows - rows, width), f32)
     grad = grad + jnp.concatenate([from_query, rest], axis=0)
-    advance()
-    for s, copy in enumerate(hidden_copies):
-        copy.wait_recv()
-        grad = grad + hidden_in[s].astype(f32)
     normed = normed_one[...]
     g_tokens[...] = norm_back(grad, normed, inverse_one[...], gains[0:1])
     g_tokens[0:rows] += grad_after[...]
     gain_row = jnp.sum(grad * normed, axis=0, keepdims=True)
     shift_row = jnp.sum(grad, axis=0, keepdims=True)
-    slots_in = jnp.concatenate([gain_row, shift_row, small[2:]], axis=0)
-    small_out[...] = small_sum(place, slots_in, slots, small_send, small_recv, advance)
-    while state[0] < total + 3 * LAG:
+    norm_rows = jnp.concatenate([gain_row, shift_row, norm_grads[...], jnp.zeros((4, width), f32)], axis=0)
+    parts = [(norm_rows, *norm_part), (decoder_grads[...], *decoder_part)]
+    norm_sums, decoder_sums = small_sum(place, parts, advance)
+    own = norm_outs[0].shape[1]
+    spot = lax.broadcasted_iota(jnp.int32, (width, own), 0) - lax.broadcasted_iota(jnp.int32, (width, own), 1)
+    pick = (spot == (place.dp * seq_size + place.seq) * own).astype(f32)
+    picked = jnp.dot(norm_sums, pick, precision=lax.Precision.HIGHEST, preferred_element_type=f32)
+    for i, ref in enumerate(norm_outs):
+        ref[...] = picked[i : i + 1]
+    hidden, inputs = g_w1.shape
+    g_w1[...] = decoder_sums[:hidden, :inputs]
+    g_w2[...] = decoder_sums[hidden : hidden + g_w2.shape[0], :hidden]
+    g_b1[...] = decoder_sums[hidden + 8 : hidden + 9, :hidden]
+    g_b2[...] = decoder_sums[hidden + 16 : hidden + 17, : g_b2.shape[1]]
+    while state[0] < total + 3 * LAG + 1:
         advance()
     scatter.finish()
     exchange.finish()
-    for copy in hidden_copies:
-        copy.wait_send()
+    line.sum_finish(*hidden_line)
 
 
 def half_tail(matrix, seq_size):
@@ -845,7 +975,9 @@
 
 
 def backward_attention(n, seq_size, matrices, inputs, loaded, early):
-    grad_after, mixed, query, normed_one, inverse_one, gains, valid, small = inputs
+    grad_after, mixed, query, normed_one, inverse_one, gains, norm_grads, decoder_grads, scene_count = inputs
+    own = query.shape[1] // (lax.axis_size("dp") * seq_size)
+    hidden, features, outs = decoder_grads.shape[0] - 24, 3 * CH, 4
     bfloat, f32 = jnp.bfloat16, jnp.float32
     vmem, any_space = pl.BlockSpec(memory_space=pltpu.VMEM), pl.BlockSpec(memory_space=pl.ANY)
     shapes = [m.shape(n, seq_size) for m in matrices]
@@ -857,13 +989,15 @@
     return pl.pallas_call(
         functools.partial(backward_kernel, n, seq_size, matrices),
         out_shape=[jax.ShapeDtypeStruct((m.rows, m.cols), f32) for m in matrices]
-        + [jax.ShapeDtypeStruct(normed_one.shape, f32), jax.ShapeDtypeStruct(small.shape, f32)],
-        in_specs=[vmem] * len(inputs) + [any_space] * (len(loaded) + len(early)),
-        out_specs=[vmem] * (len(matrices) + 2),
+        + [jax.ShapeDtypeStruct(normed_one.shape, f32)]
+        + [jax.ShapeDtypeStruct((1, own), f32)] * 4
+        + [jax.ShapeDtypeStruct(s, f32) for s in ((hidden, features), (1, hidden), (outs, hidden), (1, outs))],
+        in_specs=[vmem] * (len(inputs) - 1) + [pl.BlockSpec(memory_space=pltpu.SMEM)] + [any_space] * (len(loaded) + len(early)),
+        out_specs=[vmem] * (len(matrices) + 9),
         scratch_shapes=[pltpu.VMEM(x.shape, bfloat) for x in loaded[:3]]
         + [pltpu.VMEM((2, n) + half_tail(m, seq_size), bfloat) for m in matrices]
         + [pltpu.VMEM((2, n - 1, n + 1) + half_tail(m, seq_size), bfloat) for m in matrices]
-        + [pltpu.VMEM((seq_size - 1,) + ((1, m.rows, m.cols) if m.by_rows else (m.rows, m.cols)), bfloat) for m in matrices]
+        + [pltpu.VMEM((4,) + ((1, m.rows, m.cols) if m.by_rows else (m.rows, m.cols)), bfloat) for m in matrices]
         + [
             pltpu.VMEM((n - 1, width // n, rows), bfloat),
             pltpu.VMEM((n, width // n, rows), bfloat),
@@ -874,16 +1008,18 @@
             pltpu.VMEM((n, width // n, rows), bfloat),
             pltpu.VMEM((n, rows, width), bfloat),
             pltpu.VMEM((n, all_rows, 2 * width), bfloat),
-            pltpu.VMEM((seq_size - 1,) + normed_one.shape, bfloat),
+            pltpu.VMEM((4,) + normed_one.shape, bfloat),
             pltpu.VMEM((rows, width), bfloat),
             sem((len(loaded),)),
         ]
         + [sem((8, n - 1))] * 2
-        + [sem((seq_size - 1,))] * 2
-        + [pltpu.VMEM((4, largest) + small.shape, f32)]
+        + [sem((3,)), sem((4,))]
+        + [pltpu.VMEM((4, largest, 8, width), f32)]
+        + [sem((4, largest - 1))] * 2
+        + [pltpu.VMEM((4, largest) + decoder_grads.shape, f32)]
         + [sem((4, largest - 1))] * 2
         + [sem((chunks, 2))]
-        + [sem((chunks, seq_size - 1))] * 2
+        + [sem((chunks, 3)), sem((chunks, 4))]
         + [sem((chunks, 4, n - 1))] * 2,
         compiler_params=pltpu.CompilerParams(
             collective_id=1, has_side_effects=True, vmem_limit_bytes=VMEM_LIMIT
@@ -912,14 +1048,17 @@
         return taken
 
     shards = take(count)
-    tokens, gains, index, valid = take(4)
+    tokens, gain_one, shift_one, gain_two, shift_two, index, scene_count = take(7)
     wholes = take(count)
-    gains_out, index_out, hidden_all, query, keys, values, mixed = take(7)
-    normed_one, inverse_one, normed_two, inverse_two, hidden_two, act, slope, planes, texels = take(9)
+    gains_out, index_out, inverse_one, inverse_two = take(4)
+    kept = take(12)
     bufs = take(count)
-    after, index_send, index_recv, hidden_send, hidden_recv, slots, small_send, small_recv, out_sem = take(9)
+    made = take(12)
+    hidden_all, query, keys, values, mixed, normed_one, normed_two, hidden_two, act, slope, planes, texels = made
+    after, index_send, index_recv, hidden_send, hidden_recv, slots, small_send, small_recv, out_sem, kept_sem = take(10)
     bfloat, f32 = jnp.bfloat16, jnp.float32
     place = Place(n, seq_size)
+    line = Line(place)
     for matrix, shard, buf in zip(matrices, shards, bufs):
         if matrix.by_rows:
             buf[place.i + (place.seq,)] = shard[...].astype(bfloat)
@@ -927,19 +1066,36 @@
             at = pl.ds(pl.multiple_of(place.seq * matrix.cols, 128), matrix.cols)
             buf[place.i + (slice(None), at)] = shard[...].astype(bfloat)
     index_out[place.seq] = index[...]
+    rows_all, width = tokens.shape
+    rows = query.shape[0]
+    own = gain_one.shape[1]
+    first_own = (place.dp * seq_size + place.seq) * own
+    spot = lax.broadcasted_iota(jnp.int32, (own, width), 1) - lax.broadcasted_iota(jnp.int32, (own, width), 0)
+    spread_out = (spot == first_own).astype(f32).astype(bfloat)
+    gains = [ref[...] for ref in (gain_one, shift_one, gain_two, shift_two)]
+    gains = jnp.concatenate(gains + [jnp.zeros((4, own), f32)], axis=0).astype(bfloat)
+    gains = matmul(gains, spread_out)
     place.enter()
     gather = Gather(place, matrices, bufs, refs)
     total = len(gather.chunks)
     outs = []
     state = [0]
 
+    def put(*which):
+        for k in which:
+            copy = pltpu.make_async_copy(made[k], kept[k], kept_sem.at[k])
+            copy.start()
+            outs.append(copy)
+
     def advance():
         t = state[0]
         state[0] += 1
+        if t + AHEAD < total:
+            gather.along_seq(t + AHEAD)
+        if t + 1 < total:
+            gather.relay(t + 1)
         if t < total:
             gather.hop(t, 0)
-            if t + AHEAD < total:
-                gather.along_seq(t + AHEAD)
         if 0 <= t - LAG < total:
             gather.hop(t - LAG, 1)
         if 0 <= t - 2 * LAG < total:
@@ -958,33 +1114,32 @@
         while state[0] <= last + 3 * LAG:
             advance()
 
-    def spread(ref, send, recv):
-        copies = []
-        for step in range(1, seq_size):
-            copy = remote(ref, ref, send.at[step - 1], recv.at[step - 1], place.peer(3, step)[1])
-            copy.start()
-            copies.append(copy)
-        return copies
-
     for k in range(AHEAD):
         gather.along_seq(k)
-    later = spread(index_out.at[place.seq], index_send, index_recv)
+    index_line = (lambda j: index_out.at[j], index_send, index_recv)
+    hidden_line = (lambda j: hidden_all.at[j], hidden_send, hidden_recv)
+    line.gather_start(*index_line)
     normed, inverse = normalize(tokens[...])
     normed_one[...] = normed
     inverse_one[...] = inverse
-    gain_sum = small_sum(place, gains[...], slots, small_send, small_recv, advance)
-    gains_out[...] = gain_sum.astype(bfloat).astype(f32)
+    put(5)
+    gather.relay(0)
+    (gains_out[...],) = small_sum(place, [(gains, slots, small_send, small_recv)], advance)
     hidden_all[place.seq] = (normed_one[...] * gains_out[0:1] + gains_out[1:2]).astype(bfloat)
-    hidden_copies = spread(hidden_all.at[place.seq], hidden_send, hidden_recv)
+    line.gather_start(*hidden_line)
+    line.gather_relay(*index_line)
     w_qkv, w_out, w_up, w_down, w_unpatch = bufs
-    width = tokens.shape[1]
     tile = 512
+    advance()
+    advance()
+    advance()
+    line.gather_relay(*hidden_line)
     advance_to(0)
     for at in range(0, width, tile):
-        own = hidden_all[place.seq, pl.ds(0, query.shape[0])]
-        query[:, at : at + tile] = matmul(own, columns(w_qkv, at, tile)).astype(bfloat)
-    for copy in hidden_copies:
-        copy.wait_recv()
+        block = hidden_all[place.seq, pl.ds(0, rows)]
+        query[:, at : at + tile] = matmul(block, columns(w_qkv, at, tile)).astype(bfloat)
+    line.gather_take(*hidden_line)
+    put(0, 1)
 
     @pl.loop(0, width // tile)
     def _(t):
@@ -993,10 +1148,11 @@
         keys[:, pl.ds(at, tile)] = matmul(hidden, columns(w_qkv, at + width, tile)).astype(bfloat)
         values[:, pl.ds(at, tile)] = matmul(hidden, columns(w_qkv, at + 2 * width, tile)).astype(bfloat)
 
+    put(2, 3)
     advance()
+    valid = key_valid(scene_count, seq_size, rows, rows_all, 1)
     pair = 2 * width // HEADS
     scale = (width // HEADS) ** (-0.5)
-    rows = query.shape[0]
     first = lax.broadcasted_iota(jnp.int32, (rows, pair), 1) < pair // 2
     pairs, segments = HEADS // 2, 4
     for segment in range(segments):
@@ -1005,16 +1161,17 @@
         def _(p):
             at = pl.ds(pl.multiple_of(p * pair, pair), pair)
             query_two, key_two, value_two = query[:, at].astype(f32) * scale, keys[:, at], values[:, at]
-            made = []
+            both = []
             for mine in (first, ~first):
                 scores = matmul_nt(jnp.where(mine, query_two, 0.0).astype(bfloat), key_two)
-                scores = jnp.where(valid[...] > 0.0, scores, NEGATIVE)
+                scores = jnp.where(valid, scores, NEGATIVE)
                 expo = jnp.exp(scores - jnp.max(scores, axis=-1, keepdims=True))
                 probs = expo * (1.0 / jnp.sum(expo, axis=-1, keepdims=True))
-                made.append(matmul(probs.astype(bfloat), value_two))
-            mixed[:, at] = jnp.where(first, made[0], made[1]).astype(bfloat)
+                both.append(matmul(probs.astype(bfloat), value_two))
+            mixed[:, at] = jnp.where(first, both[0], both[1]).astype(bfloat)
 
         advance()
+    put(4)
     advance_to(1)
     for at in range(0, width, tile):
         after[:, at : at + tile] = tokens[:rows, at : at + tile] + matmul(mixed[...], columns(w_out, at, tile))
@@ -1022,6 +1179,7 @@
     normed_two[...] = normed
     inverse_two[...] = inverse
     hidden_two[...] = (normed * gains_out[2:3] + gains_out[3:4]).astype(bfloat)
+    put(6, 7)
     advance_to(2)
 
     @pl.loop(0, act.shape[1] // tile)
@@ -1031,6 +1189,7 @@
         act[:, pl.ds(at, tile)] = value.astype(bfloat)
         slope[:, pl.ds(at, tile)] = rate.astype(bfloat)
 
+    put(8, 9)
     advance_to(3)
     deep = act.shape[1] // n
     for i in range(n):
@@ -1038,21 +1197,28 @@
         for at in range(0, width, tile):
             after[:, at : at + tile] += matmul(act[:, i * deep : (i + 1) * deep], block[:, at : at + tile])
     planes[...] = after[...].astype(bfloat)
+    put(10)
     advance_to(4)
-    while state[0] < total + 3 * LAG:
-        advance()
     for at in range(0, texels.shape[1], tile):
         texels[:, at : at + tile] = matmul(planes[...], columns(w_unpatch, at, tile)).astype(bfloat)
+    put(11)
     gather.finish()
-    for copy in later:
-        copy.wait()
-    for copy in hidden_copies:
-        copy.wait_send()
+    line.gather_take(*index_line)
+    line.gather_finish(*index_line)
+    line.gather_finish(*hidden_line)
     for copy in outs:
         copy.wait()
 
 
-def forward_layer(n, seq_size, matrices, shards, tokens, gains, index, valid):
+def key_valid(scene_count, seq_size, plane_rows, rows, axis):
+    shape = (1, seq_size * rows) if axis == 1 else (seq_size * rows, 1)
+    position = lax.broadcasted_iota(jnp.int32, shape, axis)
+    owner = lax.div(position, rows)
+    offset = position - owner * rows
+    return (offset < plane_rows) | (owner * (rows - plane_rows) + offset - plane_rows < scene_count[0, 0])
+
+
+def forward_layer(n, seq_size, matrices, shards, tokens, gains, index, scene_count):
     chunks = sum(m.parts for m in matrices)
     vmem, any_space = pl.BlockSpec(memory_space=pltpu.VMEM), pl.BlockSpec(memory_space=pl.ANY)
     shapes = [m.shape(n, seq_size) for m in matrices]
@@ -1064,15 +1230,17 @@
     results = [
         ((8, width), f32),
         ((seq_size,) + index.shape, jnp.int32),
+        ((rows, 1), f32),
+        ((plane_rows, 1), f32),
+    ]
+    kept = [
         ((seq_size, rows, width), bfloat),
         ((plane_rows, width), bfloat),
         ((seq_size * rows, width), bfloat),
         ((seq_size * rows, width), bfloat),
         ((plane_rows, width), bfloat),
         ((rows, width), f32),
-        ((rows, 1), f32),
         ((plane_rows, width), f32),
-        ((plane_rows, 1), f32),
         ((plane_rows, width), bfloat),
         ((plane_rows, ff), bfloat),
         ((plane_rows, ff), bfloat),
@@ -1083,20 +1251,21 @@
     made = pl.pallas_call(
         functools.partial(forward_kernel, n, seq_size, matrices),
         out_shape=[jax.ShapeDtypeStruct(s, bfloat) for s in shapes]
-        + [jax.ShapeDtypeStruct(s, t) for s, t in results],
-        in_specs=[vmem] * (len(matrices) + 4),
-        out_specs=[any_space] * len(matrices) + [vmem] * len(results),
+        + [jax.ShapeDtypeStruct(s, t) for s, t in results + kept],
+        in_specs=[vmem] * (len(matrices) + 6) + [pl.BlockSpec(memory_space=pltpu.SMEM)],
+        out_specs=[any_space] * len(matrices) + [vmem] * len(results) + [any_space] * len(kept),
         scratch_shapes=[pltpu.VMEM(s, bfloat) for s in shapes]
+        + [pltpu.VMEM(s, t) for s, t in kept]
         + [pltpu.VMEM((plane_rows, width), f32)]
-        + [sem((seq_size - 1,))] * 4
-        + [pltpu.VMEM((4, largest) + gains.shape, f32)]
+        + [sem((4,)), sem((3,))] * 2
+        + [pltpu.VMEM((4, largest, 8, width), f32)]
         + [sem((4, largest - 1))] * 2
-        + [sem((chunks,))]
+        + [sem((chunks,)), sem((len(kept),))]
         + gather_sems(n, seq_size, chunks),
         compiler_params=pltpu.CompilerParams(
             collective_id=0, has_side_effects=True, vmem_limit_bytes=VMEM_LIMIT
         ),
-    )(*shards, tokens, gains, index, valid)
+    )(*shards, tokens, *gains, index, scene_count)
     return made[: len(matrices)], made[len(matrices) :]
 
 
@@ -1123,32 +1292,6 @@
     return lax.dot_general(
         left, right, (((1,), (1,)), ((), ())), preferred_element_type=jnp.float32
     )
-
-
-def gelu_exact(values):
-    return jax.nn.gelu(values, approximate=False)
-
-
-def norm_forward(values, gain, shift):
-    center = values - jnp.mean(values, axis=-1, keepdims=True)
-    inverse = lax.rsqrt(jnp.mean(center * center, axis=-1, keepdims=True) + EPSILON)
-    normed = center * inverse
-    return (normed * gain + shift, normed, inverse)
-
-
-def norm_backward(grad, normed, inverse, gain):
-    scaled = grad * gain
-    inner = scaled - jnp.mean(scaled, axis=-1, keepdims=True)
-    inner = inner - normed * jnp.mean(scaled * normed, axis=-1, keepdims=True)
-    return (inner * inverse, jnp.sum(grad * normed, axis=0), jnp.sum(grad, axis=0))
-
-
-def split_heads(matrix, heads):
-    return matrix.reshape(matrix.shape[0], heads, matrix.shape[1] // heads).transpose(1, 0, 2)
-
-
-def join_heads(stacked):
-    return stacked.transpose(1, 0, 2).reshape(stacked.shape[1], stacked.shape[0] * stacked.shape[2])
 
 
 def split_at(values, count):
@@ -1177,86 +1320,60 @@
 ):
     seq_size = lax.axis_size("seq")
     dp_size = lax.axis_size("dp")
-    quarter = PRES * PRES // seq_size
-    plane_dev = 3 * quarter
-    rows_in = tokens[0]
-    tok_dev = rows_in.shape[0]
-    width = rows_in.shape[1]
-    head_dim = width // HEADS
-    scale = head_dim ** (-0.5)
-    bfloat = jnp.bfloat16
     n = round(dp_size ** (1 / 3))
     shards_of = (w_qkv, w_out, w_up, w_down, w_unpatch)
     matrices = weight_list(shards_of)
-    device = lax.axis_index("dp") * seq_size + lax.axis_index("seq")
-    gains = jnp.stack([ln1_gain, ln1_bias, ln2_gain, ln2_bias])
-    spread = jnp.zeros((8, width), jnp.float32)
-    spread = lax.dynamic_update_slice(spread, gains, (0, device * gains.shape[1]))
-    position = jnp.arange(seq_size * tok_dev, dtype=jnp.int32)
-    owner = position // tok_dev
-    offset = position % tok_dev
-    key_valid = (offset < plane_dev) | (
-        owner * (tok_dev - plane_dev) + offset - plane_dev < counts[0]
-    )
-    wholes, made = forward_layer(
-        n, seq_size, matrices, shards_of, rows_in, spread, sample_texels[0], key_valid.astype(jnp.float32)[None]
-    )
-    gains_all, index_all, hidden_all, query, keys_all, values_all, mixed = made[:7]
-    normed_one, inverse_one, normed_two, inverse_two, hidden_two, activated, slope, plane_rows, own_texels = made[7:]
     qkv, out, up, down, unpatch = matrices
-    (density, color_value, grad_w_one, grad_b_one, grad_w_two, grad_b_two, grad_after, norm_grads), grads = split_at(
+    gains = [part[None] for part in (ln1_gain, ln1_bias, ln2_gain, ln2_bias)]
+    scene_count = counts[None]
+    index = sample_texels.transpose(1, 0, 2)
+    wholes, made = forward_layer(n, seq_size, matrices, shards_of, tokens[0], gains, index, scene_count)
+    gains_all, index_all, inverse_one, inverse_two = made[:4]
+    hidden_all, query, keys, values, mixed, normed_one = made[4:10]
+    normed_two, hidden_two, act, slope, planes, texels = made[10:]
+    decoder = (dec_w1.T, dec_b1[None], dec_w2.T, dec_b2[None])
+    (density, color, decoder_grads, grad_after, norm_grads), grads = split_at(
         middle(
             n,
             seq_size,
             (up, down, unpatch),
-            (own_texels, index_all, dec_w1, dec_b1, dec_w2, dec_b2, d_density, d_color[0]),
-            (plane_rows, activated, slope, hidden_two, normed_two, inverse_two, gains_all),
+            (texels, index_all) + decoder + (d_density, d_color.transpose(1, 0, 2)),
+            (planes, hidden_two, inverse_two, gains_all, act, slope, normed_two),
             wholes[2:],
         ),
-        8,
+        5,
     )
-    decoder = (grad_w_one, grad_b_one[:, 0], grad_w_two[:4].T, grad_b_two[:4, 0])
-    flat = jnp.concatenate([part.reshape(-1) for part in decoder])
-    lines = -(-(flat.shape[0] + 4 * width) // (8 * width)) * 8
-    flat = jnp.pad(flat, (0, (lines - 4) * width - flat.shape[0])).reshape(-1, width)
-    small = jnp.concatenate([jnp.zeros((2, width), jnp.float32), norm_grads, flat], axis=0)
-    valid = key_valid.astype(jnp.float32)[:, None]
-    block_sums, (grad_tokens, small_sums) = split_at(
+    block_sums, (g_tokens, *small_sums) = split_at(
         backward_attention(
             n,
             seq_size,
             (unpatch, down, up, out, qkv),
-            (grad_after, mixed, query, normed_one, inverse_one, gains_all, valid, small),
-            (wholes[1], wholes[0], keys_all, values_all, hidden_all.reshape(-1, width)),
+            (grad_after, mixed, query, normed_one, inverse_one, gains_all, norm_grads, decoder_grads, scene_count),
+            (wholes[1], wholes[0], keys, values, hidden_all.reshape(-1, hidden_all.shape[2])),
             (grads[2], grads[1], grads[0]),
         ),
         5,
     )
-    flat_sums, at, decoder_sums = small_sums[4:].reshape(-1), 0, []
-    for part in decoder:
-        decoder_sums.append(flat_sums[at : at + part.size].reshape(part.shape))
-        at += part.size
-    own = width // (dp_size * seq_size)
-    sum_unpatch, sum_down, sum_up, sum_out, sum_qkv = block_sums
-    norm_sums = lax.dynamic_slice(small_sums, (0, device * own), (4, own))
-    sum_gain_one, sum_shift_one, sum_gain_two, sum_shift_two = [norm_sums[i] for i in range(4)]
+    g_unpatch, g_down, g_up, g_out, g_qkv = block_sums
+    gain_one, shift_one, gain_two, shift_two = [part[0] for part in small_sums[:4]]
+    g_w1, g_b1, g_w2, g_b2 = small_sums[4:]
     return (
         density,
-        color_value[None],
-        grad_tokens[None],
-        sum_gain_one,
-        sum_shift_one,
-        sum_qkv,
-        sum_out,
-        sum_gain_two,
-        sum_shift_two,
-        sum_up,
-        sum_down,
-        sum_unpatch,
-        decoder_sums[0],
-        decoder_sums[1],
-        decoder_sums[2],
-        decoder_sums[3],
+        color.transpose(1, 0, 2),
+        g_tokens[None],
+        gain_one,
+        shift_one,
+        g_qkv,
+        g_out,
+        gain_two,
+        shift_two,
+        g_up,
+        g_down,
+        g_unpatch,
+        g_w1.T,
+        g_b1[0],
+        g_w2.T,
+        g_b2[0],
     )
 
 

time: 464 us -> 408 us (0.88)
  Pallas kernels: 429 us -> 391 us
  local copies, waits for them, and re-layouts: 21.9 us -> 12.8 us
  other arithmetic: 4.69 us -> 0 us
    pallas_call x1, Pallas kernels: 166 us -> 140 us  [backward_attention(): pl.pallas_call(functools.partial(backward_kernel, n, seq_size, matrices),...]
    pallas_call x1, Pallas kernels: 188 us -> 166 us  [forward_layer(): pl.pallas_call(functools.partial(forward_kernel, n, seq_size, matrices),...]
    pallas_call x1, Pallas kernels: 75 us -> 84.5 us  [middle(): pl.pallas_call(functools.partial(middle_kernel, n, seq_size, matrices), o...]
    slice x7 -> x0, local copies, waits for them, and re-layouts: 5.29 us -> none  [the longest x5 3.55 us: shards(): decoder_sums.append(flat_sums[at:at + part.size].reshape(part.shape))]
    unnamed x40 -> x42, local copies, waits for them, and re-layouts: 11 us -> 12.8 us
where the time goes in v4:
time: 408 us; the launch traced here: 405 us
  Pallas kernels  391 us (96%)
  local copies, waits for them, and re-layouts  12.8 us (3%)
    pallas_call x1, Pallas kernels, forward_layer(): pl.pallas_call(functools.partial(forward_kernel, n, seq_size, matrices),...  166 us
    pallas_call x1, Pallas kernels, backward_attention(): pl.pallas_call(functools.partial(backward_kernel, n, seq_size, matrices),...  140 us
    pallas_call x1, Pallas kernels, middle(): pl.pallas_call(functools.partial(middle_kernel, n, seq_size, matrices), o...  84.5 us
    unnamed x42, local copies, waits for them, and re-layouts  12.8 us

profile of v4, /device:TPU:0, one launch (start us, length us, event | category | flops | bytes accessed | tf_op | source)
XLA Modules:
  0.0 405.5 jit_solution(2971589505077346589)
XLA Ops:
  1.3 166.2 %shard_map.297 = (bf16[2,2,2,128,3072]{4,3,2,1,0:T(8,128)(2,1)}, bf16[2,2,2,128,1024]{4,3,2,1,0:T(8,128)(2,1)}, bf16[2,2,2,128,4096]{4,3,2,1,0:T(8,128)(2,1)}, b...) custom-call(f32[128,768]{1,0:T(8,128)} %refs_0_.1, ...), custom_call_target="tpu_custom_call" | custom-call | tf_op jit(solution)/shard_map/pallas_call | solution.py:1251
  167.5 84.5 %shard_map.298 = (f32[1,2048]{1,0:T(1,128)}, f32[3,1,2048]{2,1,0:T(1,128)}, f32[88,128]{1,0:T(8,128)}, f32[192,1024]{1,0:T(8,128)}, f32[2,1024]{1,0:T(2,128)}, /...) custom-call(bf16[192,2048]{1,0:T(8,128)(2,1)} %get-tuple-element.59.refs_0, ...), custom_call_target="tpu_custom_call" | custom-call | tf_op jit(solution)/shard_map/pallas_call | solution.py:646
  252.0 0.0 copy-start.7
  252.1 0.0 copy-start.6
  252.1 140.4 %shard_map.299 = (f32[128,512]{1,0:T(8,128)}, f32[128,1024]{1,0:T(8,128)}, f32[128,1024]{1,0:T(8,128)}, f32[128,256]{1,0:T(8,128)}, f32[128,768]{1,0:T(8,128)}, ...) custom-call(f32[192,1024]{1,0:T(8,128)} %get-tuple-element.73.refs_0, ...), custom_call_target="tpu_custom_call" | custom-call | tf_op jit(solution)/shard_map/pallas_call | solution.py:989
  392.4 0.0 copy-start.2
  392.5 0.0 copy-start.4
  392.5 0.0 copy-start.12
  392.5 0.0 copy-start.11
  392.5 0.0 copy-start.1
  392.5 0.0 copy-start
  392.5 0.0 copy-done.7
  392.5 0.6 copy.51
  393.1 0.0 copy-done.6
  393.1 0.6 copy.52
  393.7 0.0 copy-start.3
  393.7 2.2 copy.53
  396.0 0.0 copy-start.5
  396.0 0.0 copy-start.10
  396.0 0.0 copy-start.8
  396.0 0.0 copy-start.9
  396.0 1.2 copy.54
  397.2 1.1 copy.55
  398.3 0.0 copy-done.2
  398.3 0.7 copy.56
  399.1 0.0 copy-done.4
  399.1 0.7 copy.57
  399.7 0.0 copy-done.12
  399.7 0.5 copy.58
  400.2 0.0 copy-done.11
  400.2 0.5 copy.59
  400.8 0.0 copy-done.1
  400.8 0.8 copy.60
  401.6 0.0 copy-done
  401.6 0.8 copy.61
  402.4 0.0 copy-done.3
  402.4 0.7 copy.62
  403.1 0.0 copy-done.5
  403.1 0.6 copy.63
  403.7 0.0 copy-done.10
  403.7 0.5 copy.64
  404.2 0.0 copy-done.8
  404.2 0.6 copy.65
  404.8 0.0 copy-done.9
  404.8 0.5 copy.66
Async XLA Ops:
  252.0 140.5 %copy-start.7 = (f32[1,2048]{1,0:T(1,128)S(1)}, f32[1,2048]{1,0:T(1,128)}, u32[]{:S(2)}) copy-start(f32[1,2048]{1,0:T(1,128)} %get-tuple-element.118) | copy-start | bytes 24580
  252.1 141.1 %copy-start.6 = (f32[3,1,2048]{2,1,0:T(1,128)S(1)}, f32[3,1,2048]{2,1,0:T(1,128)}, u32[]{:S(2)}) copy-start(f32[3,1,2048]{2,1,0:T(1,128)} %get-tuple-element.72) | copy-start | bytes 73732
  392.4 5.9 %copy-start.2 = (f32[128,768]{1,0:T(8,128)S(1)}, f32[128,768]{1,0:T(8,128)}, u32[]{:S(2)}) copy-start(f32[128,768]{1,0:T(8,128)} %get-tuple-element.123) | copy-start | bytes 1179652
  392.5 6.6 %copy-start.4 = (f32[128,256]{1,0:T(8,128)S(1)}, f32[128,256]{1,0:T(8,128)}, u32[]{:S(2)}) copy-start(f32[128,256]{1,0:T(8,128)} %get-tuple-element.124) | copy-start | bytes 393220
  392.5 7.3 %copy-start.12 = (f32[1,32]{1,0:T(1,128)S(1)}, f32[1,32]{1,0:T(1,128)}, u32[]{:S(2)}) copy-start(f32[1,32]{1,0:T(1,128)} %get-tuple-element.93) | copy-start | bytes 388
  392.5 7.8 %copy-start.11 = (f32[1,32]{1,0:T(1,128)S(1)}, f32[1,32]{1,0:T(1,128)}, u32[]{:S(2)}) copy-start(f32[1,32]{1,0:T(1,128)} %get-tuple-element.94) | copy-start | bytes 388
  392.5 8.3 %copy-start.1 = (f32[128,1024]{1,0:T(8,128)S(1)}, f32[128,1024]{1,0:T(8,128)}, u32[]{:S(2)}) copy-start(f32[128,1024]{1,0:T(8,128)} %get-tuple-element.127) | copy-start | bytes 1572868
  392.5 9.1 %copy-start = (f32[128,1024]{1,0:T(8,128)S(1)}, f32[128,1024]{1,0:T(8,128)}, u32[]{:S(2)}) copy-start(f32[128,1024]{1,0:T(8,128)} %get-tuple-element.128) | copy-start | bytes 1572868
  393.7 8.6 %copy-start.3 = (f32[128,512]{1,0:T(8,128)S(1)}, f32[128,512]{1,0:T(8,128)}, u32[]{:S(2)}) copy-start(f32[128,512]{1,0:T(8,128)} %get-tuple-element.129) | copy-start | bytes 786436
  396.0 7.1 %copy-start.5 = (f32[64,96]{1,0:T(8,128)S(1)}, f32[64,96]{1,0:T(8,128)}, u32[]{:S(2)}) copy-start(f32[64,96]{1,0:T(8,128)} %get-tuple-element.98) | copy-start | bytes 73732
  396.0 7.7 %copy-start.10 = (f32[1,64]{1,0:T(1,128)S(1)}, f32[1,64]{1,0:T(1,128)}, u32[]{:S(2)}) copy-start(f32[1,64]{1,0:T(1,128)} %get-tuple-element.99) | copy-start | bytes 772
  396.0 8.2 %copy-start.8 = (f32[4,64]{1,0:T(4,128)S(1)}, f32[4,64]{1,0:T(4,128)}, u32[]{:S(2)}) copy-start(f32[4,64]{1,0:T(4,128)} %get-tuple-element.100) | copy-start | bytes 3076
  396.0 8.8 %copy-start.9 = (f32[1,4]{1,0:T(1,128)S(1)}, f32[1,4]{1,0:T(1,128)}, u32[]{:S(2)}) copy-start(f32[1,4]{1,0:T(1,128)} %get-tuple-element.101) | copy-start | bytes 52
